TPU v7x, 32 devices: a whole 2x2x4 slice. The times are simulated.
32 devices in a mesh: pool: 8 (over z, core), cp: 4 (over y, x).
Axes of the slice: x: 2, y: 2, z: 4, core: 2. Of those that a mesh axis runs over, the one named last changes fastest.
Arguments:
- queries: bfloat16 [8, 512, 4096], P('pool', 'cp'), may hold values from -15 to 15
- span_keys: bfloat16 [8, 512, 512], P('pool', 'cp'), may hold values from -6 to 6
- span_values: bfloat16 [8, 512, 512], P('pool', 'cp'), may hold values from -6 to 6
- pool_keys: bfloat16 [192, 128, 512], P('pool'), may hold values from -6 to 6
- pool_values: bfloat16 [192, 128, 512], P('pool'), may hold values from -6 to 6
- page_ids: int32 [8, 16], replicated, may hold values from 0 to 191, as said below
- prefix_pages: int32 [8], replicated, may hold values from 1 to 16, as said below
Outputs:
- attended: float32 [8, 512, 4096], P('pool', 'cp')
Inputs may be any that keep to these rules, and one draw needn't show every extreme that they name: `page_ids`: page p is held by index p // 24 of pool. Among the first prefix_pages[r] entries of a request, one owner holds at most 2 pages, all different; entries beyond that are unused. `prefix_pages`: some request has all 16 entries in use.
All inputs are finite; a program needn't handle non-finite values.
Results may differ from a plain program's by a relative error of at most 0.002.
Values may be sent and summed in bfloat16 or wider, within the bound.
No kernel may reach another device: no remote copies, remote signals or barrier semaphores. Data moves between devices by JAX's collectives and lax.ppermute only.
A program may use at most 128 MiB of HBM per device.

v0:
```python
import jax
import jax.numpy as jnp
from jax import lax
from jax.sharding import PartitionSpec as P

HEAD_DIM = 128
HEADS = 32
KV_HEADS = 4
PAGE = 128
CAP = 2
PAGES_DEV = 24


NEG_FILL = -1e30


def attend(running, queries_grouped4, key_row_set, value_row_set, visible):
    total_rows = key_row_set.shape[0]
    block_len = 512
    blocks = total_rows // block_len
    score_scale = HEAD_DIM ** (-0.5)
    key_blocks = key_row_set.reshape(blocks, block_len, KV_HEADS, HEAD_DIM)
    value_blocks = value_row_set.reshape(blocks, block_len, KV_HEADS, HEAD_DIM)
    vis_blocks = visible.reshape(visible.shape[0], blocks, block_len).transpose(1, 0, 2)

    def block_step(carried, inputs):
        peak, denom, weighted_values = carried
        key_tile, value_tile, vis_block = inputs
        logit_scores = (
            jnp.einsum(
                "swxl,cwl->swxc", queries_grouped4, key_tile, preferred_element_type=jnp.float32
            )
            * score_scale
        )
        live = vis_block[:, None, None, :]
        logit_scores = jnp.where(live, logit_scores, NEG_FILL)
        new_peak = jnp.maximum(peak, jnp.max(logit_scores, axis=-1))
        softmax_weights = jnp.where(live, jnp.exp(logit_scores - new_peak[..., None]), 0.0).astype(
            jnp.bfloat16
        )
        factor = jnp.exp(peak - new_peak)
        denom = denom * factor + jnp.sum(softmax_weights, axis=-1, dtype=jnp.float32)
        weighted_values = weighted_values * factor[..., None] + jnp.einsum(
            "unqy,ynx->unqx", softmax_weights, value_tile, preferred_element_type=jnp.float32
        )
        return ((new_peak, denom, weighted_values), None)

    return lax.scan(block_step, running, (key_blocks, value_blocks, vis_blocks))[0]


def body(queries, span_keys, span_values, pool_keys, pool_values, page_ids, prefix_pages):
    tok_count = queries.shape[1]
    groups = HEADS // KV_HEADS
    width = KV_HEADS * HEAD_DIM
    queries_grouped4 = queries[0].reshape(tok_count, KV_HEADS, groups, HEAD_DIM)
    pool_count = lax.axis_size("pool")
    pool_index = lax.axis_index("pool")
    ctx_count = lax.axis_size("cp")
    ctx_index = lax.axis_index("cp")
    slot_count = page_ids.shape[1]
    owners = page_ids // PAGES_DEV
    slot_iota = jnp.arange(slot_count, dtype=jnp.int32)
    live_slots = slot_iota[None, :] < prefix_pages[:, None]
    earlier = slot_iota[None, :] < slot_iota[:, None]
    same_owner = (owners[:, :, None] == owners[:, None, :]) & live_slots[:, None, :] & earlier[None]
    slot_rank = jnp.sum(same_owner.astype(jnp.int32), axis=2)
    held_here = live_slots & (owners == pool_index)
    cap_iota = jnp.arange(CAP, dtype=jnp.int32)
    picked = held_here[:, None, :] & (slot_rank[:, None, :] == cap_iota[None, :, None])
    local_pages = jnp.sum(jnp.where(picked, page_ids[:, None, :] % PAGES_DEV, 0), axis=2)
    own_owners = lax.dynamic_index_in_dim(owners, pool_index, 0, keepdims=False)
    own_live = lax.dynamic_index_in_dim(live_slots, pool_index, 0, keepdims=False)
    owner_iota = jnp.arange(pool_count, dtype=jnp.int32)
    per_owner = jnp.sum(
        ((own_owners[None, :] == owner_iota[:, None]) & own_live[None, :]).astype(jnp.int32), axis=1
    )
    usable = cap_iota[None, :] < per_owner[:, None]
    empty = (
        jnp.full((tok_count, KV_HEADS, groups), NEG_FILL, jnp.float32),
        jnp.zeros((tok_count, KV_HEADS, groups), jnp.float32),
        jnp.zeros((tok_count, KV_HEADS, groups, HEAD_DIM), jnp.float32),
    )
    query_pos = ctx_index * tok_count + jnp.arange(tok_count, dtype=jnp.int32)
    key_piece = lax.all_gather(span_keys, "cp", axis=1, tiled=True)
    value_piece = lax.all_gather(span_values, "cp", axis=1, tiled=True)
    piece_len = key_piece.shape[1]
    key_pos = jnp.arange(piece_len, dtype=jnp.int32)
    visible = key_pos[None, :] <= query_pos[:, None]
    local_state = attend(empty, queries_grouped4, key_piece[0], value_piece[0], visible)
    part_len = PAGE // ctx_count
    key_slice = lax.dynamic_slice_in_dim(pool_keys, ctx_index * part_len, part_len, 1)[local_pages]
    value_slice = lax.dynamic_slice_in_dim(pool_values, ctx_index * part_len, part_len, 1)[
        local_pages
    ]
    fetched_keys, fetched_values = (
        lax.all_to_all(key_slice, "pool", split_axis=0, concat_axis=0, tiled=True),
        lax.all_to_all(value_slice, "pool", split_axis=0, concat_axis=0, tiled=True),
    )
    key_part = lax.all_gather(fetched_keys, "cp", axis=2, tiled=True)
    part_len = key_part.shape[2]
    visible = jnp.broadcast_to(usable[:, :, None], (pool_count, CAP, part_len)).reshape(1, -1)
    prefix_state = attend(
        empty,
        queries_grouped4,
        key_part.reshape(-1, width),
        lax.all_gather(fetched_values, "cp", axis=2, tiled=True).reshape(-1, width),
        visible,
    )
    peak_one, denom_one, mixed_one = local_state
    peak_two, denom_two, mixed_two = prefix_state
    peak = jnp.maximum(peak_one, peak_two)
    factor_one = jnp.exp(peak_one - peak)
    factor_two = jnp.exp(peak_two - peak)
    denom = denom_one * factor_one + denom_two * factor_two
    weighted_values = mixed_one * factor_one[..., None] + mixed_two * factor_two[..., None]
    attended = weighted_values / denom[..., None]
    return attended.reshape(1, tok_count, HEADS * HEAD_DIM)


def solution(mesh):
    in_specs = (
        P("pool", "cp", None),
        P("pool", "cp", None),
        P("pool", "cp", None),
        P("pool", None, None),
        P("pool", None, None),
        P(),
        P(),
    )
    out_specs = P("pool", "cp", None)
    return jax.shard_map(body, mesh=mesh, in_specs=in_specs, out_specs=out_specs, check_vma=False)
```

profile of v0, /device:TPU:16, one launch (start us, length us, event | category | flops | bytes accessed | tf_op | source)
XLA Modules:
  0.0 204.0 jit_solution(14461215009607959577)
XLA Ops:
  6.5 0.7 add_select_fusion
  7.2 0.8 compare_and_fusion
  8.0 0.3 convert_reduce_fusion.2
  8.3 0.2 select_reduce_fusion
  8.5 0.1 copy.33
  8.6 0.1 reshape.103
  8.7 1.6 constant_dynamic-slice_fusion.2
  10.3 0.6 gather_fusion
  10.9 17.3 %all_to_all.10 = bf16[8,2,32,512]{3,2,1,0:T(8,128)(2,1)} all-to-all(bf16[8,2,32,512]{3,2,1,0:T(8,128)(2,1)S(1)} %bitcast.91), channel_id=1, replica_groups=mesh['pool'=8,'cp'=4] {'pool'}, dimensions={0} | all-to-all | bytes 1048576 | tf_op jit(solution)/shard_map/all_to_all | solution.py:96
  28.3 0.6 gather_fusion.1
  28.9 18.4 %all_to_all.11 = bf16[8,2,32,512]{3,2,1,0:T(8,128)(2,1)} all-to-all(bf16[8,2,32,512]{3,2,1,0:T(8,128)(2,1)S(1)} %bitcast.90), channel_id=1, replica_groups=mesh['pool'=8,'cp'=4] {'pool'}, dimensions={0} | all-to-all | bytes 1048576 | tf_op jit(solution)/shard_map/all_to_all | solution.py:97
  47.4 0.1 convert_reduce_fusion.3
  47.6 0.1 broadcast_in_dim.111
  47.7 1.3 copy.28
  49.0 1.6 copy.36
  50.6 1.0 copy.27
  51.7 16.0 %all_gather.13 = bf16[1,512,512]{2,1,0:T(8,128)(2,1)} all-gather(bf16[1,128,512]{2,1,0:T(8,128)(2,1)S(1)} %copy-done.2), channel_id=1, replica_groups=mesh['pool'=8,'cp'=4] {'cp'}, dimensions={1}, use_global_device_ids=true | all-gather | bytes 655360 | tf_op jit(solution)/shard_map/all_gather | solution.py:85
  67.7 2.1 %copy.31 = bf16[1,512,512]{1,2,0:T(8,128)(2,1)} copy(bf16[1,512,512]{2,1,0:T(8,128)(2,1)} %all_gather.13) | data formatting | bytes 1048576 | tf_op jit(solution)/shard_map/all_gather | solution.py:85
  69.7 10.4 %all_gather.12 = bf16[1,512,512]{1,2,0:T(8,128)(2,1)S(1)} all-gather(bf16[1,128,512]{1,2,0:T(8,128)(2,1)S(1)} %copy.27), channel_id=1, replica_groups=mesh['pool'=8,'cp'=4] {'cp'}, dimensions={1}, use_global_device_ids=true | all-gather | bytes 655360 | tf_op jit(solution)/shard_map/all_gather | solution.py:84
  80.2 2.6 %fusion.6 = (f32[128,4,8]{0,2,1:T(8,128)S(1)}, f32[4,512,128,8]{2,1,3,0:T(8,128)S(1)}) fusion(pred[128,512]{0,1:T(8,128)(4,1)S(1)} %iota_compare_fusion, bf16[512,4,128,1]{0,2,3,1:T(8,128)(2,1)S(1)} %bitcast.88, bf16[128,4,8,128]{0,3,2,1:T(8,128)(2,1)} %bitcast.87), kind=kOutput, calls=%fused_computation.24 | convolution fusion | flops 543158272 | bytes 10043392 | tf_op jit(solution)/shard_map/while/body/eval_jaxpr/swxl,cwl->swxc/dot_general | solution.py:30
  82.9 3.2 %copy-done = f32[4,512,128,8]{2,1,3,0:T(8,128)} copy-done((f32[4,512,128,8]{2,1,3,0:T(8,128)}, f32[4,512,128,8]{2,1,3,0:T(8,128)S(1)}, u32[]{:S(2)}) %copy-start) | copy-done | bytes 8388632
  86.1 2.1 %convert_reduce_fusion.1 = f32[128,4,8]{0,2,1:T(8,128)S(1)} fusion(f32[128,4,8]{0,2,1:T(8,128)S(1)} %broadcast_maximum_fusion, f32[4,512,128,8]{2,1,3,0:T(8,128)S(1)} %get-tuple-element.151, pred[128,512]{0,1:T(8,128)(4,1)S(1)} %iota_compare_fusion), kind=kLoop, calls=%fused_computation.22 | loop fusion | flops 14675968 | bytes 8486912 | tf_op jit(solution)/shard_map/while/body/eval_jaxpr/reduce_sum | solution.py:42
  88.2 4.0 %reshape_reshape.6 = bf16[4,512,4,128]{3,2,1,0:T(4,128)(2,1)} reshape(bf16[8,2,128,512]{3,2,1,0:T(8,128)(2,1)} %all-gather.3.cloned.1.call-done) | data formatting | bytes 4194304 | tf_op jit(solution)/shard_map/reshape;reshape | solution.py:22
  92.1 14.7 %all-gather.5.cloned.1.call-done = bf16[8,2,128,512]{3,2,1,0:T(8,128)(2,1)} async-done(((bf16[8,2,32,512]{3,2,1,0:T(8,128)(2,1)}), bf16[8,2,128,512]{3,2,1,0:T(8,128)(2,1)}) %all-gather.5.cloned.1.call-update) | async-done | bytes 2097168 | tf_op jit(solution)/shard_map/all_gather | solution.py:106
  106.8 4.0 %reshape_reshape.7 = bf16[4,512,4,128]{3,2,1,0:T(4,128)(2,1)} reshape(bf16[8,2,128,512]{3,2,1,0:T(8,128)(2,1)} %all-gather.5.cloned.1.call-done) | data formatting | bytes 4194304 | tf_op jit(solution)/shard_map/reshape;reshape | solution.py:23
  110.8 76.1 %while.3 = (s32[]{:T(128)}, f32[128,4,8]{0,2,1:T(8,128)S(1)}, f32[128,4,8]{0,2,1:T(8,128)S(1)}, f32[128,4,8,128]{0,3,2,1:T(8,128)S(1)}, pred[4,1,512]{2,1,0:T(4,...) while((s32[]{:T(128)}, f32[128,4,8]{0,2,1:T(8,128)S(1)}, ...), condition=%wide.region_7.8_spmd.clone, body=%wide.region_4.7_spmd.clone.sunk | while | flops 1096306688 | bytes 34850936 | solution.py:48
  110.8 2.4 %constant_dynamic-slice_fusion.6 = (bf16[1,512,4,128]{3,2,1,0:T(4,128)(2,1)}, bf16[1,512,4,128]{3,2,1,0:T(4,128)(2,1)S(1)}) fusion(bf16[4,512,4,128]{3,2,1,0:T(4,128)(2,1)} %get-tuple-element.246, s32[]{:T(128)} %get-tuple-element.229, bf16[4,512,4,128]{3,2,1,0:T(4,128)(2,1)} %get-tuple-element.244), kind=kLoop, calls=%fused_computation.19.clone.1 | loop fusion | bytes 2097156 | tf_op jit(solution)/shard_map/while/body/jit(dynamic_index_in_dim)/dynamic_slice | solution.py:48
  113.2 4.6 %bitcast_reduce_fusion.2 = (f32[128,4,8]{0,2,1:T(8,128)S(1)}, f32[4,512,128,8]{2,1,3,0:T(8,128)}) fusion(pred[512]{0:T(512)(128)(4,1)S(1)} %dynamic-slice_reduce_fusion.2, bf16[128,4,8,128]{3,0,2,1:T(8,128)(2,1)S(1)} %get-tuple-element.245, bf16[1,512,4,128]{3,2,1,0:T(4,128)(2,1)S(1)} %get-tuple-element.211), kind=kOutput, calls=%fused_computation.3.clone.1 | convolution fusion | flops 543158272 | bytes 9978368 | tf_op jit(solution)/shard_map/while/body/eval_jaxpr/swxl,cwl->swxc/dot_general | solution.py:30
  117.8 6.3 %convert_reduce_fusion.5 = (f32[128,4,8]{0,2,1:T(8,128)S(1)}, bf16[128,4,8,512]{0,3,2,1:T(8,128)(2,1)}) fusion(f32[128,4,8]{0,2,1:T(8,128)S(1)} %select_maximum_fusion.2, f32[4,512,128,8]{2,1,3,0:T(8,128)} %get-tuple-element.213, pred[512]{0:T(512)(128)(4,1)S(1)} %dynamic-slice_reduce_fusion.2), kind=kLoop, calls=%fused_computation.7.clone.1 | loop fusion | flops 14675968 | bytes 12616192 | tf_op jit(solution)/shard_map/while/body/eval_jaxpr/reduce_sum | solution.py:42
  124.1 2.2 %copy.57 = bf16[1,512,4,128]{1,3,2,0:T(8,128)(2,1)} copy(bf16[1,512,4,128]{3,2,1,0:T(4,128)(2,1)} %get-tuple-element.218) | data formatting | bytes 1048576 | tf_op jit(solution)/shard_map/while/body/jit(dynamic_index_in_dim)/dynamic_slice | solution.py:48
  126.3 3.5 %bitcast_add_fusion.3 = f32[128,4,8,128]{0,3,2,1:T(8,128)S(1)} fusion(f32[128,4,8,128]{0,3,2,1:T(8,128)S(1)} %get-tuple-element.232, bf16[128,4,8,512]{0,3,2,1:T(8,128)(2,1)} %get-tuple-element.216, f32[128,4,8]{0,2,1:T(8,128)S(1)} %get-tuple-element.217, pred[]{:T(512)S(6)} %compare.3, bf16[1,512,4,128]{1,3,2,0:T(8,128)(2,1)} %copy.57), kind=kOutput, calls=%fused_computation.9.clone.1 | convolution fusion | flops 538443776 | bytes 8929281 | tf_op jit(solution)/shard_map/while/body/eval_jaxpr/unqy,ynx->unqx/dot_general | solution.py:43
  129.8 2.4 %constant_dynamic-slice_fusion.6 = (bf16[1,512,4,128]{3,2,1,0:T(4,128)(2,1)}, bf16[1,512,4,128]{3,2,1,0:T(4,128)(2,1)S(1)}) fusion(bf16[4,512,4,128]{3,2,1,0:T(4,128)(2,1)} %get-tuple-element.246, s32[]{:T(128)} %get-tuple-element.229, bf16[4,512,4,128]{3,2,1,0:T(4,128)(2,1)} %get-tuple-element.244), kind=kLoop, calls=%fused_computation.19.clone.1 | loop fusion | bytes 2097156 | tf_op jit(solution)/shard_map/while/body/jit(dynamic_index_in_dim)/dynamic_slice | solution.py:48
  132.2 4.6 %bitcast_reduce_fusion.2 = (f32[128,4,8]{0,2,1:T(8,128)S(1)}, f32[4,512,128,8]{2,1,3,0:T(8,128)}) fusion(pred[512]{0:T(512)(128)(4,1)S(1)} %dynamic-slice_reduce_fusion.2, bf16[128,4,8,128]{3,0,2,1:T(8,128)(2,1)S(1)} %get-tuple-element.245, bf16[1,512,4,128]{3,2,1,0:T(4,128)(2,1)S(1)} %get-tuple-element.211), kind=kOutput, calls=%fused_computation.3.clone.1 | convolution fusion | flops 543158272 | bytes 9978368 | tf_op jit(solution)/shard_map/while/body/eval_jaxpr/swxl,cwl->swxc/dot_general | solution.py:30
  136.8 6.3 %convert_reduce_fusion.5 = (f32[128,4,8]{0,2,1:T(8,128)S(1)}, bf16[128,4,8,512]{0,3,2,1:T(8,128)(2,1)}) fusion(f32[128,4,8]{0,2,1:T(8,128)S(1)} %select_maximum_fusion.2, f32[4,512,128,8]{2,1,3,0:T(8,128)} %get-tuple-element.213, pred[512]{0:T(512)(128)(4,1)S(1)} %dynamic-slice_reduce_fusion.2), kind=kLoop, calls=%fused_computation.7.clone.1 | loop fusion | flops 14675968 | bytes 12616192 | tf_op jit(solution)/shard_map/while/body/eval_jaxpr/reduce_sum | solution.py:42
  143.1 2.2 %copy.57 = bf16[1,512,4,128]{1,3,2,0:T(8,128)(2,1)} copy(bf16[1,512,4,128]{3,2,1,0:T(4,128)(2,1)} %get-tuple-element.218) | data formatting | bytes 1048576 | tf_op jit(solution)/shard_map/while/body/jit(dynamic_index_in_dim)/dynamic_slice | solution.py:48
  145.3 3.5 %bitcast_add_fusion.3 = f32[128,4,8,128]{0,3,2,1:T(8,128)S(1)} fusion(f32[128,4,8,128]{0,3,2,1:T(8,128)S(1)} %get-tuple-element.232, bf16[128,4,8,512]{0,3,2,1:T(8,128)(2,1)} %get-tuple-element.216, f32[128,4,8]{0,2,1:T(8,128)S(1)} %get-tuple-element.217, pred[]{:T(512)S(6)} %compare.3, bf16[1,512,4,128]{1,3,2,0:T(8,128)(2,1)} %copy.57), kind=kOutput, calls=%fused_computation.9.clone.1 | convolution fusion | flops 538443776 | bytes 8929281 | tf_op jit(solution)/shard_map/while/body/eval_jaxpr/unqy,ynx->unqx/dot_general | solution.py:43
  148.9 2.4 %constant_dynamic-slice_fusion.6 = (bf16[1,512,4,128]{3,2,1,0:T(4,128)(2,1)}, bf16[1,512,4,128]{3,2,1,0:T(4,128)(2,1)S(1)}) fusion(bf16[4,512,4,128]{3,2,1,0:T(4,128)(2,1)} %get-tuple-element.246, s32[]{:T(128)} %get-tuple-element.229, bf16[4,512,4,128]{3,2,1,0:T(4,128)(2,1)} %get-tuple-element.244), kind=kLoop, calls=%fused_computation.19.clone.1 | loop fusion | bytes 2097156 | tf_op jit(solution)/shard_map/while/body/jit(dynamic_index_in_dim)/dynamic_slice | solution.py:48
  151.3 4.6 %bitcast_reduce_fusion.2 = (f32[128,4,8]{0,2,1:T(8,128)S(1)}, f32[4,512,128,8]{2,1,3,0:T(8,128)}) fusion(pred[512]{0:T(512)(128)(4,1)S(1)} %dynamic-slice_reduce_fusion.2, bf16[128,4,8,128]{3,0,2,1:T(8,128)(2,1)S(1)} %get-tuple-element.245, bf16[1,512,4,128]{3,2,1,0:T(4,128)(2,1)S(1)} %get-tuple-element.211), kind=kOutput, calls=%fused_computation.3.clone.1 | convolution fusion | flops 543158272 | bytes 9978368 | tf_op jit(solution)/shard_map/while/body/eval_jaxpr/swxl,cwl->swxc/dot_general | solution.py:30
  155.9 6.3 %convert_reduce_fusion.5 = (f32[128,4,8]{0,2,1:T(8,128)S(1)}, bf16[128,4,8,512]{0,3,2,1:T(8,128)(2,1)}) fusion(f32[128,4,8]{0,2,1:T(8,128)S(1)} %select_maximum_fusion.2, f32[4,512,128,8]{2,1,3,0:T(8,128)} %get-tuple-element.213, pred[512]{0:T(512)(128)(4,1)S(1)} %dynamic-slice_reduce_fusion.2), kind=kLoop, calls=%fused_computation.7.clone.1 | loop fusion | flops 14675968 | bytes 12616192 | tf_op jit(solution)/shard_map/while/body/eval_jaxpr/reduce_sum | solution.py:42
  162.2 2.2 %copy.57 = bf16[1,512,4,128]{1,3,2,0:T(8,128)(2,1)} copy(bf16[1,512,4,128]{3,2,1,0:T(4,128)(2,1)} %get-tuple-element.218) | data formatting | bytes 1048576 | tf_op jit(solution)/shard_map/while/body/jit(dynamic_index_in_dim)/dynamic_slice | solution.py:48
  164.3 3.5 %bitcast_add_fusion.3 = f32[128,4,8,128]{0,3,2,1:T(8,128)S(1)} fusion(f32[128,4,8,128]{0,3,2,1:T(8,128)S(1)} %get-tuple-element.232, bf16[128,4,8,512]{0,3,2,1:T(8,128)(2,1)} %get-tuple-element.216, f32[128,4,8]{0,2,1:T(8,128)S(1)} %get-tuple-element.217, pred[]{:T(512)S(6)} %compare.3, bf16[1,512,4,128]{1,3,2,0:T(8,128)(2,1)} %copy.57), kind=kOutput, calls=%fused_computation.9.clone.1 | convolution fusion | flops 538443776 | bytes 8929281 | tf_op jit(solution)/shard_map/while/body/eval_jaxpr/unqy,ynx->unqx/dot_general | solution.py:43
  167.9 2.4 %constant_dynamic-slice_fusion.6 = (bf16[1,512,4,128]{3,2,1,0:T(4,128)(2,1)}, bf16[1,512,4,128]{3,2,1,0:T(4,128)(2,1)S(1)}) fusion(bf16[4,512,4,128]{3,2,1,0:T(4,128)(2,1)} %get-tuple-element.246, s32[]{:T(128)} %get-tuple-element.229, bf16[4,512,4,128]{3,2,1,0:T(4,128)(2,1)} %get-tuple-element.244), kind=kLoop, calls=%fused_computation.19.clone.1 | loop fusion | bytes 2097156 | tf_op jit(solution)/shard_map/while/body/jit(dynamic_index_in_dim)/dynamic_slice | solution.py:48
  170.3 4.6 %bitcast_reduce_fusion.2 = (f32[128,4,8]{0,2,1:T(8,128)S(1)}, f32[4,512,128,8]{2,1,3,0:T(8,128)}) fusion(pred[512]{0:T(512)(128)(4,1)S(1)} %dynamic-slice_reduce_fusion.2, bf16[128,4,8,128]{3,0,2,1:T(8,128)(2,1)S(1)} %get-tuple-element.245, bf16[1,512,4,128]{3,2,1,0:T(4,128)(2,1)S(1)} %get-tuple-element.211), kind=kOutput, calls=%fused_computation.3.clone.1 | convolution fusion | flops 543158272 | bytes 9978368 | tf_op jit(solution)/shard_map/while/body/eval_jaxpr/swxl,cwl->swxc/dot_general | solution.py:30
  174.9 6.3 %convert_reduce_fusion.5 = (f32[128,4,8]{0,2,1:T(8,128)S(1)}, bf16[128,4,8,512]{0,3,2,1:T(8,128)(2,1)}) fusion(f32[128,4,8]{0,2,1:T(8,128)S(1)} %select_maximum_fusion.2, f32[4,512,128,8]{2,1,3,0:T(8,128)} %get-tuple-element.213, pred[512]{0:T(512)(128)(4,1)S(1)} %dynamic-slice_reduce_fusion.2), kind=kLoop, calls=%fused_computation.7.clone.1 | loop fusion | flops 14675968 | bytes 12616192 | tf_op jit(solution)/shard_map/while/body/eval_jaxpr/reduce_sum | solution.py:42
  181.2 2.2 %copy.57 = bf16[1,512,4,128]{1,3,2,0:T(8,128)(2,1)} copy(bf16[1,512,4,128]{3,2,1,0:T(4,128)(2,1)} %get-tuple-element.218) | data formatting | bytes 1048576 | tf_op jit(solution)/shard_map/while/body/jit(dynamic_index_in_dim)/dynamic_slice | solution.py:48
  183.4 3.5 %bitcast_add_fusion.3 = f32[128,4,8,128]{0,3,2,1:T(8,128)S(1)} fusion(f32[128,4,8,128]{0,3,2,1:T(8,128)S(1)} %get-tuple-element.232, bf16[128,4,8,512]{0,3,2,1:T(8,128)(2,1)} %get-tuple-element.216, f32[128,4,8]{0,2,1:T(8,128)S(1)} %get-tuple-element.217, pred[]{:T(512)S(6)} %compare.3, bf16[1,512,4,128]{1,3,2,0:T(8,128)(2,1)} %copy.57), kind=kOutput, calls=%fused_computation.9.clone.1 | convolution fusion | flops 538443776 | bytes 8929281 | tf_op jit(solution)/shard_map/while/body/eval_jaxpr/unqy,ynx->unqx/dot_general | solution.py:43
  187.0 7.3 %fusion.9 = f32[128,4,8,128]{0,3,2,1:T(8,128)} fusion(f32[128,4,8,128]{0,3,2,1:T(8,128)S(1)} %get-tuple-element.74, bf16[512,4,128,1]{0,2,3,1:T(8,128)(2,1)} %bitcast.92, f32[128,4,8]{0,2,1:T(8,128)S(1)} %get-tuple-element.139, f32[128,4,8]{0,2,1:T(8,128)S(1)} %get-tuple-element.141, f32[128,4,8]{0,2,1:T(8,128)S(1)} %get-tuple-element.140, ...), kind=kOutput, calls=%fused_computation.28 | convolution fusion | flops 549978112 | bytes 13254656 | tf_op jit(solution)/shard_map/while/body/eval_jaxpr/unqy,ynx->unqx/dot_general | solution.py:43
  194.3 2.9 %copy.38 = f32[1,128,4096]{2,1,0:T(8,128)} copy(f32[1,128,4096]{1,2,0:T(8,128)} %bitcast.89) | data formatting | bytes 4194304 | tf_op jit(solution)/shard_map/reshape | solution.py:117
  (40 shorter events, 0.5 us)
Async XLA Ops:
  6.5 81.6 %all-gather.3.cloned.1.call-start = ((), (), s32[]{:S(2)}) async-start(), calls=%async_computation.2 | async-start | bytes 2621440 | tf_op jit(solution)/shard_map/all_gather | solution.py:99
  8.7 39.0 %copy-start.1 = (bf16[1,128,4096]{2,1,0:T(8,128)(2,1)S(1)}, bf16[1,128,4096]{2,1,0:T(8,128)(2,1)}, u32[]{:S(2)}) copy-start(bf16[1,128,4096]{2,1,0:T(8,128)(2,1)} %param.9) | copy-start | bytes 3145732
  10.9 40.8 %copy-start.2 = (bf16[1,128,512]{2,1,0:T(8,128)(2,1)S(1)}, bf16[1,128,512]{2,1,0:T(8,128)(2,1)}, u32[]{:S(2)}) copy-start(bf16[1,128,512]{2,1,0:T(8,128)(2,1)} %param.11) | copy-start | bytes 393220
  28.2 78.6 %all-gather.5.cloned.1.call-start = ((), (), s32[]{:S(2)}) async-start(), calls=%async_computation.3 | async-start | bytes 2621440 | tf_op jit(solution)/shard_map/all_gather | solution.py:106
  82.8 3.2 %copy-start = (f32[4,512,128,8]{2,1,3,0:T(8,128)}, f32[4,512,128,8]{2,1,3,0:T(8,128)S(1)}, u32[]{:S(2)}) copy-start(f32[4,512,128,8]{2,1,3,0:T(8,128)S(1)} %get-tuple-element.151) | copy-start | bytes 25165828
Sparse Core Ops, SparseCore 0:
  28.3 41.2 all-gather.2
  71.5 35.2 all-gather.4
where the time goes:
time: 207 us; the launch traced here: 204 us
  blocking collectives  62.1 us (30%)
  matrix products  42.4 us (20%)
  local copies, waits for them, and re-layouts  41.4 us (20%)
  other arithmetic  29.6 us (14%)
  waiting for transfers between devices  14.7 us (7%)
  between operations  13.6 us (7%)
    reduce_sum x5, other arithmetic, block_step(): jnp.sum(softmax_weights, axis=-1, dtype=jnp.float32)  27.3 us
    dot_general x5, matrix products, block_step(): jnp.einsum('unqy,ynx->unqx', softmax_weights, value_tile, preferred_eleme...  21.4 us
    dot_general x5, matrix products, block_step(): jnp.einsum('swxl,cwl->swxc', queries_grouped4, key_tile, preferred_elemen...  21 us
    all_to_all x1, blocking collectives, body(): lax.all_to_all(value_slice, 'pool', split_axis=0, concat_axis=0, tiled=True)  18.4 us
    dynamic_slice x12, local copies, waits for them, and re-layouts, attend(): lax.scan(block_step, running, (key_blocks, value_blocks, vis_blocks))[0]  18.3 us
    all_to_all x1, blocking collectives, body(): lax.all_to_all(key_slice, 'pool', split_axis=0, concat_axis=0, tiled=True)  17.3 us
    all_gather x1, blocking collectives, body(): value_piece = lax.all_gather(span_values, 'cp', axis=1, tiled=True)  16 us
    all_gather x1, waiting for transfers between devices, body(): lax.all_gather(fetched_values, 'cp', axis=2, tiled=True).reshape(-1, width)  14.7 us
  transfers between devices with their start and end apart: 2, of which 1 were waited for; matrix products, arithmetic and copies ran while one was open for 8% of the time, Pallas kernels for 0%

commit v1 on v0

v1 whole, which is shorter than its diff:
```python
import functools
import math

import jax
import jax.numpy as jnp
from jax import lax
from jax.experimental import pallas as pl
from jax.experimental.pallas import tpu as pltpu
from jax.sharding import PartitionSpec as P

HEAD_DIM = 128
HEADS = 32
KV_HEADS = 4
CAP = 2

NEG_FILL = -1e30
EXP2_SCALE = math.log2(math.e) / math.sqrt(HEAD_DIM)
ANY = pl.BlockSpec(memory_space=pl.ANY)
SMEM = pl.BlockSpec(memory_space=pltpu.SMEM)
VMEM = pl.BlockSpec(memory_space=pltpu.VMEM)


def kv_head(ctx, ctx_count):
    return ctx * KV_HEADS // ctx_count


def prep_pages_kernel(ids_ref, len_ref, keys_ref, values_ref, *rest):
    pool_count = ids_ref.shape[0]
    slot_count = ids_ref.shape[1]
    out_refs = rest[:pool_count]
    pages_ref, sems = rest[pool_count:]
    pages_dev = keys_ref.shape[0]
    me = lax.axis_index("pool")
    head = kv_head(lax.axis_index("cp"), lax.axis_size("cp"))
    columns = pl.ds(pl.multiple_of(head * HEAD_DIM, HEAD_DIM), HEAD_DIM)
    low = me * pages_dev
    copies = []
    for step in reversed(range(pool_count)):
        request = me ^ step
        live = len_ref[request]
        for rank in range(CAP):
            pages_ref[step, rank] = 0
        count = jnp.int32(0)
        for slot in range(slot_count):
            local = ids_ref[request, slot] - low
            hit = (local >= 0) & (local < pages_dev) & (slot < live)
            pages_ref[step, count] = jnp.where(hit, local, 0)
            count = jnp.minimum(count + hit.astype(jnp.int32), CAP)
        for rank in range(CAP):
            page = pages_ref[step, rank]
            for which, source in enumerate((keys_ref, values_ref)):
                copy = pltpu.make_async_copy(
                    source.at[page, :, columns],
                    out_refs[step].at[which, rank],
                    sems.at[step, which, rank],
                )
                copy.start()
                copies.append(copy)
    for copy in copies:
        copy.wait()


def prep_pages(page_ids, prefix_pages, pool_keys, pool_values):
    pool_count = page_ids.shape[0]
    page = pool_keys.shape[1]
    shape = jax.ShapeDtypeStruct((2, CAP, page, HEAD_DIM), jnp.bfloat16)
    return pl.pallas_call(
        prep_pages_kernel,
        out_shape=[shape] * pool_count,
        in_specs=[SMEM, SMEM, ANY, ANY],
        out_specs=[ANY] * pool_count,
        scratch_shapes=[
            pltpu.SMEM((pool_count, CAP + 1), jnp.int32),
            pltpu.SemaphoreType.DMA((pool_count, 2, CAP)),
        ],
        name="prep_pages",
    )(page_ids, prefix_pages, pool_keys, pool_values)


def prep_span_kernel(q_ref, k_ref, v_ref, out_ref, sems):
    ctx_count = out_ref.shape[0]
    width = HEADS // ctx_count * HEAD_DIM
    copies = []
    for ctx in range(ctx_count):
        head = kv_head(ctx, ctx_count) * HEAD_DIM
        for part, (source, begin, size, place) in enumerate(
            (
                (q_ref, ctx * width, width, 0),
                (k_ref, head, HEAD_DIM, width),
                (v_ref, head, HEAD_DIM, width + HEAD_DIM),
            )
        ):
            copy = pltpu.make_async_copy(
                source.at[0, :, pl.ds(begin, size)],
                out_ref.at[ctx, :, pl.ds(place, size)],
                sems.at[ctx, part],
            )
            copy.start()
            copies.append(copy)
    for copy in copies:
        copy.wait()


def prep_span(queries, span_keys, span_values):
    ctx_count = lax.axis_size("cp")
    tok_count = queries.shape[1]
    width = (HEADS // ctx_count + 2) * HEAD_DIM
    return pl.pallas_call(
        prep_span_kernel,
        out_shape=jax.ShapeDtypeStruct((ctx_count, tok_count, width), jnp.bfloat16),
        in_specs=[ANY] * 3,
        out_specs=ANY,
        scratch_shapes=[pltpu.SemaphoreType.DMA((ctx_count, 3))],
        name="prep_span",
    )(queries, span_keys, span_values)


def attend_kernel(chunk, pages_dev, ids_ref, len_ref, span_ref, *rest):
    pool_count, slot_count = ids_ref.shape
    page_refs = rest[:pool_count]
    out_ref, k_ref, v_ref, count_ref = rest[pool_count:]
    ctx_count, tok_count, width = span_ref.shape
    heads = width // HEAD_DIM - 2
    page = page_refs[0].shape[2]
    me = lax.axis_index("pool")

    for owner in range(pool_count):
        count_ref[owner] = 0
    live = len_ref[me]
    for slot in range(slot_count):
        owner = ids_ref[me, slot] // pages_dev
        count_ref[owner] = count_ref[owner] + (slot < live).astype(jnp.int32)

    first_key = span_ref[0, 0:1, heads * HEAD_DIM : (heads + 1) * HEAD_DIM]
    first_key = jnp.broadcast_to(first_key, (page, HEAD_DIM))
    zeros = jnp.zeros((page, HEAD_DIM), jnp.bfloat16)
    ones = jnp.ones((page, HEAD_DIM), jnp.bfloat16)
    for step in range(pool_count):
        for rank in range(CAP):
            rows = pl.ds((step * CAP + rank) * page, page)
            used = count_ref[me ^ step] > rank
            k_ref[rows, :] = jnp.where(used, page_refs[step][0, rank], first_key)
            v_ref[rows, :HEAD_DIM] = jnp.where(used, page_refs[step][1, rank], zeros)
            v_ref[rows, HEAD_DIM:] = jnp.where(used, ones, zeros)
    prefix = pool_count * CAP * page
    for ctx in range(ctx_count):
        rows = pl.ds(prefix + ctx * tok_count, tok_count)
        k_ref[rows, :] = span_ref[ctx, :, heads * HEAD_DIM : (heads + 1) * HEAD_DIM]
        v_ref[rows, :HEAD_DIM] = span_ref[ctx, :, (heads + 1) * HEAD_DIM :]
        v_ref[rows, HEAD_DIM:] = ones

    row_pos = lax.broadcasted_iota(jnp.int32, (tok_count, tok_count), 0)
    col_pos = lax.broadcasted_iota(jnp.int32, (tok_count, tok_count), 1)
    causal = jnp.concatenate([col_pos <= row_pos] * heads, axis=0)

    for ctx in range(ctx_count):
        query = jnp.concatenate(
            [span_ref[ctx, :, h * HEAD_DIM : (h + 1) * HEAD_DIM] for h in range(heads)], axis=0
        )
        parts = [(begin, chunk, False) for begin in range(0, prefix, chunk)]
        if ctx:
            parts.append((prefix, ctx * tok_count, False))
        parts.append((prefix + ctx * tok_count, tok_count, True))
        scores = []
        for begin, size, diagonal in parts:
            part = lax.dot_general(
                query,
                k_ref[begin : begin + size, :],
                (((1,), (1,)), ((), ())),
                preferred_element_type=jnp.float32,
            )
            scores.append(jnp.where(causal, part, NEG_FILL) if diagonal else part)
        peak = functools.reduce(
            jnp.maximum, [jnp.max(part, axis=1, keepdims=True) for part in scores]
        )
        total = None
        for (begin, size, _), part in zip(parts, scores):
            weights = jnp.exp2((part - peak) * EXP2_SCALE).astype(jnp.bfloat16)
            term = jnp.dot(
                weights, v_ref[begin : begin + size, :], preferred_element_type=jnp.float32
            )
            total = term if total is None else total + term
        mixed = (total[:, :HEAD_DIM] / total[:, HEAD_DIM:]).astype(jnp.bfloat16)
        for h in range(heads):
            out_ref[ctx, :, h * HEAD_DIM : (h + 1) * HEAD_DIM] = mixed[
                h * tok_count : (h + 1) * tok_count
            ]


def attend(page_ids, prefix_pages, span, pages, pages_dev):
    ctx_count, tok_count, width = span.shape
    pool_count = page_ids.shape[0]
    page = pages[0].shape[2]
    prefix = pool_count * CAP * page
    rows = prefix + ctx_count * tok_count
    heads = width // HEAD_DIM - 2
    return pl.pallas_call(
        functools.partial(attend_kernel, 512, pages_dev),
        out_shape=jax.ShapeDtypeStruct((ctx_count, tok_count, heads * HEAD_DIM), jnp.bfloat16),
        in_specs=[SMEM, SMEM, VMEM] + [VMEM] * pool_count,
        out_specs=VMEM,
        scratch_shapes=[
            pltpu.VMEM((rows, HEAD_DIM), jnp.bfloat16),
            pltpu.VMEM((rows, 2 * HEAD_DIM), jnp.bfloat16),
            pltpu.SMEM((pool_count,), jnp.int32),
        ],
        compiler_params=pltpu.CompilerParams(vmem_limit_bytes=56 * 2**20),
        name="attend",
    )(page_ids, prefix_pages, span, *pages)


def body(queries, span_keys, span_values, pool_keys, pool_values, page_ids, prefix_pages):
    tok_count = queries.shape[1]
    pool_count = lax.axis_size("pool")
    pages = prep_pages(page_ids, prefix_pages, pool_keys, pool_values)
    fetched = [pages[0]]
    for step in range(1, pool_count):
        pairs = [(i, i ^ step) for i in range(pool_count)]
        fetched.append(lax.ppermute(pages[step], "pool", pairs))
    span = lax.all_to_all(
        prep_span(queries, span_keys, span_values), "cp", split_axis=0, concat_axis=0, tiled=True
    )
    mixed = attend(page_ids, prefix_pages, span, fetched, pool_keys.shape[0])
    mixed = lax.all_to_all(mixed, "cp", split_axis=0, concat_axis=0, tiled=True)
    attended = mixed.transpose(1, 0, 2).astype(jnp.float32)
    return attended.reshape(1, tok_count, HEADS * HEAD_DIM)


def solution(mesh):
    in_specs = (
        P("pool", "cp", None),
        P("pool", "cp", None),
        P("pool", "cp", None),
        P("pool", None, None),
        P("pool", None, None),
        P(),
        P(),
    )
    out_specs = P("pool", "cp", None)
    return jax.shard_map(body, mesh=mesh, in_specs=in_specs, out_specs=out_specs, check_vma=False)
```

time: 207 us -> 150 us (0.72); the launches traced: 204 us -> 150 us
  Pallas kernels: 0 us -> 92.8 us
  blocking collectives: 62.1 us -> 18.9 us
  matrix products: 42.4 us -> 0 us
  local copies, waits for them, and re-layouts: 41.4 us -> 5.78 us
  other arithmetic: 29.6 us -> 0.23 us
  between operations: 13.6 us -> 0.09 us
  starting transfers between devices: 0.04 us -> 8.79 us
  waiting for transfers between devices: 14.7 us -> 23 us
    pallas_call x0 -> x3, Pallas kernels: none -> 92.8 us  [the longest x1 40.9 us: prep_span(): pl.pallas_call(prep_span_kernel, out_shape=jax.ShapeDtypeStruct((ctx_coun...]
    dot_general x10 -> x0, matrix products: 42.4 us -> none  [the longest x5 21.4 us: block_step(): jnp.einsum('unqy,ynx->unqx', softmax_weights, value_tile, preferred_eleme...]
    reduce_sum x8 -> x0, other arithmetic: 27.9 us -> none  [the longest x5 27.3 us: block_step(): jnp.sum(softmax_weights, axis=-1, dtype=jnp.float32)]
    all_gather x2 -> x0, blocking collectives: 26.4 us -> none  [the longest x1 16 us: body(): value_piece = lax.all_gather(span_values, 'cp', axis=1, tiled=True)]
    ppermute x0 -> x7, waiting for transfers between devices: none -> 22.9 us  [body(): fetched.append(lax.ppermute(pages[step], 'pool', pairs))]
    dynamic_slice x13 -> x0, local copies, waits for them, and re-layouts: 19.9 us -> none  [the longest x12 18.3 us: attend(): lax.scan(block_step, running, (key_blocks, value_blocks, vis_blocks))[0]]
    all_to_all x2 -> x1, blocking collectives: 35.7 us -> 18.9 us  [body(): mixed = lax.all_to_all(mixed, 'cp', split_axis=0, concat_axis=0, tiled=True)]
    all_gather x2 -> x0, waiting for transfers between devices: 14.7 us -> none  [the longest x1 14.7 us: body(): lax.all_gather(fetched_values, 'cp', axis=2, tiled=True).reshape(-1, width)]
  transfers between devices with their start and end apart: 2 -> 8, of which waited for: 1 -> 6; matrix products, arithmetic and copies ran while one was open for 8% -> 0% of each run, Pallas kernels for 0% -> 23%
where the time goes in v1:
time: 150 us
  Pallas kernels  92.8 us (62%)
  waiting for transfers between devices  23 us (15%)
  blocking collectives  18.9 us (13%)
  starting transfers between devices  8.79 us (6%)
  local copies, waits for them, and re-layouts  5.78 us (4%)
    pallas_call x1, Pallas kernels, prep_span(): pl.pallas_call(prep_span_kernel, out_shape=jax.ShapeDtypeStruct((ctx_coun...  40.9 us
    pallas_call x1, Pallas kernels, prep_pages(): pl.pallas_call(prep_pages_kernel, out_shape=[shape] * pool_count, in_spec...  34 us
    ppermute x7, waiting for transfers between devices, body(): fetched.append(lax.ppermute(pages[step], 'pool', pairs))  22.9 us
    all_to_all x1, blocking collectives, body(): mixed = lax.all_to_all(mixed, 'cp', split_axis=0, concat_axis=0, tiled=True)  18.9 us
    pallas_call x1, Pallas kernels, attend(): pl.pallas_call(functools.partial(attend_kernel, 512, pages_dev), out_shap...  17.9 us
    ppermute x7, starting transfers between devices, body(): fetched.append(lax.ppermute(pages[step], 'pool', pairs))  5.06 us
    reshape x2, local copies, waits for them, and re-layouts, body(): return attended.reshape(1, tok_count, HEADS * HEAD_DIM)  4.72 us
    all_to_all x1, starting transfers between devices, body(): lax.all_to_all(prep_span(queries, span_keys, span_values), 'cp', split_ax...  3.73 us
  transfers between devices with their start and end apart: 8, of which 6 were waited for; matrix products, arithmetic and copies ran while one was open for 0% of the time, Pallas kernels for 23%

profile of v1, /device:TPU:16, one launch (start us, length us, event | category | flops | bytes accessed | tf_op | source)
XLA Modules:
  0.0 149.6 jit_solution(2089047030345982449)
XLA Ops:
  0.0 40.9 %prep_span.1 = bf16[4,128,1280]{2,1,0:T(8,128)(2,1)} custom-call(bf16[1,128,4096]{2,1,0:T(8,128)(2,1)} %q_ref.1, bf16[1,128,512]{2,1,0:T(8,128)(2,1)} %k_ref.1, bf16[1,128,512]{2,1,0:T(8,128)(2,1)} %v_ref.1), custom_call_target="tpu_custom_call" | custom-call | tf_op jit(solution)/shard_map/prep_span/pallas_call | solution.py:108
  40.9 3.7 %all-to-all-start = ((bf16[4,128,1280]{2,1,0:T(8,128)(2,1)}), bf16[4,128,1280]{2,1,0:T(8,128)(2,1)S(1)}, u32[]{:S(2)}, u32[]{:S(2)}) async-start(bf16[4,128,1280]{2,1,0:T(8,128)(2,1)} %prep_span.1), calls=%async_computation | async-start | bytes 2621440 | tf_op jit(solution)/shard_map/all_to_all | solution.py:220
  44.6 34.0 %prep_pages.1 = (bf16[2,2,128,128]{3,2,1,0:T(8,128)(2,1)}, bf16[2,2,128,128]{3,2,1,0:T(8,128)(2,1)}, bf16[2,2,128,128]{3,2,1,0:T(8,128)(2,1)}, bf16[2,2,128,128]...) custom-call(s32[8,16]{1,0:T(8,128)} %ids_ref.3, ...), custom_call_target="tpu_custom_call" | custom-call | tf_op jit(solution)/shard_map/prep_pages/pallas_call | solution.py:67
  78.6 0.1 collective-permute-start
  78.7 1.6 %collective-permute-start.1 = (bf16[2,2,128,128]{3,2,1,0:T(8,128)(2,1)}, bf16[2,2,128,128]{3,2,1,0:T(8,128)(2,1)S(1)}, u32[]{:S(2)}, u32[]{:S(2)}) collective-permute-start(bf16[2,2,128,128]{3,2,1,0:T(8,128)(2,1)} %get-tuple-element.15), channel_id=1, source_target_pairs={{0,8},{4,12},{8,0},{12,4},{16,24},{20,28},{24,16},{28,20},{1,9},{5... | collective-permute-start | bytes 393224 | tf_op jit(solution)/shard_map/ppermute | solution.py:219
  80.4 0.2 collective-permute-start.2
  80.6 0.3 collective-permute-start.3
  80.9 2.3 %collective-permute-start.4 = (bf16[2,2,128,128]{3,2,1,0:T(8,128)(2,1)}, bf16[2,2,128,128]{3,2,1,0:T(8,128)(2,1)S(1)}, u32[]{:S(2)}, u32[]{:S(2)}) collective-permute-start(bf16[2,2,128,128]{3,2,1,0:T(8,128)(2,1)} %get-tuple-element.18), channel_id=1, source_target_pairs={{0,20},{4,16},{8,28},{12,24},{16,4},{20,0},{24,12},{28,8},{1,21},{... | collective-permute-start | bytes 393224 | tf_op jit(solution)/shard_map/ppermute | solution.py:219
  83.2 0.0 collective-permute-done.rest_1_
  83.2 0.0 copy-start.1
  83.2 0.5 collective-permute-start.5
  83.7 3.2 %collective-permute-done.1.rest_2_ = bf16[2,2,128,128]{3,2,1,0:T(8,128)(2,1)S(1)} collective-permute-done((bf16[2,2,128,128]{3,2,1,0:T(8,128)(2,1)}, bf16[2,2,128,128]{3,2,1,0:T(8,128)(2,1)S(1)}, u32[]{:S(2)}, u32[]{:S(2)}) %collective-permute-start.1) | collective-permute-done | bytes 131104 | tf_op jit(solution)/shard_map/ppermute | solution.py:219
  86.9 0.0 copy-start.2
  86.9 0.0 collective-permute-start.6
  86.9 2.8 %collective-permute-done.2.rest_3_ = bf16[2,2,128,128]{3,2,1,0:T(8,128)(2,1)S(1)} collective-permute-done((bf16[2,2,128,128]{3,2,1,0:T(8,128)(2,1)}, bf16[2,2,128,128]{3,2,1,0:T(8,128)(2,1)S(1)}, u32[]{:S(2)}, u32[]{:S(2)}) %collective-permute-start.2) | collective-permute-done | bytes 131104 | tf_op jit(solution)/shard_map/ppermute | solution.py:219
  89.7 0.0 copy-start.3
  89.7 1.2 collective-permute-done.3.rest_4_
  90.9 0.0 copy-start.4
  90.9 7.7 %collective-permute-done.4.rest_5_ = bf16[2,2,128,128]{3,2,1,0:T(8,128)(2,1)S(1)} collective-permute-done((bf16[2,2,128,128]{3,2,1,0:T(8,128)(2,1)}, bf16[2,2,128,128]{3,2,1,0:T(8,128)(2,1)S(1)}, u32[]{:S(2)}, u32[]{:S(2)}) %collective-permute-start.4) | collective-permute-done | bytes 131104 | tf_op jit(solution)/shard_map/ppermute | solution.py:219
  98.6 0.0 copy-start.5
  98.6 6.4 %collective-permute-done.5.rest_6_ = bf16[2,2,128,128]{3,2,1,0:T(8,128)(2,1)S(1)} collective-permute-done((bf16[2,2,128,128]{3,2,1,0:T(8,128)(2,1)}, bf16[2,2,128,128]{3,2,1,0:T(8,128)(2,1)S(1)}, u32[]{:S(2)}, u32[]{:S(2)}) %collective-permute-start.5) | collective-permute-done | bytes 131104 | tf_op jit(solution)/shard_map/ppermute | solution.py:219
  105.0 0.0 copy-start.6
  105.0 1.7 %collective-permute-done.6.rest_7_ = bf16[2,2,128,128]{3,2,1,0:T(8,128)(2,1)S(1)} collective-permute-done((bf16[2,2,128,128]{3,2,1,0:T(8,128)(2,1)}, bf16[2,2,128,128]{3,2,1,0:T(8,128)(2,1)S(1)}, u32[]{:S(2)}, u32[]{:S(2)}) %collective-permute-start.6) | collective-permute-done | bytes 131104 | tf_op jit(solution)/shard_map/ppermute | solution.py:219
  106.7 0.0 copy-start.7
  106.7 0.0 all-to-all-done.span_ref
  106.7 0.0 copy-start
  106.7 0.0 copy-done.1
  106.7 0.0 copy-done.2
  106.7 0.0 copy-done.3
  106.7 0.0 copy-done.4
  106.7 0.0 copy-done.5
  106.7 0.0 copy-done.6
  106.8 0.6 copy-done.7
  107.3 0.4 copy-done
  107.8 17.9 %attend.1 = bf16[4,128,1024]{2,1,0:T(8,128)(2,1)} custom-call(s32[8,16]{1,0:T(8,128)} %ids_ref.3, s32[8]{0:T(128)} %len_ref.3, bf16[4,128,1280]{2,1,0:T(8,128)(2,1)} %copy-done, bf16[2,2,128,128]{3,2,1,0:T(8,128)(2,1)} %get-tuple-element.13.rest_0_, bf16[2,2,128,128]{3,2,1,0:T(8,128)(2,1)} %copy-done.1, bf16[2,2,128,128]{3,2,1,0:T(8,128)(2,1)} %copy-done.2, ...), custom_call_target="tpu_custom_call" | custom-call | tf_op jit(solution)/shard_map/attend/pallas_call | solution.py:197
  125.7 18.9 %all_to_all.10 = bf16[4,128,1024]{2,1,0:T(8,128)(2,1)S(1)} all-to-all(bf16[4,128,1024]{2,1,0:T(8,128)(2,1)} %attend.1), channel_id=1, replica_groups=mesh['pool'=8,'cp'=4] {'cp'}, dimensions={0} | all-to-all | bytes 2097152 | tf_op jit(solution)/shard_map/all_to_all | solution.py:224
  144.6 0.2 convert_bitcast_fusion
  144.9 1.8 %copy.8 = f32[128,4,1024]{0,2,1:T(8,128)} copy(f32[128,4,1024]{2,0,1:T(8,128)S(1)} %convert_bitcast_fusion) | data formatting | bytes 4194304 | tf_op jit(solution)/shard_map/reshape | solution.py:226
  146.7 2.9 %copy.9 = f32[1,128,4096]{2,1,0:T(8,128)} copy(f32[1,128,4096]{1,2,0:T(8,128)} %bitcast.3) | data formatting | bytes 4194304 | tf_op jit(solution)/shard_map/reshape | solution.py:226
Async XLA Ops:
  40.9 65.8 %all-to-all-start = ((bf16[4,128,1280]{2,1,0:T(8,128)(2,1)}), bf16[4,128,1280]{2,1,0:T(8,128)(2,1)S(1)}, u32[]{:S(2)}, u32[]{:S(2)}) async-start(bf16[4,128,1280]{2,1,0:T(8,128)(2,1)} %prep_span.1), calls=%async_computation | async-start | bytes 2621440 | tf_op jit(solution)/shard_map/all_to_all | solution.py:220
  78.6 4.5 %collective-permute-start = (bf16[2,2,128,128]{3,2,1,0:T(8,128)(2,1)}, bf16[2,2,128,128]{3,2,1,0:T(8,128)(2,1)S(1)}, u32[]{:S(2)}, u32[]{:S(2)}) collective-permute-start(bf16[2,2,128,128]{3,2,1,0:T(8,128)(2,1)} %get-tuple-element.14), channel_id=1, source_target_pairs={{0,4},{4,0},{8,12},{12,8},{16,20},{20,16},{24,28},{28,24},{1,5},{5... | collective-permute-start | bytes 393224 | tf_op jit(solution)/shard_map/ppermute | solution.py:219
  78.7 8.2 %collective-permute-start.1 = (bf16[2,2,128,128]{3,2,1,0:T(8,128)(2,1)}, bf16[2,2,128,128]{3,2,1,0:T(8,128)(2,1)S(1)}, u32[]{:S(2)}, u32[]{:S(2)}) collective-permute-start(bf16[2,2,128,128]{3,2,1,0:T(8,128)(2,1)} %get-tuple-element.15), channel_id=1, source_target_pairs={{0,8},{4,12},{8,0},{12,4},{16,24},{20,28},{24,16},{28,20},{1,9},{5... | collective-permute-start | bytes 393224 | tf_op jit(solution)/shard_map/ppermute | solution.py:219
  80.4 9.3 %collective-permute-start.2 = (bf16[2,2,128,128]{3,2,1,0:T(8,128)(2,1)}, bf16[2,2,128,128]{3,2,1,0:T(8,128)(2,1)S(1)}, u32[]{:S(2)}, u32[]{:S(2)}) collective-permute-start(bf16[2,2,128,128]{3,2,1,0:T(8,128)(2,1)} %get-tuple-element.16), channel_id=1, source_target_pairs={{0,12},{4,8},{8,4},{12,0},{16,28},{20,24},{24,20},{28,16},{1,13},{... | collective-permute-start | bytes 393224 | tf_op jit(solution)/shard_map/ppermute | solution.py:219
  80.6 10.3 %collective-permute-start.3 = (bf16[2,2,128,128]{3,2,1,0:T(8,128)(2,1)}, bf16[2,2,128,128]{3,2,1,0:T(8,128)(2,1)S(1)}, u32[]{:S(2)}, u32[]{:S(2)}) collective-permute-start(bf16[2,2,128,128]{3,2,1,0:T(8,128)(2,1)} %get-tuple-element.17), channel_id=1, source_target_pairs={{0,16},{4,20},{8,24},{12,28},{16,0},{20,4},{24,8},{28,12},{1,17},{... | collective-permute-start | bytes 393224 | tf_op jit(solution)/shard_map/ppermute | solution.py:219
  80.9 17.7 %collective-permute-start.4 = (bf16[2,2,128,128]{3,2,1,0:T(8,128)(2,1)}, bf16[2,2,128,128]{3,2,1,0:T(8,128)(2,1)S(1)}, u32[]{:S(2)}, u32[]{:S(2)}) collective-permute-start(bf16[2,2,128,128]{3,2,1,0:T(8,128)(2,1)} %get-tuple-element.18), channel_id=1, source_target_pairs={{0,20},{4,16},{8,28},{12,24},{16,4},{20,0},{24,12},{28,8},{1,21},{... | collective-permute-start | bytes 393224 | tf_op jit(solution)/shard_map/ppermute | solution.py:219
  83.2 23.5 %copy-start.1 = (bf16[2,2,128,128]{3,2,1,0:T(8,128)(2,1)}, bf16[2,2,128,128]{3,2,1,0:T(8,128)(2,1)S(1)}, u32[]{:S(2)}) copy-start(bf16[2,2,128,128]{3,2,1,0:T(8,128)(2,1)S(1)} %collective-permute-done.rest_1_) | copy-start | bytes 393220
  83.2 21.8 %collective-permute-start.5 = (bf16[2,2,128,128]{3,2,1,0:T(8,128)(2,1)}, bf16[2,2,128,128]{3,2,1,0:T(8,128)(2,1)S(1)}, u32[]{:S(2)}, u32[]{:S(2)}) collective-permute-start(bf16[2,2,128,128]{3,2,1,0:T(8,128)(2,1)} %get-tuple-element.19), channel_id=1, source_target_pairs={{0,24},{4,28},{8,16},{12,20},{16,8},{20,12},{24,0},{28,4},{1,25},{... | collective-permute-start | bytes 393224 | tf_op jit(solution)/shard_map/ppermute | solution.py:219
  86.9 19.8 %copy-start.2 = (bf16[2,2,128,128]{3,2,1,0:T(8,128)(2,1)}, bf16[2,2,128,128]{3,2,1,0:T(8,128)(2,1)S(1)}, u32[]{:S(2)}) copy-start(bf16[2,2,128,128]{3,2,1,0:T(8,128)(2,1)S(1)} %collective-permute-done.1.rest_2_) | copy-start | bytes 393220
  86.9 19.8 %collective-permute-start.6 = (bf16[2,2,128,128]{3,2,1,0:T(8,128)(2,1)}, bf16[2,2,128,128]{3,2,1,0:T(8,128)(2,1)S(1)}, u32[]{:S(2)}, u32[]{:S(2)}) collective-permute-start(bf16[2,2,128,128]{3,2,1,0:T(8,128)(2,1)} %get-tuple-element.20), channel_id=1, source_target_pairs={{0,28},{4,24},{8,20},{12,16},{16,12},{20,8},{24,4},{28,0},{1,29},{... | collective-permute-start | bytes 393224 | tf_op jit(solution)/shard_map/ppermute | solution.py:219
  89.7 17.0 %copy-start.3 = (bf16[2,2,128,128]{3,2,1,0:T(8,128)(2,1)}, bf16[2,2,128,128]{3,2,1,0:T(8,128)(2,1)S(1)}, u32[]{:S(2)}) copy-start(bf16[2,2,128,128]{3,2,1,0:T(8,128)(2,1)S(1)} %collective-permute-done.2.rest_3_) | copy-start | bytes 393220
  90.9 15.8 %copy-start.4 = (bf16[2,2,128,128]{3,2,1,0:T(8,128)(2,1)}, bf16[2,2,128,128]{3,2,1,0:T(8,128)(2,1)S(1)}, u32[]{:S(2)}) copy-start(bf16[2,2,128,128]{3,2,1,0:T(8,128)(2,1)S(1)} %collective-permute-done.3.rest_4_) | copy-start | bytes 393220
  98.6 8.1 %copy-start.5 = (bf16[2,2,128,128]{3,2,1,0:T(8,128)(2,1)}, bf16[2,2,128,128]{3,2,1,0:T(8,128)(2,1)S(1)}, u32[]{:S(2)}) copy-start(bf16[2,2,128,128]{3,2,1,0:T(8,128)(2,1)S(1)} %collective-permute-done.4.rest_5_) | copy-start | bytes 393220
  105.0 1.7 %copy-start.6 = (bf16[2,2,128,128]{3,2,1,0:T(8,128)(2,1)}, bf16[2,2,128,128]{3,2,1,0:T(8,128)(2,1)S(1)}, u32[]{:S(2)}) copy-start(bf16[2,2,128,128]{3,2,1,0:T(8,128)(2,1)S(1)} %collective-permute-done.5.rest_6_) | copy-start | bytes 393220
  106.7 0.7 copy-start.7
  106.7 1.1 copy-start

commit v2 on v1

--- a/solution.py
+++ b/solution.py
@@ -68,7 +68,7 @@
         prep_pages_kernel,
         out_shape=[shape] * pool_count,
         in_specs=[SMEM, SMEM, ANY, ANY],
-        out_specs=[ANY] * pool_count,
+        out_specs=[VMEM] * pool_count,
         scratch_shapes=[
             pltpu.SMEM((pool_count, CAP + 1), jnp.int32),
             pltpu.SemaphoreType.DMA((pool_count, 2, CAP)),
@@ -77,42 +77,43 @@
     )(page_ids, prefix_pages, pool_keys, pool_values)
 
 
-def prep_span_kernel(q_ref, k_ref, v_ref, out_ref, sems):
+def prep_span_kernel(q_ref, k_ref, v_ref, _, out_ref):
     ctx_count = out_ref.shape[0]
     width = HEADS // ctx_count * HEAD_DIM
-    copies = []
     for ctx in range(ctx_count):
         head = kv_head(ctx, ctx_count) * HEAD_DIM
-        for part, (source, begin, size, place) in enumerate(
-            (
-                (q_ref, ctx * width, width, 0),
-                (k_ref, head, HEAD_DIM, width),
-                (v_ref, head, HEAD_DIM, width + HEAD_DIM),
-            )
-        ):
-            copy = pltpu.make_async_copy(
-                source.at[0, :, pl.ds(begin, size)],
-                out_ref.at[ctx, :, pl.ds(place, size)],
-                sems.at[ctx, part],
-            )
-            copy.start()
-            copies.append(copy)
-    for copy in copies:
-        copy.wait()
-
-
-def prep_span(queries, span_keys, span_values):
+        out_ref[ctx, :, :width] = q_ref[0, :, ctx * width : (ctx + 1) * width]
+        out_ref[ctx, :, width : width + HEAD_DIM] = k_ref[0, :, head : head + HEAD_DIM]
+        out_ref[ctx, :, width + HEAD_DIM :] = v_ref[0, :, head : head + HEAD_DIM]
+
+
+def prep_span(queries, span_keys, span_values, after):
     ctx_count = lax.axis_size("cp")
     tok_count = queries.shape[1]
     width = (HEADS // ctx_count + 2) * HEAD_DIM
     return pl.pallas_call(
         prep_span_kernel,
         out_shape=jax.ShapeDtypeStruct((ctx_count, tok_count, width), jnp.bfloat16),
-        in_specs=[ANY] * 3,
-        out_specs=ANY,
-        scratch_shapes=[pltpu.SemaphoreType.DMA((ctx_count, 3))],
+        in_specs=[VMEM] * 3 + [ANY],
+        out_specs=VMEM,
         name="prep_span",
-    )(queries, span_keys, span_values)
+    )(queries, span_keys, span_values, after)
+
+
+def widen_kernel(in_ref, out_ref):
+    out_ref[0] = in_ref[0].astype(jnp.float32)
+
+
+def widen(mixed):
+    count, tok_count, width = mixed.shape
+    return pl.pallas_call(
+        widen_kernel,
+        grid=(count,),
+        out_shape=jax.ShapeDtypeStruct((1, tok_count, count * width), jnp.float32),
+        in_specs=[pl.BlockSpec((1, tok_count, width), lambda i: (i, 0, 0))],
+        out_specs=pl.BlockSpec((1, tok_count, width), lambda i: (0, 0, i)),
+        name="widen",
+    )(mixed)
 
 
 def attend_kernel(chunk, pages_dev, ids_ref, len_ref, span_ref, *rest):
@@ -210,7 +211,6 @@
 
 
 def body(queries, span_keys, span_values, pool_keys, pool_values, page_ids, prefix_pages):
-    tok_count = queries.shape[1]
     pool_count = lax.axis_size("pool")
     pages = prep_pages(page_ids, prefix_pages, pool_keys, pool_values)
     fetched = [pages[0]]
@@ -218,12 +218,11 @@
         pairs = [(i, i ^ step) for i in range(pool_count)]
         fetched.append(lax.ppermute(pages[step], "pool", pairs))
     span = lax.all_to_all(
-        prep_span(queries, span_keys, span_values), "cp", split_axis=0, concat_axis=0, tiled=True
+        prep_span(queries, span_keys, span_values, pages[0]), "cp", split_axis=0, concat_axis=0, tiled=True
     )
     mixed = attend(page_ids, prefix_pages, span, fetched, pool_keys.shape[0])
     mixed = lax.all_to_all(mixed, "cp", split_axis=0, concat_axis=0, tiled=True)
-    attended = mixed.transpose(1, 0, 2).astype(jnp.float32)
-    return attended.reshape(1, tok_count, HEADS * HEAD_DIM)
+    return widen(mixed)
 
 
 def solution(mesh):

time: 150 us -> 81.1 us (0.54)
  Pallas kernels: 92.8 us -> 28.2 us
  local copies, waits for them, and re-layouts: 5.78 us -> 1.7 us
    pallas_call x1, Pallas kernels: 40.9 us -> 2.56 us  [prep_span(): pl.pallas_call(prep_span_kernel, out_shape=jax.ShapeDtypeStruct((ctx_coun...]
    pallas_call x1, Pallas kernels: 34 us -> 4.15 us  [prep_pages(): pl.pallas_call(prep_pages_kernel, out_shape=[shape] * pool_count, in_spec...]
    reshape x2 -> x0, local copies, waits for them, and re-layouts: 4.72 us -> none  [body(): return attended.reshape(1, tok_count, HEADS * HEAD_DIM)]
    pallas_call x0 -> x1, Pallas kernels: none -> 3.57 us  [widen(): pl.pallas_call(widen_kernel, grid=(count,), out_shape=jax.ShapeDtypeStruc...]
  transfers between devices with their start and end apart: 8 -> 8, of which waited for: 6 -> 6; matrix products, arithmetic and copies ran while one was open for 0% -> 0% of each run, Pallas kernels for 23% -> 0%
where the time goes in v2:
time: 81.1 us; the launch traced here: 80.6 us
  Pallas kernels  28.2 us (35%)
  waiting for transfers between devices  22.6 us (28%)
  blocking collectives  19.5 us (24%)
  starting transfers between devices  8.41 us (10%)
  local copies, waits for them, and re-layouts  1.7 us (2%)
    ppermute x7, waiting for transfers between devices, body(): fetched.append(lax.ppermute(pages[step], 'pool', pairs))  22.6 us
    all_to_all x1, blocking collectives, body(): mixed = lax.all_to_all(mixed, 'cp', split_axis=0, concat_axis=0, tiled=True)  19.5 us
    pallas_call x1, Pallas kernels, attend(): pl.pallas_call(functools.partial(attend_kernel, 512, pages_dev), out_shap...  17.9 us
    ppermute x7, starting transfers between devices, body(): fetched.append(lax.ppermute(pages[step], 'pool', pairs))  4.71 us
    pallas_call x1, Pallas kernels, prep_pages(): pl.pallas_call(prep_pages_kernel, out_shape=[shape] * pool_count, in_spec...  4.15 us
    all_to_all x1, starting transfers between devices, body(): lax.all_to_all(prep_span(queries, span_keys, span_values, pages[0]), 'cp'...  3.7 us
    pallas_call x1, Pallas kernels, widen(): pl.pallas_call(widen_kernel, grid=(count,), out_shape=jax.ShapeDtypeStruc...  3.57 us
    pallas_call x1, Pallas kernels, prep_span(): pl.pallas_call(prep_span_kernel, out_shape=jax.ShapeDtypeStruct((ctx_coun...  2.56 us
  transfers between devices with their start and end apart: 8, of which 6 were waited for; matrix products, arithmetic and copies ran while one was open for 0% of the time, Pallas kernels for 0%

profile of v2, /device:TPU:16, one launch (start us, length us, event | category | flops | bytes accessed | tf_op | source)
XLA Modules:
  0.0 80.6 jit_solution(15242930832153895223)
XLA Ops:
  0.0 4.1 %prep_pages.1 = (bf16[2,2,128,128]{3,2,1,0:T(8,128)(2,1)}, bf16[2,2,128,128]{3,2,1,0:T(8,128)(2,1)}, bf16[2,2,128,128]{3,2,1,0:T(8,128)(2,1)}, bf16[2,2,128,128]...) custom-call(s32[8,16]{1,0:T(8,128)} %ids_ref.3, ...), custom_call_target="tpu_custom_call" | custom-call | tf_op jit(solution)/shard_map/prep_pages/pallas_call | solution.py:67
  4.2 0.0 copy-start.14
  4.2 0.0 copy-start.13
  4.2 0.0 copy-start.12
  4.2 0.0 copy-start.11
  4.2 0.0 copy-start.10
  4.2 0.0 copy-start.9
  4.2 0.0 copy-start.8
  4.2 2.6 %prep_span.1 = bf16[4,128,1280]{2,1,0:T(8,128)(2,1)} custom-call(bf16[1,128,4096]{2,1,0:T(8,128)(2,1)} %q_ref.1, bf16[1,128,512]{2,1,0:T(8,128)(2,1)} %k_ref.1, bf16[1,128,512]{2,1,0:T(8,128)(2,1)} %v_ref.1, bf16[2,2,128,128]{3,2,1,0:T(8,128)(2,1)} %get-tuple-element.13._.rest_0_), custom_call_target="tpu_custom_call" | custom-call | tf_op jit(solution)/shard_map/prep_span/pallas_call | solution.py:94
  6.8 3.7 %all-to-all-start = ((bf16[4,128,1280]{2,1,0:T(8,128)(2,1)}), bf16[4,128,1280]{2,1,0:T(8,128)(2,1)S(1)}, u32[]{:S(2)}, u32[]{:S(2)}) async-start(bf16[4,128,1280]{2,1,0:T(8,128)(2,1)} %prep_span.1), calls=%async_computation | async-start | bytes 2621440 | tf_op jit(solution)/shard_map/all_to_all | solution.py:220
  10.5 0.0 copy-done.14
  10.5 0.0 collective-permute-start
  10.5 0.0 copy-done.13
  10.5 1.2 %collective-permute-start.1 = (bf16[2,2,128,128]{3,2,1,0:T(8,128)(2,1)S(1)}, bf16[2,2,128,128]{3,2,1,0:T(8,128)(2,1)S(1)}, u32[]{:S(2)}, u32[]{:S(2)}) collective-permute-start(bf16[2,2,128,128]{3,2,1,0:T(8,128)(2,1)S(1)} %copy-done.13), channel_id=1, source_target_pairs={{0,8},{4,12},{8,0},{12,4},{16,24},{20,28},{24,16},{28,20},{1,9},{5... | collective-permute-start | bytes 393224 | tf_op jit(solution)/shard_map/ppermute | solution.py:219
  11.7 0.0 copy-done.12
  11.7 0.7 collective-permute-start.2
  12.4 0.0 copy-done.11
  12.4 0.0 collective-permute-start.3
  12.4 0.0 copy-done.10
  12.4 2.6 %collective-permute-start.4 = (bf16[2,2,128,128]{3,2,1,0:T(8,128)(2,1)S(1)}, bf16[2,2,128,128]{3,2,1,0:T(8,128)(2,1)S(1)}, u32[]{:S(2)}, u32[]{:S(2)}) collective-permute-start(bf16[2,2,128,128]{3,2,1,0:T(8,128)(2,1)S(1)} %copy-done.10), channel_id=1, source_target_pairs={{0,20},{4,16},{8,28},{12,24},{16,4},{20,0},{24,12},{28,8},{1,21},{... | collective-permute-start | bytes 393224 | tf_op jit(solution)/shard_map/ppermute | solution.py:219
  15.0 0.0 collective-permute-done.rest_1_
  15.0 0.0 copy-start.1
  15.0 0.0 copy-done.9
  15.0 0.3 collective-permute-start.5
  15.2 2.9 %collective-permute-done.1.rest_2_ = bf16[2,2,128,128]{3,2,1,0:T(8,128)(2,1)S(1)} collective-permute-done((bf16[2,2,128,128]{3,2,1,0:T(8,128)(2,1)S(1)}, bf16[2,2,128,128]{3,2,1,0:T(8,128)(2,1)S(1)}, u32[]{:S(2)}, u32[]{:S(2)}) %collective-permute-start.1) | collective-permute-done | bytes 131104 | tf_op jit(solution)/shard_map/ppermute | solution.py:219
  18.1 0.0 copy-start.2
  18.1 0.0 copy-done.8
  18.1 0.0 collective-permute-start.6
  18.1 2.8 %collective-permute-done.2.rest_3_ = bf16[2,2,128,128]{3,2,1,0:T(8,128)(2,1)S(1)} collective-permute-done((bf16[2,2,128,128]{3,2,1,0:T(8,128)(2,1)S(1)}, bf16[2,2,128,128]{3,2,1,0:T(8,128)(2,1)S(1)}, u32[]{:S(2)}, u32[]{:S(2)}) %collective-permute-start.2) | collective-permute-done | bytes 131104 | tf_op jit(solution)/shard_map/ppermute | solution.py:219
  20.9 0.0 copy-start.3
  20.9 1.3 %collective-permute-done.3.rest_4_ = bf16[2,2,128,128]{3,2,1,0:T(8,128)(2,1)S(1)} collective-permute-done((bf16[2,2,128,128]{3,2,1,0:T(8,128)(2,1)S(1)}, bf16[2,2,128,128]{3,2,1,0:T(8,128)(2,1)S(1)}, u32[]{:S(2)}, u32[]{:S(2)}) %collective-permute-start.3) | collective-permute-done | bytes 131104 | tf_op jit(solution)/shard_map/ppermute | solution.py:219
  22.2 0.0 copy-start.4
  22.2 7.8 %collective-permute-done.4.rest_5_ = bf16[2,2,128,128]{3,2,1,0:T(8,128)(2,1)S(1)} collective-permute-done((bf16[2,2,128,128]{3,2,1,0:T(8,128)(2,1)S(1)}, bf16[2,2,128,128]{3,2,1,0:T(8,128)(2,1)S(1)}, u32[]{:S(2)}, u32[]{:S(2)}) %collective-permute-start.4) | collective-permute-done | bytes 131104 | tf_op jit(solution)/shard_map/ppermute | solution.py:219
  30.0 0.0 copy-start.5
  30.0 6.1 %collective-permute-done.5.rest_6_ = bf16[2,2,128,128]{3,2,1,0:T(8,128)(2,1)S(1)} collective-permute-done((bf16[2,2,128,128]{3,2,1,0:T(8,128)(2,1)S(1)}, bf16[2,2,128,128]{3,2,1,0:T(8,128)(2,1)S(1)}, u32[]{:S(2)}, u32[]{:S(2)}) %collective-permute-start.5) | collective-permute-done | bytes 131104 | tf_op jit(solution)/shard_map/ppermute | solution.py:219
  36.2 1.7 %collective-permute-done.6.rest_7_ = bf16[2,2,128,128]{3,2,1,0:T(8,128)(2,1)S(1)} collective-permute-done((bf16[2,2,128,128]{3,2,1,0:T(8,128)(2,1)S(1)}, bf16[2,2,128,128]{3,2,1,0:T(8,128)(2,1)S(1)}, u32[]{:S(2)}, u32[]{:S(2)}) %collective-permute-start.6) | collective-permute-done | bytes 131104 | tf_op jit(solution)/shard_map/ppermute | solution.py:219
  37.8 0.0 all-to-all-done.span_ref
  37.8 0.0 copy-done.1
  37.8 0.0 copy-done.2
  37.8 0.0 copy-done.3
  37.9 0.0 copy-done.4
  37.9 0.0 copy-done.5
  37.9 0.0 copy-done.6
  37.9 0.6 copy-done.7
  38.5 1.1 %copy-done = bf16[4,128,1280]{2,1,0:T(8,128)(2,1)} copy-done((bf16[4,128,1280]{2,1,0:T(8,128)(2,1)}, bf16[4,128,1280]{2,1,0:T(8,128)(2,1)S(1)}, u32[]{:S(2)}) %copy-start) | copy-done | bytes 1310744
  39.5 17.9 %attend.1 = bf16[4,128,1024]{2,1,0:T(8,128)(2,1)} custom-call(s32[8,16]{1,0:T(8,128)} %ids_ref.3, s32[8]{0:T(128)} %len_ref.3, bf16[4,128,1280]{2,1,0:T(8,128)(2,1)} %copy-done, bf16[2,2,128,128]{3,2,1,0:T(8,128)(2,1)} %get-tuple-element.13._.rest_0_, bf16[2,2,128,128]{3,2,1,0:T(8,128)(2,1)} %copy-done.1, bf16[2,2,128,128]{3,2,1,0:T(8,128)(2,1)} %copy-done.2, ...), custom_call_target="tpu_custom_call" | custom-call | tf_op jit(solution)/shard_map/attend/pallas_call | solution.py:198
  57.4 19.5 %all_to_all.10.in_ref = bf16[4,128,1024]{2,1,0:T(8,128)(2,1)} all-to-all(bf16[4,128,1024]{2,1,0:T(8,128)(2,1)} %attend.1), channel_id=1, replica_groups=mesh['pool'=8,'cp'=4] {'cp'}, dimensions={0} | all-to-all | bytes 2097152 | tf_op jit(solution)/shard_map/all_to_all | solution.py:224
  77.0 3.6 %widen.1 = f32[1,128,4096]{2,1,0:T(8,128)} custom-call(bf16[4,128,1024]{2,1,0:T(8,128)(2,1)} %all_to_all.10.in_ref), custom_call_target="tpu_custom_call" | custom-call | tf_op jit(solution)/shard_map/widen/pallas_call | solution.py:109
  (3 shorter events, 0.0 us)
Async XLA Ops:
  4.2 6.3 %copy-start.14 = (bf16[2,2,128,128]{3,2,1,0:T(8,128)(2,1)S(1)}, bf16[2,2,128,128]{3,2,1,0:T(8,128)(2,1)}, u32[]{:S(2)}) copy-start(bf16[2,2,128,128]{3,2,1,0:T(8,128)(2,1)} %get-tuple-element.14) | copy-start | bytes 393220
  4.2 6.3 %copy-start.13 = (bf16[2,2,128,128]{3,2,1,0:T(8,128)(2,1)S(1)}, bf16[2,2,128,128]{3,2,1,0:T(8,128)(2,1)}, u32[]{:S(2)}) copy-start(bf16[2,2,128,128]{3,2,1,0:T(8,128)(2,1)} %get-tuple-element.15) | copy-start | bytes 393220
  4.2 7.5 %copy-start.12 = (bf16[2,2,128,128]{3,2,1,0:T(8,128)(2,1)S(1)}, bf16[2,2,128,128]{3,2,1,0:T(8,128)(2,1)}, u32[]{:S(2)}) copy-start(bf16[2,2,128,128]{3,2,1,0:T(8,128)(2,1)} %get-tuple-element.16) | copy-start | bytes 393220
  4.2 8.2 %copy-start.11 = (bf16[2,2,128,128]{3,2,1,0:T(8,128)(2,1)S(1)}, bf16[2,2,128,128]{3,2,1,0:T(8,128)(2,1)}, u32[]{:S(2)}) copy-start(bf16[2,2,128,128]{3,2,1,0:T(8,128)(2,1)} %get-tuple-element.17) | copy-start | bytes 393220
  4.2 8.2 %copy-start.10 = (bf16[2,2,128,128]{3,2,1,0:T(8,128)(2,1)S(1)}, bf16[2,2,128,128]{3,2,1,0:T(8,128)(2,1)}, u32[]{:S(2)}) copy-start(bf16[2,2,128,128]{3,2,1,0:T(8,128)(2,1)} %get-tuple-element.18) | copy-start | bytes 393220
  4.2 10.8 %copy-start.9 = (bf16[2,2,128,128]{3,2,1,0:T(8,128)(2,1)S(1)}, bf16[2,2,128,128]{3,2,1,0:T(8,128)(2,1)}, u32[]{:S(2)}) copy-start(bf16[2,2,128,128]{3,2,1,0:T(8,128)(2,1)} %get-tuple-element.19) | copy-start | bytes 393220
  4.2 13.9 %copy-start.8 = (bf16[2,2,128,128]{3,2,1,0:T(8,128)(2,1)S(1)}, bf16[2,2,128,128]{3,2,1,0:T(8,128)(2,1)}, u32[]{:S(2)}) copy-start(bf16[2,2,128,128]{3,2,1,0:T(8,128)(2,1)} %get-tuple-element.20) | copy-start | bytes 393220
  6.8 31.0 %all-to-all-start = ((bf16[4,128,1280]{2,1,0:T(8,128)(2,1)}), bf16[4,128,1280]{2,1,0:T(8,128)(2,1)S(1)}, u32[]{:S(2)}, u32[]{:S(2)}) async-start(bf16[4,128,1280]{2,1,0:T(8,128)(2,1)} %prep_span.1), calls=%async_computation | async-start | bytes 2621440 | tf_op jit(solution)/shard_map/all_to_all | solution.py:220
  10.5 4.5 %collective-permute-start = (bf16[2,2,128,128]{3,2,1,0:T(8,128)(2,1)S(1)}, bf16[2,2,128,128]{3,2,1,0:T(8,128)(2,1)S(1)}, u32[]{:S(2)}, u32[]{:S(2)}) collective-permute-start(bf16[2,2,128,128]{3,2,1,0:T(8,128)(2,1)S(1)} %copy-done.14), channel_id=1, source_target_pairs={{0,4},{4,0},{8,12},{12,8},{16,20},{20,16},{24,28},{28,24},{1,5},{5... | collective-permute-start | bytes 393224 | tf_op jit(solution)/shard_map/ppermute | solution.py:219
  10.5 7.6 %collective-permute-start.1 = (bf16[2,2,128,128]{3,2,1,0:T(8,128)(2,1)S(1)}, bf16[2,2,128,128]{3,2,1,0:T(8,128)(2,1)S(1)}, u32[]{:S(2)}, u32[]{:S(2)}) collective-permute-start(bf16[2,2,128,128]{3,2,1,0:T(8,128)(2,1)S(1)} %copy-done.13), channel_id=1, source_target_pairs={{0,8},{4,12},{8,0},{12,4},{16,24},{20,28},{24,16},{28,20},{1,9},{5... | collective-permute-start | bytes 393224 | tf_op jit(solution)/shard_map/ppermute | solution.py:219
  11.7 9.2 %collective-permute-start.2 = (bf16[2,2,128,128]{3,2,1,0:T(8,128)(2,1)S(1)}, bf16[2,2,128,128]{3,2,1,0:T(8,128)(2,1)S(1)}, u32[]{:S(2)}, u32[]{:S(2)}) collective-permute-start(bf16[2,2,128,128]{3,2,1,0:T(8,128)(2,1)S(1)} %copy-done.12), channel_id=1, source_target_pairs={{0,12},{4,8},{8,4},{12,0},{16,28},{20,24},{24,20},{28,16},{1,13},{... | collective-permute-start | bytes 393224 | tf_op jit(solution)/shard_map/ppermute | solution.py:219
  12.4 9.8 %collective-permute-start.3 = (bf16[2,2,128,128]{3,2,1,0:T(8,128)(2,1)S(1)}, bf16[2,2,128,128]{3,2,1,0:T(8,128)(2,1)S(1)}, u32[]{:S(2)}, u32[]{:S(2)}) collective-permute-start(bf16[2,2,128,128]{3,2,1,0:T(8,128)(2,1)S(1)} %copy-done.11), channel_id=1, source_target_pairs={{0,16},{4,20},{8,24},{12,28},{16,0},{20,4},{24,8},{28,12},{1,17},{... | collective-permute-start | bytes 393224 | tf_op jit(solution)/shard_map/ppermute | solution.py:219
  12.4 17.7 %collective-permute-start.4 = (bf16[2,2,128,128]{3,2,1,0:T(8,128)(2,1)S(1)}, bf16[2,2,128,128]{3,2,1,0:T(8,128)(2,1)S(1)}, u32[]{:S(2)}, u32[]{:S(2)}) collective-permute-start(bf16[2,2,128,128]{3,2,1,0:T(8,128)(2,1)S(1)} %copy-done.10), channel_id=1, source_target_pairs={{0,20},{4,16},{8,28},{12,24},{16,4},{20,0},{24,12},{28,8},{1,21},{... | collective-permute-start | bytes 393224 | tf_op jit(solution)/shard_map/ppermute | solution.py:219
  15.0 22.9 %copy-start.1 = (bf16[2,2,128,128]{3,2,1,0:T(8,128)(2,1)}, bf16[2,2,128,128]{3,2,1,0:T(8,128)(2,1)S(1)}, u32[]{:S(2)}) copy-start(bf16[2,2,128,128]{3,2,1,0:T(8,128)(2,1)S(1)} %collective-permute-done.rest_1_) | copy-start | bytes 393220
  15.0 21.2 %collective-permute-start.5 = (bf16[2,2,128,128]{3,2,1,0:T(8,128)(2,1)S(1)}, bf16[2,2,128,128]{3,2,1,0:T(8,128)(2,1)S(1)}, u32[]{:S(2)}, u32[]{:S(2)}) collective-permute-start(bf16[2,2,128,128]{3,2,1,0:T(8,128)(2,1)S(1)} %copy-done.9), channel_id=1, source_target_pairs={{0,24},{4,28},{8,16},{12,20},{16,8},{20,12},{24,0},{28,4},{1,25},{... | collective-permute-start | bytes 393224 | tf_op jit(solution)/shard_map/ppermute | solution.py:219
  18.1 19.7 %copy-start.2 = (bf16[2,2,128,128]{3,2,1,0:T(8,128)(2,1)}, bf16[2,2,128,128]{3,2,1,0:T(8,128)(2,1)S(1)}, u32[]{:S(2)}) copy-start(bf16[2,2,128,128]{3,2,1,0:T(8,128)(2,1)S(1)} %collective-permute-done.1.rest_2_) | copy-start | bytes 393220
  18.1 19.7 %collective-permute-start.6 = (bf16[2,2,128,128]{3,2,1,0:T(8,128)(2,1)S(1)}, bf16[2,2,128,128]{3,2,1,0:T(8,128)(2,1)S(1)}, u32[]{:S(2)}, u32[]{:S(2)}) collective-permute-start(bf16[2,2,128,128]{3,2,1,0:T(8,128)(2,1)S(1)} %copy-done.8), channel_id=1, source_target_pairs={{0,28},{4,24},{8,20},{12,16},{16,12},{20,8},{24,4},{28,0},{1,29},{... | collective-permute-start | bytes 393224 | tf_op jit(solution)/shard_map/ppermute | solution.py:219
  20.9 16.9 %copy-start.3 = (bf16[2,2,128,128]{3,2,1,0:T(8,128)(2,1)}, bf16[2,2,128,128]{3,2,1,0:T(8,128)(2,1)S(1)}, u32[]{:S(2)}) copy-start(bf16[2,2,128,128]{3,2,1,0:T(8,128)(2,1)S(1)} %collective-permute-done.2.rest_3_) | copy-start | bytes 393220
  22.2 15.6 %copy-start.4 = (bf16[2,2,128,128]{3,2,1,0:T(8,128)(2,1)}, bf16[2,2,128,128]{3,2,1,0:T(8,128)(2,1)S(1)}, u32[]{:S(2)}) copy-start(bf16[2,2,128,128]{3,2,1,0:T(8,128)(2,1)S(1)} %collective-permute-done.3.rest_4_) | copy-start | bytes 393220
  30.0 7.8 %copy-start.5 = (bf16[2,2,128,128]{3,2,1,0:T(8,128)(2,1)}, bf16[2,2,128,128]{3,2,1,0:T(8,128)(2,1)S(1)}, u32[]{:S(2)}) copy-start(bf16[2,2,128,128]{3,2,1,0:T(8,128)(2,1)S(1)} %collective-permute-done.4.rest_5_) | copy-start | bytes 393220
  36.2 1.7 %copy-start.6 = (bf16[2,2,128,128]{3,2,1,0:T(8,128)(2,1)}, bf16[2,2,128,128]{3,2,1,0:T(8,128)(2,1)S(1)}, u32[]{:S(2)}) copy-start(bf16[2,2,128,128]{3,2,1,0:T(8,128)(2,1)S(1)} %collective-permute-done.5.rest_6_) | copy-start | bytes 393220
  37.8 0.7 copy-start.7
  38.5 1.1 %copy-start = (bf16[4,128,1280]{2,1,0:T(8,128)(2,1)}, bf16[4,128,1280]{2,1,0:T(8,128)(2,1)S(1)}, u32[]{:S(2)}) copy-start(bf16[4,128,1280]{2,1,0:T(8,128)(2,1)S(1)} %all-to-all-done.span_ref) | copy-start | bytes 3932164

commit v3 on v2

v3 whole, which is shorter than its diff:
```python
import functools
import math

import jax
import jax.numpy as jnp
from jax import lax
from jax.experimental import pallas as pl
from jax.experimental.pallas import tpu as pltpu
from jax.sharding import PartitionSpec as P

HEAD_DIM = 128
HEADS = 32
KV_HEADS = 4
CAP = 2

NEG_FILL = -1e30
EXP2_SCALE = math.log2(math.e) / math.sqrt(HEAD_DIM)
SMALL = 8 * 2**20
ANY = pl.BlockSpec(memory_space=pl.ANY)
HBM = pl.BlockSpec(memory_space=pltpu.HBM)
SMEM = pl.BlockSpec(memory_space=pltpu.SMEM)
VMEM = pl.BlockSpec(memory_space=pltpu.VMEM)


def kv_head(ctx, ctx_count):
    return ctx * KV_HEADS // ctx_count


def pack_kernel(ids_ref, len_ref, q_ref, k_ref, v_ref, keys_ref, values_ref, *rest):
    pool_count, slot_count = ids_ref.shape
    span_ref, page_refs = rest[0], rest[1 : 1 + pool_count]
    found_ref, span_sems, sems = rest[1 + pool_count :]
    ctx_count = span_ref.shape[0]
    pages_dev = keys_ref.shape[0]
    me = lax.axis_index("pool")
    width = HEADS // ctx_count * HEAD_DIM
    copies = []
    for ctx in range(ctx_count):
        head = kv_head(ctx, ctx_count) * HEAD_DIM
        for part, (source, begin, size, place) in enumerate(
            (
                (q_ref, ctx * width, width, 0),
                (k_ref, head, HEAD_DIM, width),
                (v_ref, head, HEAD_DIM, width + HEAD_DIM),
            )
        ):
            copy = pltpu.make_async_copy(
                source.at[0, :, pl.ds(begin, size)],
                span_ref.at[ctx, :, pl.ds(place, size)],
                span_sems.at[ctx, part],
            )
            copy.start()
            copies.append(copy)
    head = kv_head(lax.axis_index("cp"), ctx_count)
    columns = pl.ds(pl.multiple_of(head * HEAD_DIM, HEAD_DIM), HEAD_DIM)
    low = me * pages_dev
    for step in reversed(range(pool_count)):
        request = me ^ step
        live = len_ref[request]
        for rank in range(CAP):
            found_ref[step, rank] = 0
        count = jnp.int32(0)
        for slot in range(slot_count):
            local = ids_ref[request, slot] - low
            hit = (local >= 0) & (local < pages_dev) & (slot < live)
            found_ref[step, count] = jnp.where(hit, local, 0)
            count = jnp.minimum(count + hit.astype(jnp.int32), CAP)
        for rank in range(CAP):
            page = found_ref[step, rank]
            for which, source in enumerate((keys_ref, values_ref)):
                copy = pltpu.make_async_copy(
                    source.at[page, :, columns],
                    page_refs[step].at[which, rank],
                    sems.at[step, which, rank],
                )
                copy.start()
                copies.append(copy)
    for copy in copies:
        copy.wait()


def pack(page_ids, prefix_pages, queries, span_keys, span_values, pool_keys, pool_values):
    ctx_count = lax.axis_size("cp")
    tok_count = queries.shape[1]
    width = (HEADS // ctx_count + 2) * HEAD_DIM
    pool_count = page_ids.shape[0]
    page = pool_keys.shape[1]
    shape = jax.ShapeDtypeStruct((2, CAP, page, HEAD_DIM), jnp.bfloat16)
    span, *pages = pl.pallas_call(
        pack_kernel,
        out_shape=[jax.ShapeDtypeStruct((ctx_count, tok_count, width), jnp.bfloat16)]
        + [shape] * pool_count,
        in_specs=[SMEM, SMEM] + [HBM] * 5,
        out_specs=[VMEM] * (1 + pool_count),
        scratch_shapes=[
            pltpu.SMEM((pool_count, CAP + 1), jnp.int32),
            pltpu.SemaphoreType.DMA((ctx_count, 3)),
            pltpu.SemaphoreType.DMA((pool_count, 2, CAP)),
        ],
        compiler_params=pltpu.CompilerParams(vmem_limit_bytes=59 * 2**20),
        name="pack",
    )(page_ids, prefix_pages, queries, span_keys, span_values, pool_keys, pool_values)
    return span, pages


def count_pages(ids_ref, len_ref, count_ref, pages_dev):
    me = lax.axis_index("pool")
    for owner in range(ids_ref.shape[0]):
        count_ref[owner] = 0
    live = len_ref[me]
    for slot in range(ids_ref.shape[1]):
        owner = ids_ref[me, slot] // pages_dev
        count_ref[owner] = count_ref[owner] + (slot < live).astype(jnp.int32)


def place_pages(steps, count_ref, span_ref, page_refs, k_ref, v_ref):
    me = lax.axis_index("pool")
    page = page_refs[0].shape[2]
    begin = span_ref.shape[2] - 2 * HEAD_DIM
    first_key = jnp.broadcast_to(span_ref[0, 0:1, begin : begin + HEAD_DIM], (page, HEAD_DIM))
    zeros = jnp.zeros((page, HEAD_DIM), jnp.bfloat16)
    ones = jnp.ones((page, HEAD_DIM), jnp.bfloat16)
    row = 0
    for step, page_ref in zip(steps, page_refs):
        for rank in range(CAP):
            rows = pl.ds(row, page)
            used = count_ref[me ^ step] > rank
            k_ref[rows, :] = jnp.where(used, page_ref[0, rank], first_key)
            v_ref[rows, :HEAD_DIM] = jnp.where(used, page_ref[1, rank], zeros)
            v_ref[rows, HEAD_DIM:] = jnp.where(used, ones, zeros)
            row += page


def stack_heads(span_ref, ctx, first, count):
    return jnp.concatenate(
        [
            span_ref[ctx, :, h * HEAD_DIM : (h + 1) * HEAD_DIM]
            for h in range(first, first + count)
        ],
        axis=0,
    )


def score(query, keys):
    return lax.dot_general(
        query, keys, (((1,), (1,)), ((), ())), preferred_element_type=jnp.float32
    )


def weigh(part, peak, values):
    weights = jnp.exp2((part - peak) * EXP2_SCALE).astype(jnp.bfloat16)
    return jnp.dot(weights, values, preferred_element_type=jnp.float32)


def near_kernel(chunk, pages_dev, steps, ids_ref, len_ref, span_ref, *rest):
    page_refs = rest[: len(steps)]
    sum_ref, peak_ref, k_ref, v_ref, count_ref = rest[len(steps) :]
    ctx_count, tok_count, width = span_ref.shape
    heads = width // HEAD_DIM - 2
    count_pages(ids_ref, len_ref, count_ref, pages_dev)
    place_pages(steps, count_ref, span_ref, page_refs, k_ref, v_ref)
    prefix = k_ref.shape[0] - ctx_count * tok_count
    for ctx in range(ctx_count):
        rows = pl.ds(prefix + ctx * tok_count, tok_count)
        k_ref[rows, :] = span_ref[ctx, :, heads * HEAD_DIM : (heads + 1) * HEAD_DIM]
        v_ref[rows, :HEAD_DIM] = span_ref[ctx, :, (heads + 1) * HEAD_DIM :]
        v_ref[rows, HEAD_DIM:] = jnp.ones((tok_count, HEAD_DIM), jnp.bfloat16)

    row_pos = lax.broadcasted_iota(jnp.int32, (tok_count, tok_count), 0)
    col_pos = lax.broadcasted_iota(jnp.int32, (tok_count, tok_count), 1)
    group = 256 // tok_count
    causal = jnp.concatenate([col_pos <= row_pos] * group, axis=0)
    for ctx in range(ctx_count):
        parts = [(begin, chunk, False) for begin in range(0, prefix, chunk)]
        if ctx:
            parts.append((prefix, ctx * tok_count, False))
        parts.append((prefix + ctx * tok_count, tok_count, True))
        for first in range(0, heads, group):
            rows = pl.ds(first * tok_count, group * tok_count)
            query = stack_heads(span_ref, ctx, first, group)
            scores = []
            for begin, size, diagonal in parts:
                part = score(query, k_ref[begin : begin + size, :])
                scores.append(jnp.where(causal, part, NEG_FILL) if diagonal else part)
            peak = functools.reduce(
                jnp.maximum, [jnp.max(part, axis=1, keepdims=True) for part in scores]
            )
            total = None
            for (begin, size, _), part in zip(parts, scores):
                term = weigh(part, peak, v_ref[begin : begin + size, :])
                total = term if total is None else total + term
            sum_ref[ctx, rows, :] = total
            peak_ref[ctx, rows, :] = jnp.broadcast_to(peak, (group * tok_count, HEAD_DIM))


def attend_near(page_ids, prefix_pages, span, pages, steps, pages_dev):
    ctx_count, tok_count, width = span.shape
    pool_count = page_ids.shape[0]
    page = pages[0].shape[2]
    keys = len(steps) * CAP * page + ctx_count * tok_count
    rows = (width // HEAD_DIM - 2) * tok_count
    return pl.pallas_call(
        functools.partial(near_kernel, 512, pages_dev, steps),
        out_shape=[
            jax.ShapeDtypeStruct((ctx_count, rows, 2 * HEAD_DIM), jnp.float32),
            jax.ShapeDtypeStruct((ctx_count, rows, HEAD_DIM), jnp.float32),
        ],
        in_specs=[SMEM, SMEM, VMEM] + [VMEM] * len(steps),
        out_specs=[VMEM, VMEM],
        scratch_shapes=[
            pltpu.VMEM((keys, HEAD_DIM), jnp.bfloat16),
            pltpu.VMEM((keys, 2 * HEAD_DIM), jnp.bfloat16),
            pltpu.SMEM((pool_count,), jnp.int32),
        ],
        compiler_params=pltpu.CompilerParams(vmem_limit_bytes=40 * 2**20),
        name="attend_near",
    )(page_ids, prefix_pages, span, *pages)


def far_kernel(chunk, pages_dev, steps, ctx_step, ids_ref, len_ref, span_ref, sum_ref, peak_ref, *rest):
    page_refs = rest[: len(steps)]
    out_ref, k_ref, v_ref, count_ref = rest[len(steps) :]
    tok_count = span_ref.shape[1]
    ctx = lax.axis_index("cp") ^ ctx_step
    count_pages(ids_ref, len_ref, count_ref, pages_dev)
    place_pages(steps, count_ref, span_ref, page_refs, k_ref, v_ref)
    keys = k_ref.shape[0]
    begins = range(0, keys, chunk)
    group = 256 // tok_count
    for first in range(0, span_ref.shape[2] // HEAD_DIM - 2, group):
        rows = pl.ds(first * tok_count, group * tok_count)
        query = stack_heads(span_ref, ctx, first, group)
        scores = [score(query, k_ref[begin : begin + chunk, :]) for begin in begins]
        near_peak = peak_ref[ctx, rows, :1]
        peak = functools.reduce(
            jnp.maximum, [jnp.max(part, axis=1, keepdims=True) for part in scores], near_peak
        )
        total = sum_ref[ctx, rows, :] * jnp.exp2((near_peak - peak) * EXP2_SCALE)
        for begin, part in zip(begins, scores):
            total = total + weigh(part, peak, v_ref[begin : begin + chunk, :])
        mixed = (total[:, :HEAD_DIM] / total[:, HEAD_DIM:]).astype(out_ref.dtype)
        for h in range(group):
            place = (first + h) * HEAD_DIM
            out_ref[:, place : place + HEAD_DIM] = mixed[h * tok_count : (h + 1) * tok_count]


def attend_far(page_ids, prefix_pages, span, state, pages, steps, pages_dev, ctx_step):
    ctx_count, tok_count, width = span.shape
    pool_count = page_ids.shape[0]
    page = pages[0].shape[2]
    keys = len(steps) * CAP * page
    kind = jnp.bfloat16 if ctx_step else jnp.float32
    return pl.pallas_call(
        functools.partial(far_kernel, 512, pages_dev, steps, ctx_step),
        out_shape=jax.ShapeDtypeStruct((tok_count, width - 2 * HEAD_DIM), kind),
        in_specs=[SMEM, SMEM, VMEM, VMEM, VMEM] + [VMEM] * len(steps),
        out_specs=VMEM,
        scratch_shapes=[
            pltpu.VMEM((keys, HEAD_DIM), jnp.bfloat16),
            pltpu.VMEM((keys, 2 * HEAD_DIM), jnp.bfloat16),
            pltpu.SMEM((pool_count,), jnp.int32),
        ],
        compiler_params=pltpu.CompilerParams(vmem_limit_bytes=40 * 2**20),
        name="attend_far",
    )(page_ids, prefix_pages, span, *state, *pages)


def join_kernel(*refs):
    count = len(refs) - 3
    part_refs, (out_ref, wide_ref, sems) = refs[:count], refs[count:]
    me = lax.axis_index("cp")
    width = part_refs[0].shape[1]
    copies = []
    for step, part_ref in enumerate(part_refs):
        source = part_ref
        if step:
            source = wide_ref.at[step - 1]
            source[...] = part_ref[...].astype(jnp.float32)
        place = pl.ds(pl.multiple_of((me ^ step) * width, width), width)
        copy = pltpu.make_async_copy(source, out_ref.at[0, :, place], sems.at[step])
        copy.start()
        copies.append(copy)
    for copy in copies:
        copy.wait()


def join(parts):
    tok_count, width = parts[0].shape
    count = len(parts)
    return pl.pallas_call(
        join_kernel,
        out_shape=jax.ShapeDtypeStruct((1, tok_count, count * width), jnp.float32),
        in_specs=[VMEM] * count,
        out_specs=ANY,
        scratch_shapes=[
            pltpu.VMEM((count - 1, tok_count, width), jnp.float32),
            pltpu.SemaphoreType.DMA((count,)),
        ],
        compiler_params=pltpu.CompilerParams(vmem_limit_bytes=SMALL),
        name="join",
    )(*parts)


def swap(x, axis, step):
    return lax.ppermute(x, axis, [(i, i ^ step) for i in range(lax.axis_size(axis))])


def body(queries, span_keys, span_values, pool_keys, pool_values, page_ids, prefix_pages):
    pool_count = lax.axis_size("pool")
    ctx_count = lax.axis_size("cp")
    pages_dev = pool_keys.shape[0]
    packed, pages = pack(
        page_ids, prefix_pages, queries, span_keys, span_values, pool_keys, pool_values
    )
    fetched = [pages[0]] + [swap(pages[step], "pool", step) for step in range(1, pool_count)]
    span = lax.all_to_all(packed, "cp", split_axis=0, concat_axis=0, tiled=True)
    near = tuple(range(pool_count // 2))
    far = tuple(range(pool_count // 2, pool_count))
    state = attend_near(page_ids, prefix_pages, span, fetched[: len(near)], near, pages_dev)
    parts = [None] * ctx_count
    for step in list(range(ctx_count - 1, -1, -1)):
        part = attend_far(
            page_ids, prefix_pages, span, state, fetched[len(near) :], far, pages_dev, step
        )
        parts[step] = swap(part, "cp", step) if step else part
    return join(parts)


def solution(mesh):
    in_specs = (
        P("pool", "cp", None),
        P("pool", "cp", None),
        P("pool", "cp", None),
        P("pool", None, None),
        P("pool", None, None),
        P(),
        P(),
    )
    out_specs = P("pool", "cp", None)
    return jax.shard_map(body, mesh=mesh, in_specs=in_specs, out_specs=out_specs, check_vma=False)
```

time: 81.1 us -> 60.1 us (0.74)
  blocking collectives: 19.5 us -> 0 us
  starting transfers between devices: 8.41 us -> 12.4 us
  waiting for transfers between devices: 22.6 us -> 19.7 us
  local copies, waits for them, and re-layouts: 1.7 us -> 0.05 us
    all_to_all x1 -> x0, blocking collectives: 19.5 us -> none  [body(): mixed = lax.all_to_all(mixed, 'cp', split_axis=0, concat_axis=0, tiled=True)]
    ppermute x7 -> x10, waiting for transfers between devices: 22.6 us -> 13.8 us  [swap(): lax.ppermute(x, axis, [(i, i ^ step) for i in range(lax.axis_size(axis))])]
    all_to_all x1, waiting for transfers between devices: 0.01 us -> 5.85 us  [body(): span = lax.all_to_all(packed, 'cp', split_axis=0, concat_axis=0, tiled=True)]
    ppermute x7 -> x10, starting transfers between devices: 4.71 us -> 8.39 us  [swap(): lax.ppermute(x, axis, [(i, i ^ step) for i in range(lax.axis_size(axis))])]
    unnamed x30 -> x20, local copies, waits for them, and re-layouts: 1.7 us -> 0.05 us
    pallas_call x4 -> x7, Pallas kernels: 28.2 us -> 27.4 us  [the longest x4 11.4 us: attend_far(): pl.pallas_call(functools.partial(far_kernel, 512, pages_dev, steps, ctx_s...]
  transfers between devices with their start and end apart: 8 -> 11, of which waited for: 6 -> 5; matrix products, arithmetic and copies ran while one was open for 0% -> 0% of each run, Pallas kernels for 0% -> 31%
where the time goes in v3:
time: 60.1 us; the launch traced here: 59.8 us
  Pallas kernels  27.4 us (46%)
  waiting for transfers between devices  19.7 us (33%)
  starting transfers between devices  12.4 us (21%)
    ppermute x10, waiting for transfers between devices, swap(): lax.ppermute(x, axis, [(i, i ^ step) for i in range(lax.axis_size(axis))])  13.8 us
    pallas_call x4, Pallas kernels, attend_far(): pl.pallas_call(functools.partial(far_kernel, 512, pages_dev, steps, ctx_s...  11.4 us
    pallas_call x1, Pallas kernels, attend_near(): pl.pallas_call(functools.partial(near_kernel, 512, pages_dev, steps), out...  9.74 us
    ppermute x10, starting transfers between devices, swap(): lax.ppermute(x, axis, [(i, i ^ step) for i in range(lax.axis_size(axis))])  8.39 us
    all_to_all x1, waiting for transfers between devices, body(): span = lax.all_to_all(packed, 'cp', split_axis=0, concat_axis=0, tiled=True)  5.85 us
    pallas_call x1, Pallas kernels, pack(): pl.pallas_call(pack_kernel, out_shape=[jax.ShapeDtypeStruct((ctx_count, t...  4.83 us
    all_to_all x1, starting transfers between devices, body(): span = lax.all_to_all(packed, 'cp', split_axis=0, concat_axis=0, tiled=True)  4 us
    pallas_call x1, Pallas kernels, join(): pl.pallas_call(join_kernel, out_shape=jax.ShapeDtypeStruct((1, tok_count,...  1.35 us
  transfers between devices with their start and end apart: 11, of which 5 were waited for; matrix products, arithmetic and copies ran while one was open for 0% of the time, Pallas kernels for 31%

profile of v3, /device:TPU:16, one launch (start us, length us, event | category | flops | bytes accessed | tf_op | source)
XLA Modules:
  0.0 59.8 jit_solution(15040501106329728371)
XLA Ops:
  0.0 4.8 %pack.1 = (bf16[4,128,1280]{2,1,0:T(8,128)(2,1)}, bf16[2,2,128,128]{3,2,1,0:T(8,128)(2,1)}, bf16[2,2,128,128]{3,2,1,0:T(8,128)(2,1)}, bf16[2,2,128,128]{3,2,1,0:...) custom-call(s32[8,16]{1,0:T(8,128)} %ids_ref.11, ...), custom_call_target="tpu_custom_call" | custom-call | tf_op jit(solution)/shard_map/pack/pallas_call | solution.py:89
  4.8 0.0 copy-start.9
  4.9 0.0 copy-start.8
  4.9 0.0 copy-start.7
  4.9 0.0 copy-start.6
  4.9 0.0 copy-start.5
  4.9 0.0 copy-start.4
  4.9 0.0 copy-start.3
  4.9 0.0 copy-start
  4.9 0.0 copy-start.1
  4.9 0.0 copy-start.2
  4.9 4.0 %all-to-all-start = ((bf16[4,128,1280]{2,1,0:T(8,128)(2,1)}), bf16[4,128,1280]{2,1,0:T(8,128)(2,1)S(1)}, u32[]{:S(2)}, u32[]{:S(2)}) async-start(bf16[4,128,1280]{2,1,0:T(8,128)(2,1)} %get-tuple-element.16), calls=%async_computation | async-start | bytes 2621440 | tf_op jit(solution)/shard_map/all_to_all | solution.py:316
  8.9 0.0 copy-done.9
  9.0 0.0 collective-permute-start
  9.0 0.0 copy-done.8
  9.0 1.3 %collective-permute-start.1 = (bf16[2,2,128,128]{3,2,1,0:T(8,128)(2,1)S(1)}, bf16[2,2,128,128]{3,2,1,0:T(8,128)(2,1)S(1)}, u32[]{:S(2)}, u32[]{:S(2)}) collective-permute-start(bf16[2,2,128,128]{3,2,1,0:T(8,128)(2,1)S(1)} %copy-done.8), channel_id=1, source_target_pairs={{0,8},{4,12},{8,0},{12,4},{16,24},{20,28},{24,16},{28,20},{1,9},{5... | collective-permute-start | bytes 393224 | tf_op jit(solution)/shard_map/ppermute | solution.py:305
  10.3 0.0 copy-done.7
  10.3 0.5 collective-permute-start.2
  10.8 0.0 copy-done.6
  10.8 0.1 collective-permute-start.3
  11.0 0.0 copy-done.5
  11.0 2.5 %collective-permute-start.4 = (bf16[2,2,128,128]{3,2,1,0:T(8,128)(2,1)S(1)}, bf16[2,2,128,128]{3,2,1,0:T(8,128)(2,1)S(1)}, u32[]{:S(2)}, u32[]{:S(2)}) collective-permute-start(bf16[2,2,128,128]{3,2,1,0:T(8,128)(2,1)S(1)} %copy-done.5), channel_id=1, source_target_pairs={{0,20},{4,16},{8,28},{12,24},{16,4},{20,0},{24,12},{28,8},{1,21},{... | collective-permute-start | bytes 393224 | tf_op jit(solution)/shard_map/ppermute | solution.py:305
  13.4 0.0 collective-permute-done.rest_1_
  13.4 0.0 copy-done.4
  13.4 0.2 collective-permute-start.5
  13.6 2.8 %collective-permute-done.1.rest_2_ = bf16[2,2,128,128]{3,2,1,0:T(8,128)(2,1)S(1)} collective-permute-done((bf16[2,2,128,128]{3,2,1,0:T(8,128)(2,1)S(1)}, bf16[2,2,128,128]{3,2,1,0:T(8,128)(2,1)S(1)}, u32[]{:S(2)}, u32[]{:S(2)}) %collective-permute-start.1) | collective-permute-done | bytes 131104 | tf_op jit(solution)/shard_map/ppermute | solution.py:305
  16.5 0.0 copy-done.3
  16.5 0.0 collective-permute-start.6
  16.5 2.8 %collective-permute-done.2.rest_3_ = bf16[2,2,128,128]{3,2,1,0:T(8,128)(2,1)S(1)} collective-permute-done((bf16[2,2,128,128]{3,2,1,0:T(8,128)(2,1)S(1)}, bf16[2,2,128,128]{3,2,1,0:T(8,128)(2,1)S(1)}, u32[]{:S(2)}, u32[]{:S(2)}) %collective-permute-start.2) | collective-permute-done | bytes 131104 | tf_op jit(solution)/shard_map/ppermute | solution.py:305
  19.3 5.8 %all-to-all-done.span_ref = bf16[4,128,1280]{2,1,0:T(8,128)(2,1)S(1)} async-done(((bf16[4,128,1280]{2,1,0:T(8,128)(2,1)}), bf16[4,128,1280]{2,1,0:T(8,128)(2,1)S(1)}, u32[]{:S(2)}, u32[]{:S(2)}) %all-to-all-start) | async-done | bytes 1310752 | tf_op jit(solution)/shard_map/all_to_all | solution.py:316
  25.1 0.0 copy-done
  25.1 0.0 copy-done.1
  25.1 9.7 %attend_near.1 = (f32[4,1024,256]{2,1,0:T(8,128)S(1)}, f32[4,1024,128]{2,1,0:T(8,128)S(1)}) custom-call(s32[8,16]{1,0:T(8,128)S(1)} %copy-done, s32[8]{0:T(128)S(1)} %copy-done.2, bf16[4,128,1280]{2,1,0:T(8,128)(2,1)S(1)} %all-to-all-done.span_ref, bf16[2,2,128,128]{3,2,1,0:T(8,128)(2,1)S(1)} %copy-done.1, ...), custom_call_target="tpu_custom_call" | custom-call | tf_op jit(solution)/shard_map/attend_near/pallas_call | solution.py:202
  34.9 0.0 collective-permute-done.3.rest_0_
  34.9 0.0 collective-permute-done.4.rest_1_
  34.9 0.0 collective-permute-done.5.rest_2_
  34.9 1.5 %collective-permute-done.6.rest_3_ = bf16[2,2,128,128]{3,2,1,0:T(8,128)(2,1)S(1)} collective-permute-done((bf16[2,2,128,128]{3,2,1,0:T(8,128)(2,1)S(1)}, bf16[2,2,128,128]{3,2,1,0:T(8,128)(2,1)S(1)}, u32[]{:S(2)}, u32[]{:S(2)}) %collective-permute-start.6) | collective-permute-done | bytes 131104 | tf_op jit(solution)/shard_map/ppermute | solution.py:305
  36.4 2.8 %attend_far.5 = bf16[128,1024]{1,0:T(8,128)(2,1)S(1)} custom-call(s32[8,16]{1,0:T(8,128)S(1)} %copy-done, s32[8]{0:T(128)S(1)} %copy-done.2, bf16[4,128,1280]{2,1,0:T(8,128)(2,1)S(1)} %all-to-all-done.span_ref, f32[4,1024,256]{2,1,0:T(8,128)S(1)} %get-tuple-element.21.sum_ref, f32[4,1024,128]{2,1,0:T(8,128)S(1)} %get-tuple-element.22.peak_ref, ...), custom_call_target="tpu_custom_call" | custom-call | tf_op jit(solution)/shard_map/attend_far/pallas_call | solution.py:253
  39.2 2.1 %collective-permute-start.7 = (bf16[128,1024]{1,0:T(8,128)(2,1)S(1)}, bf16[128,1024]{1,0:T(8,128)(2,1)S(1)}, u32[]{:S(2)}, u32[]{:S(2)}) collective-permute-start(bf16[128,1024]{1,0:T(8,128)(2,1)S(1)} %attend_far.5), channel_id=1, source_target_pairs={{0,1},{1,0},{2,3},{3,2},{4,5},{5,4},{6,7},{7,6},{8,9},{9,8},{10,11... | collective-permute-start | bytes 786440 | tf_op jit(solution)/shard_map/ppermute | solution.py:305
  41.3 3.0 %attend_far.6 = bf16[128,1024]{1,0:T(8,128)(2,1)S(1)} custom-call(s32[8,16]{1,0:T(8,128)S(1)} %copy-done, s32[8]{0:T(128)S(1)} %copy-done.2, bf16[4,128,1280]{2,1,0:T(8,128)(2,1)S(1)} %all-to-all-done.span_ref, f32[4,1024,256]{2,1,0:T(8,128)S(1)} %get-tuple-element.21.sum_ref, f32[4,1024,128]{2,1,0:T(8,128)S(1)} %get-tuple-element.22.peak_ref, ...), custom_call_target="tpu_custom_call" | custom-call | tf_op jit(solution)/shard_map/attend_far/pallas_call | solution.py:253
  44.4 1.5 %collective-permute-start.8 = (bf16[128,1024]{1,0:T(8,128)(2,1)S(1)}, bf16[128,1024]{1,0:T(8,128)(2,1)S(1)}, u32[]{:S(2)}, u32[]{:S(2)}) collective-permute-start(bf16[128,1024]{1,0:T(8,128)(2,1)S(1)} %attend_far.6), channel_id=1, source_target_pairs={{0,2},{1,3},{2,0},{3,1},{4,6},{5,7},{6,4},{7,5},{8,10},{9,11},{10,... | collective-permute-start | bytes 786440 | tf_op jit(solution)/shard_map/ppermute | solution.py:305
  45.9 2.8 %attend_far.7 = bf16[128,1024]{1,0:T(8,128)(2,1)S(1)} custom-call(s32[8,16]{1,0:T(8,128)S(1)} %copy-done, s32[8]{0:T(128)S(1)} %copy-done.2, bf16[4,128,1280]{2,1,0:T(8,128)(2,1)S(1)} %all-to-all-done.span_ref, f32[4,1024,256]{2,1,0:T(8,128)S(1)} %get-tuple-element.21.sum_ref, f32[4,1024,128]{2,1,0:T(8,128)S(1)} %get-tuple-element.22.peak_ref, ...), custom_call_target="tpu_custom_call" | custom-call | tf_op jit(solution)/shard_map/attend_far/pallas_call | solution.py:253
  48.7 0.1 collective-permute-start.9
  48.8 2.8 %attend_far.4.refs_0_ = f32[128,1024]{1,0:T(8,128)S(1)} custom-call(s32[8,16]{1,0:T(8,128)S(1)} %copy-done, s32[8]{0:T(128)S(1)} %copy-done.2, bf16[4,128,1280]{2,1,0:T(8,128)(2,1)S(1)} %all-to-all-done.span_ref, f32[4,1024,256]{2,1,0:T(8,128)S(1)} %get-tuple-element.21.sum_ref, f32[4,1024,128]{2,1,0:T(8,128)S(1)} %get-tuple-element.22.peak_ref, ...), custom_call_target="tpu_custom_call" | custom-call | tf_op jit(solution)/shard_map/attend_far/pallas_call | solution.py:253
  51.6 0.0 collective-permute-done.7.refs_1_
  51.6 6.7 %collective-permute-done.8.refs_2_ = bf16[128,1024]{1,0:T(8,128)(2,1)S(1)} collective-permute-done((bf16[128,1024]{1,0:T(8,128)(2,1)S(1)}, bf16[128,1024]{1,0:T(8,128)(2,1)S(1)}, u32[]{:S(2)}, u32[]{:S(2)}) %collective-permute-start.8) | collective-permute-done | bytes 262176 | tf_op jit(solution)/shard_map/ppermute | solution.py:305
  58.3 0.0 collective-permute-done.9.refs_3_
  58.3 1.4 %join.1 = f32[1,128,4096]{2,1,0:T(8,128)} custom-call(f32[128,1024]{1,0:T(8,128)S(1)} %attend_far.4.refs_0_, bf16[128,1024]{1,0:T(8,128)(2,1)S(1)} %collective-permute-done.7.refs_1_, bf16[128,1024]{1,0:T(8,128)(2,1)S(1)} %collective-permute-done.8.refs_2_, bf16[128,1024]{1,0:T(8,128)(2,1)S(1)} %collective-permute-done.9.refs_3_), custom_call_target="tpu_custom_call" | custom-call | tf_op jit(solution)/shard_map/join/pallas_call | solution.py:290
  (1 shorter events, 0.0 us)
Async XLA Ops:
  4.8 4.1 %copy-start.9 = (bf16[2,2,128,128]{3,2,1,0:T(8,128)(2,1)S(1)}, bf16[2,2,128,128]{3,2,1,0:T(8,128)(2,1)}, u32[]{:S(2)}) copy-start(bf16[2,2,128,128]{3,2,1,0:T(8,128)(2,1)} %get-tuple-element.18) | copy-start | bytes 393220
  4.9 4.1 %copy-start.8 = (bf16[2,2,128,128]{3,2,1,0:T(8,128)(2,1)S(1)}, bf16[2,2,128,128]{3,2,1,0:T(8,128)(2,1)}, u32[]{:S(2)}) copy-start(bf16[2,2,128,128]{3,2,1,0:T(8,128)(2,1)} %get-tuple-element.19) | copy-start | bytes 393220
  4.9 5.4 %copy-start.7 = (bf16[2,2,128,128]{3,2,1,0:T(8,128)(2,1)S(1)}, bf16[2,2,128,128]{3,2,1,0:T(8,128)(2,1)}, u32[]{:S(2)}) copy-start(bf16[2,2,128,128]{3,2,1,0:T(8,128)(2,1)} %get-tuple-element.20) | copy-start | bytes 393220
  4.9 6.0 %copy-start.6 = (bf16[2,2,128,128]{3,2,1,0:T(8,128)(2,1)S(1)}, bf16[2,2,128,128]{3,2,1,0:T(8,128)(2,1)}, u32[]{:S(2)}) copy-start(bf16[2,2,128,128]{3,2,1,0:T(8,128)(2,1)} %get-tuple-element.23) | copy-start | bytes 393220
  4.9 6.1 %copy-start.5 = (bf16[2,2,128,128]{3,2,1,0:T(8,128)(2,1)S(1)}, bf16[2,2,128,128]{3,2,1,0:T(8,128)(2,1)}, u32[]{:S(2)}) copy-start(bf16[2,2,128,128]{3,2,1,0:T(8,128)(2,1)} %get-tuple-element.24) | copy-start | bytes 393220
  4.9 8.5 %copy-start.4 = (bf16[2,2,128,128]{3,2,1,0:T(8,128)(2,1)S(1)}, bf16[2,2,128,128]{3,2,1,0:T(8,128)(2,1)}, u32[]{:S(2)}) copy-start(bf16[2,2,128,128]{3,2,1,0:T(8,128)(2,1)} %get-tuple-element.25) | copy-start | bytes 393220
  4.9 11.6 %copy-start.3 = (bf16[2,2,128,128]{3,2,1,0:T(8,128)(2,1)S(1)}, bf16[2,2,128,128]{3,2,1,0:T(8,128)(2,1)}, u32[]{:S(2)}) copy-start(bf16[2,2,128,128]{3,2,1,0:T(8,128)(2,1)} %get-tuple-element.26) | copy-start | bytes 393220
  4.9 20.2 %copy-start = (s32[8,16]{1,0:T(8,128)S(1)}, s32[8,16]{1,0:T(8,128)}, u32[]{:S(2)}) copy-start(s32[8,16]{1,0:T(8,128)} %ids_ref.11) | copy-start | bytes 1540
  4.9 20.2 %copy-start.1 = (bf16[2,2,128,128]{3,2,1,0:T(8,128)(2,1)S(1)}, bf16[2,2,128,128]{3,2,1,0:T(8,128)(2,1)}, u32[]{:S(2)}) copy-start(bf16[2,2,128,128]{3,2,1,0:T(8,128)(2,1)} %get-tuple-element.17.rest_0_) | copy-start | bytes 393220
  4.9 20.2 %copy-start.2 = (s32[8]{0:T(128)S(1)}, s32[8]{0:T(128)}, u32[]{:S(2)}) copy-start(s32[8]{0:T(128)} %len_ref.11) | copy-start | bytes 100
  4.9 20.2 %all-to-all-start = ((bf16[4,128,1280]{2,1,0:T(8,128)(2,1)}), bf16[4,128,1280]{2,1,0:T(8,128)(2,1)S(1)}, u32[]{:S(2)}, u32[]{:S(2)}) async-start(bf16[4,128,1280]{2,1,0:T(8,128)(2,1)} %get-tuple-element.16), calls=%async_computation | async-start | bytes 2621440 | tf_op jit(solution)/shard_map/all_to_all | solution.py:316
  9.0 4.5 %collective-permute-start = (bf16[2,2,128,128]{3,2,1,0:T(8,128)(2,1)S(1)}, bf16[2,2,128,128]{3,2,1,0:T(8,128)(2,1)S(1)}, u32[]{:S(2)}, u32[]{:S(2)}) collective-permute-start(bf16[2,2,128,128]{3,2,1,0:T(8,128)(2,1)S(1)} %copy-done.9), channel_id=1, source_target_pairs={{0,4},{4,0},{8,12},{12,8},{16,20},{20,16},{24,28},{28,24},{1,5},{5... | collective-permute-start | bytes 393224 | tf_op jit(solution)/shard_map/ppermute | solution.py:305
  9.0 7.5 %collective-permute-start.1 = (bf16[2,2,128,128]{3,2,1,0:T(8,128)(2,1)S(1)}, bf16[2,2,128,128]{3,2,1,0:T(8,128)(2,1)S(1)}, u32[]{:S(2)}, u32[]{:S(2)}) collective-permute-start(bf16[2,2,128,128]{3,2,1,0:T(8,128)(2,1)S(1)} %copy-done.8), channel_id=1, source_target_pairs={{0,8},{4,12},{8,0},{12,4},{16,24},{20,28},{24,16},{28,20},{1,9},{5... | collective-permute-start | bytes 393224 | tf_op jit(solution)/shard_map/ppermute | solution.py:305
  10.3 9.0 %collective-permute-start.2 = (bf16[2,2,128,128]{3,2,1,0:T(8,128)(2,1)S(1)}, bf16[2,2,128,128]{3,2,1,0:T(8,128)(2,1)S(1)}, u32[]{:S(2)}, u32[]{:S(2)}) collective-permute-start(bf16[2,2,128,128]{3,2,1,0:T(8,128)(2,1)S(1)} %copy-done.7), channel_id=1, source_target_pairs={{0,12},{4,8},{8,4},{12,0},{16,28},{20,24},{24,20},{28,16},{1,13},{... | collective-permute-start | bytes 393224 | tf_op jit(solution)/shard_map/ppermute | solution.py:305
  10.8 24.0 %collective-permute-start.3 = (bf16[2,2,128,128]{3,2,1,0:T(8,128)(2,1)S(1)}, bf16[2,2,128,128]{3,2,1,0:T(8,128)(2,1)S(1)}, u32[]{:S(2)}, u32[]{:S(2)}) collective-permute-start(bf16[2,2,128,128]{3,2,1,0:T(8,128)(2,1)S(1)} %copy-done.6), channel_id=1, source_target_pairs={{0,16},{4,20},{8,24},{12,28},{16,0},{20,4},{24,8},{28,12},{1,17},{... | collective-permute-start | bytes 393224 | tf_op jit(solution)/shard_map/ppermute | solution.py:305
  11.0 23.9 %collective-permute-start.4 = (bf16[2,2,128,128]{3,2,1,0:T(8,128)(2,1)S(1)}, bf16[2,2,128,128]{3,2,1,0:T(8,128)(2,1)S(1)}, u32[]{:S(2)}, u32[]{:S(2)}) collective-permute-start(bf16[2,2,128,128]{3,2,1,0:T(8,128)(2,1)S(1)} %copy-done.5), channel_id=1, source_target_pairs={{0,20},{4,16},{8,28},{12,24},{16,4},{20,0},{24,12},{28,8},{1,21},{... | collective-permute-start | bytes 393224 | tf_op jit(solution)/shard_map/ppermute | solution.py:305
  13.4 21.5 %collective-permute-start.5 = (bf16[2,2,128,128]{3,2,1,0:T(8,128)(2,1)S(1)}, bf16[2,2,128,128]{3,2,1,0:T(8,128)(2,1)S(1)}, u32[]{:S(2)}, u32[]{:S(2)}) collective-permute-start(bf16[2,2,128,128]{3,2,1,0:T(8,128)(2,1)S(1)} %copy-done.4), channel_id=1, source_target_pairs={{0,24},{4,28},{8,16},{12,20},{16,8},{20,12},{24,0},{28,4},{1,25},{... | collective-permute-start | bytes 393224 | tf_op jit(solution)/shard_map/ppermute | solution.py:305
  16.5 19.9 %collective-permute-start.6 = (bf16[2,2,128,128]{3,2,1,0:T(8,128)(2,1)S(1)}, bf16[2,2,128,128]{3,2,1,0:T(8,128)(2,1)S(1)}, u32[]{:S(2)}, u32[]{:S(2)}) collective-permute-start(bf16[2,2,128,128]{3,2,1,0:T(8,128)(2,1)S(1)} %copy-done.3), channel_id=1, source_target_pairs={{0,28},{4,24},{8,20},{12,16},{16,12},{20,8},{24,4},{28,0},{1,29},{... | collective-permute-start | bytes 393224 | tf_op jit(solution)/shard_map/ppermute | solution.py:305
  39.2 12.4 %collective-permute-start.7 = (bf16[128,1024]{1,0:T(8,128)(2,1)S(1)}, bf16[128,1024]{1,0:T(8,128)(2,1)S(1)}, u32[]{:S(2)}, u32[]{:S(2)}) collective-permute-start(bf16[128,1024]{1,0:T(8,128)(2,1)S(1)} %attend_far.5), channel_id=1, source_target_pairs={{0,1},{1,0},{2,3},{3,2},{4,5},{5,4},{6,7},{7,6},{8,9},{9,8},{10,11... | collective-permute-start | bytes 786440 | tf_op jit(solution)/shard_map/ppermute | solution.py:305
  44.4 14.0 %collective-permute-start.8 = (bf16[128,1024]{1,0:T(8,128)(2,1)S(1)}, bf16[128,1024]{1,0:T(8,128)(2,1)S(1)}, u32[]{:S(2)}, u32[]{:S(2)}) collective-permute-start(bf16[128,1024]{1,0:T(8,128)(2,1)S(1)} %attend_far.6), channel_id=1, source_target_pairs={{0,2},{1,3},{2,0},{3,1},{4,6},{5,7},{6,4},{7,5},{8,10},{9,11},{10,... | collective-permute-start | bytes 786440 | tf_op jit(solution)/shard_map/ppermute | solution.py:305
  48.7 9.6 %collective-permute-start.9 = (bf16[128,1024]{1,0:T(8,128)(2,1)S(1)}, bf16[128,1024]{1,0:T(8,128)(2,1)S(1)}, u32[]{:S(2)}, u32[]{:S(2)}) collective-permute-start(bf16[128,1024]{1,0:T(8,128)(2,1)S(1)} %attend_far.7), channel_id=1, source_target_pairs={{0,3},{1,2},{2,1},{3,0},{4,7},{5,6},{6,5},{7,4},{8,11},{9,10},{10,... | collective-permute-start | bytes 786440 | tf_op jit(solution)/shard_map/ppermute | solution.py:305

commit v4 on v3

v4 whole, which is shorter than its diff:
```python
import functools
import math

import jax
import jax.numpy as jnp
from jax import lax
from jax.experimental import pallas as pl
from jax.experimental.pallas import tpu as pltpu
from jax.sharding import PartitionSpec as P

HEAD_DIM = 128
HEADS = 32
KV_HEADS = 4
CAP = 2

NEG_FILL = -1e30
EXP2_SCALE = math.log2(math.e) / math.sqrt(HEAD_DIM)
SMALL = 8 * 2**20
KERNEL_VMEM = 32 * 2**20
ROWS = 256
ANY = pl.BlockSpec(memory_space=pl.ANY)
HBM = pl.BlockSpec(memory_space=pltpu.HBM)
SMEM = pl.BlockSpec(memory_space=pltpu.SMEM)
VMEM = pl.BlockSpec(memory_space=pltpu.VMEM)


def kv_head(ctx, ctx_count):
    return ctx * KV_HEADS // ctx_count


def pack_kernel(ids_hbm, len_hbm, q_ref, k_ref, v_ref, keys_ref, values_ref, *rest):
    span_out, rest = rest[0], rest[1:]
    pool_count, slot_count = ids_hbm.shape
    page_outs, rest = rest[:pool_count], rest[pool_count:]
    used_ref, ids_ref, len_ref, found_ref, span_ref, pages_ref, list_sems, span_sems, sems, out_sems = rest
    ctx_count = span_ref.shape[0]
    pages_dev = keys_ref.shape[0]
    me = lax.axis_index("pool")
    lists = [
        pltpu.make_async_copy(ids_hbm, ids_ref, list_sems.at[0]),
        pltpu.make_async_copy(len_hbm, len_ref, list_sems.at[1]),
    ]
    for copy in lists:
        copy.start()
    width = HEADS // ctx_count * HEAD_DIM
    span_copies = []
    for ctx in range(ctx_count):
        head = kv_head(ctx, ctx_count) * HEAD_DIM
        for part, (source, begin, size, place) in enumerate(
            (
                (q_ref, ctx * width, width, 0),
                (k_ref, head, HEAD_DIM, width),
                (v_ref, head, HEAD_DIM, width + HEAD_DIM),
            )
        ):
            copy = pltpu.make_async_copy(
                source.at[0, :, pl.ds(begin, size)],
                span_ref.at[ctx, :, pl.ds(place, size)],
                span_sems.at[ctx, part],
            )
            copy.start()
            span_copies.append(copy)
    for copy in lists:
        copy.wait()
    head = kv_head(lax.axis_index("cp"), ctx_count)
    columns = pl.ds(pl.multiple_of(head * HEAD_DIM, HEAD_DIM), HEAD_DIM)
    low = me * pages_dev
    page_copies = []
    for step in reversed(range(pool_count)):
        request = me ^ step
        live = len_ref[request]
        for rank in range(CAP):
            found_ref[step, rank] = 0
        count = jnp.int32(0)
        for slot in range(slot_count):
            local = ids_ref[request, slot] - low
            hit = (local >= 0) & (local < pages_dev) & (slot < live)
            found_ref[step, count] = jnp.where(hit, local, 0)
            count = jnp.minimum(count + hit.astype(jnp.int32), CAP)
        for rank in range(CAP):
            page = found_ref[step, rank]
            for which, source in enumerate((keys_ref, values_ref)):
                copy = pltpu.make_async_copy(
                    source.at[page, :, columns],
                    pages_ref.at[step, which, rank],
                    sems.at[step, which, rank],
                )
                copy.start()
                page_copies.append(copy)
    out_copies = [pltpu.make_async_copy(span_ref, span_out, out_sems.at[pool_count])]
    for copy in span_copies:
        copy.wait()
    out_copies[0].start()
    live = len_ref[me]
    for step in range(pool_count):
        count = jnp.int32(0)
        low = (me ^ step) * pages_dev
        for slot in range(slot_count):
            local = ids_ref[me, slot] - low
            hit = (local >= 0) & (local < pages_dev) & (slot < live)
            count = count + hit.astype(jnp.int32)
        for rank in range(CAP):
            row = step * CAP + rank
            used_ref[row : row + 1, :] = jnp.full(
                (1, HEAD_DIM), jnp.where(count > rank, 1.0, 0.0), jnp.float32
            )
    for index, step in enumerate(reversed(range(pool_count))):
        for copy in page_copies[index * 2 * CAP : (index + 1) * 2 * CAP]:
            copy.wait()
        copy = pltpu.make_async_copy(pages_ref.at[step], page_outs[step], out_sems.at[step])
        copy.start()
        out_copies.append(copy)
    for copy in out_copies:
        copy.wait()


def pack(page_ids, prefix_pages, queries, span_keys, span_values, pool_keys, pool_values):
    ctx_count = lax.axis_size("cp")
    tok_count = queries.shape[1]
    width = (HEADS // ctx_count + 2) * HEAD_DIM
    pool_count = page_ids.shape[0]
    page = pool_keys.shape[1]
    span_shape = (ctx_count, tok_count, width)
    page_shape = (2, CAP, page, HEAD_DIM)
    span, *pages, used = pl.pallas_call(
        pack_kernel,
        out_shape=[jax.ShapeDtypeStruct(span_shape, jnp.bfloat16)]
        + [jax.ShapeDtypeStruct(page_shape, jnp.bfloat16)] * pool_count
        + [jax.ShapeDtypeStruct((pool_count * CAP, HEAD_DIM), jnp.float32)],
        in_specs=[HBM] * 7,
        out_specs=[HBM] * (1 + pool_count) + [VMEM],
        scratch_shapes=[
            pltpu.SMEM(page_ids.shape, jnp.int32),
            pltpu.SMEM(prefix_pages.shape, jnp.int32),
            pltpu.SMEM((pool_count, CAP + 1), jnp.int32),
            pltpu.VMEM(span_shape, jnp.bfloat16),
            pltpu.VMEM((pool_count,) + page_shape, jnp.bfloat16),
            pltpu.SemaphoreType.DMA((2,)),
            pltpu.SemaphoreType.DMA((ctx_count, 3)),
            pltpu.SemaphoreType.DMA((pool_count, 2, CAP)),
            pltpu.SemaphoreType.DMA((pool_count + 1,)),
        ],
        compiler_params=pltpu.CompilerParams(vmem_limit_bytes=59 * 2**20),
        name="pack",
    )(page_ids, prefix_pages, queries, span_keys, span_values, pool_keys, pool_values)
    return span, pages, used


def place_pages(steps, used_ref, page_refs, k_ref, v_ref):
    page = page_refs[0].shape[2]
    ones = jnp.ones((page, HEAD_DIM), jnp.bfloat16)
    biases = []
    row = 0
    for step, page_ref in zip(steps, page_refs):
        for rank in range(CAP):
            rows = pl.ds(row, page)
            used = used_ref[step * CAP + rank : step * CAP + rank + 1, :]
            kept = jnp.broadcast_to(used, (page, HEAD_DIM)).astype(jnp.bfloat16)
            k_ref[rows, :] = page_ref[0, rank]
            v_ref[rows, :HEAD_DIM] = page_ref[1, rank] * kept
            v_ref[rows, HEAD_DIM:] = ones * kept
            biases.append((1.0 - used) * NEG_FILL)
            row += page
    return jnp.concatenate(biases, axis=1)


def stack_heads(span_ref, ctx, first, count):
    return jnp.concatenate(
        [
            span_ref[ctx, :, h * HEAD_DIM : (h + 1) * HEAD_DIM]
            for h in range(first, first + count)
        ],
        axis=0,
    )


def score(query, keys):
    return lax.dot_general(
        query, keys, (((1,), (1,)), ((), ())), preferred_element_type=jnp.float32
    )


def weigh(part, peak, values):
    weights = jnp.exp2((part - peak) * EXP2_SCALE).astype(jnp.bfloat16)
    return jnp.dot(weights, values, preferred_element_type=jnp.float32)


def near_kernel(steps, used_ref, span_ref, *rest):
    page_refs = rest[: len(steps)]
    sum_ref, peak_ref, k_ref, v_ref = rest[len(steps) :]
    ctx_count, tok_count, width = span_ref.shape
    heads = width // HEAD_DIM - 2
    bias = place_pages(steps, used_ref, page_refs, k_ref, v_ref)
    prefix = k_ref.shape[0] - ctx_count * tok_count
    for ctx in range(ctx_count):
        rows = pl.ds(prefix + ctx * tok_count, tok_count)
        k_ref[rows, :] = span_ref[ctx, :, heads * HEAD_DIM : (heads + 1) * HEAD_DIM]
        v_ref[rows, :HEAD_DIM] = span_ref[ctx, :, (heads + 1) * HEAD_DIM :]
        v_ref[rows, HEAD_DIM:] = jnp.ones((tok_count, HEAD_DIM), jnp.bfloat16)

    row_pos = lax.broadcasted_iota(jnp.int32, (tok_count, tok_count), 0)
    col_pos = lax.broadcasted_iota(jnp.int32, (tok_count, tok_count), 1)
    group = ROWS // tok_count
    causal = jnp.concatenate([col_pos <= row_pos] * group, axis=0)
    for ctx in range(ctx_count):
        begin = prefix + ctx * tok_count
        end = begin + tok_count
        for first in range(0, heads, group):
            rows = pl.ds(first * tok_count, group * tok_count)
            part = score(stack_heads(span_ref, ctx, first, group), k_ref[:end, :])
            pieces = [part[:, :prefix] + bias]
            if ctx:
                pieces.append(part[:, prefix:begin])
            pieces.append(jnp.where(causal, part[:, begin:], NEG_FILL))
            part = jnp.concatenate(pieces, axis=1)
            peak = jnp.max(part, axis=1, keepdims=True)
            sum_ref[ctx, rows, :] = weigh(part, peak, v_ref[:end, :])
            peak_ref[ctx, rows, :] = jnp.broadcast_to(peak, (group * tok_count, HEAD_DIM))


def attend_near(used, span, pages, steps):
    ctx_count, tok_count, width = span.shape
    page = pages[0].shape[2]
    keys = len(steps) * CAP * page + ctx_count * tok_count
    rows = (width // HEAD_DIM - 2) * tok_count
    return pl.pallas_call(
        functools.partial(near_kernel, steps),
        out_shape=[
            jax.ShapeDtypeStruct((ctx_count, rows, 2 * HEAD_DIM), jnp.float32),
            jax.ShapeDtypeStruct((ctx_count, rows, HEAD_DIM), jnp.float32),
        ],
        in_specs=[VMEM] * (2 + len(steps)),
        out_specs=[VMEM, VMEM],
        scratch_shapes=[
            pltpu.VMEM((keys, HEAD_DIM), jnp.bfloat16),
            pltpu.VMEM((keys, 2 * HEAD_DIM), jnp.bfloat16),
        ],
        compiler_params=pltpu.CompilerParams(vmem_limit_bytes=KERNEL_VMEM),
        name="attend_near",
    )(used, span, *pages)


def far_kernel(steps, ctx_step, used_ref, span_ref, sum_ref, peak_ref, *rest):
    page_refs = rest[: len(steps)]
    out_ref, k_ref, v_ref = rest[len(steps) :]
    tok_count = span_ref.shape[1]
    ctx = lax.axis_index("cp") ^ ctx_step
    bias = place_pages(steps, used_ref, page_refs, k_ref, v_ref)
    group = ROWS // tok_count
    for first in range(0, span_ref.shape[2] // HEAD_DIM - 2, group):
        rows = pl.ds(first * tok_count, group * tok_count)
        part = score(stack_heads(span_ref, ctx, first, group), k_ref[...]) + bias
        near_peak = peak_ref[ctx, rows, :1]
        peak = jnp.maximum(jnp.max(part, axis=1, keepdims=True), near_peak)
        total = weigh(part, peak, v_ref[...])
        total = total + sum_ref[ctx, rows, :] * jnp.exp2((near_peak - peak) * EXP2_SCALE)
        mixed = (total[:, :HEAD_DIM] / total[:, HEAD_DIM:]).astype(out_ref.dtype)
        for h in range(group):
            place = (first + h) * HEAD_DIM
            out_ref[:, place : place + HEAD_DIM] = mixed[h * tok_count : (h + 1) * tok_count]


def attend_far(used, span, state, pages, steps, ctx_step):
    ctx_count, tok_count, width = span.shape
    keys = len(steps) * CAP * pages[0].shape[2]
    kind = jnp.bfloat16 if ctx_step else jnp.float32
    return pl.pallas_call(
        functools.partial(far_kernel, steps, ctx_step),
        out_shape=jax.ShapeDtypeStruct((tok_count, width - 2 * HEAD_DIM), kind),
        in_specs=[VMEM] * (4 + len(steps)),
        out_specs=VMEM,
        scratch_shapes=[
            pltpu.VMEM((keys, HEAD_DIM), jnp.bfloat16),
            pltpu.VMEM((keys, 2 * HEAD_DIM), jnp.bfloat16),
        ],
        compiler_params=pltpu.CompilerParams(vmem_limit_bytes=KERNEL_VMEM),
        name="attend_far",
    )(used, span, *state, *pages)


def join_kernel(*refs):
    count = len(refs) - 3
    part_refs, (out_ref, wide_ref, sems) = refs[:count], refs[count:]
    me = lax.axis_index("cp")
    width = part_refs[0].shape[1]
    copies = []
    for step, part_ref in enumerate(part_refs):
        source = part_ref
        if step:
            source = wide_ref.at[step - 1]
            source[...] = part_ref[...].astype(jnp.float32)
        place = pl.ds(pl.multiple_of((me ^ step) * width, width), width)
        copy = pltpu.make_async_copy(source, out_ref.at[0, :, place], sems.at[step])
        copy.start()
        copies.append(copy)
    for copy in copies:
        copy.wait()


def join(parts):
    tok_count, width = parts[0].shape
    count = len(parts)
    return pl.pallas_call(
        join_kernel,
        out_shape=jax.ShapeDtypeStruct((1, tok_count, count * width), jnp.float32),
        in_specs=[VMEM] * count,
        out_specs=ANY,
        scratch_shapes=[
            pltpu.VMEM((count - 1, tok_count, width), jnp.float32),
            pltpu.SemaphoreType.DMA((count,)),
        ],
        compiler_params=pltpu.CompilerParams(vmem_limit_bytes=SMALL),
        name="join",
    )(*parts)


def swap(x, axis, step):
    return lax.ppermute(x, axis, [(i, i ^ step) for i in range(lax.axis_size(axis))])


def body(queries, span_keys, span_values, pool_keys, pool_values, page_ids, prefix_pages):
    pool_count = lax.axis_size("pool")
    ctx_count = lax.axis_size("cp")
    packed, pages, used = pack(
        page_ids, prefix_pages, queries, span_keys, span_values, pool_keys, pool_values
    )
    span = lax.all_to_all(packed, "cp", split_axis=0, concat_axis=0, tiled=True)
    fetched = [swap(part, "pool", step) if step else part for step, part in enumerate(pages)]
    near = tuple(range(pool_count // 2))
    far = tuple(range(pool_count // 2, pool_count))
    state = attend_near(used, span, fetched[: len(near)], near)
    parts = [None] * ctx_count
    for step in reversed(range(ctx_count)):
        part = attend_far(used, span, state, fetched[len(near) :], far, step)
        parts[step] = swap(part, "cp", step) if step else part
    return join(parts)


def solution(mesh):
    in_specs = (
        P("pool", "cp", None),
        P("pool", "cp", None),
        P("pool", "cp", None),
        P("pool", None, None),
        P("pool", None, None),
        P(),
        P(),
    )
    out_specs = P("pool", "cp", None)
    return jax.shard_map(body, mesh=mesh, in_specs=in_specs, out_specs=out_specs, check_vma=False)
```

time: 60.1 us -> 58.4 us (0.972)
  Pallas kernels: 27.4 us -> 22.7 us
  waiting for transfers between devices: 19.7 us -> 22.4 us
    pallas_call x6, Pallas kernels: 26 us -> 21.3 us  [the longest x1 8.47 us: attend_near(): pl.pallas_call(functools.partial(near_kernel, steps), out_shape=[jax.Shap...]
    ppermute x10, waiting for transfers between devices: 13.8 us -> 16.8 us  [swap(): lax.ppermute(x, axis, [(i, i ^ step) for i in range(lax.axis_size(axis))])]
  transfers between devices with their start and end apart: 11 -> 11, of which waited for: 5 -> 6; matrix products, arithmetic and copies ran while one was open for 0% -> 0% of each run, Pallas kernels for 31% -> 26%
where the time goes in v4:
time: 58.4 us; the launch traced here: 58 us
  Pallas kernels  22.7 us (39%)
  waiting for transfers between devices  22.4 us (38%)
  starting transfers between devices  12.6 us (22%)
    ppermute x10, waiting for transfers between devices, swap(): lax.ppermute(x, axis, [(i, i ^ step) for i in range(lax.axis_size(axis))])  16.8 us
    ppermute x10, starting transfers between devices, swap(): lax.ppermute(x, axis, [(i, i ^ step) for i in range(lax.axis_size(axis))])  8.8 us
    pallas_call x1, Pallas kernels, attend_near(): pl.pallas_call(functools.partial(near_kernel, steps), out_shape=[jax.Shap...  8.47 us
    pallas_call x4, Pallas kernels, attend_far(): pl.pallas_call(functools.partial(far_kernel, steps, ctx_step), out_shape=...  8.41 us
    all_to_all x1, waiting for transfers between devices, body(): span = lax.all_to_all(packed, 'cp', split_axis=0, concat_axis=0, tiled=True)  5.56 us
    pallas_call x1, Pallas kernels, pack(): pl.pallas_call(pack_kernel, out_shape=[jax.ShapeDtypeStruct(span_shape, j...  4.46 us
    all_to_all x1, starting transfers between devices, body(): span = lax.all_to_all(packed, 'cp', split_axis=0, concat_axis=0, tiled=True)  3.82 us
    pallas_call x1, Pallas kernels, join(): pl.pallas_call(join_kernel, out_shape=jax.ShapeDtypeStruct((1, tok_count,...  1.35 us
  transfers between devices with their start and end apart: 11, of which 6 were waited for; matrix products, arithmetic and copies ran while one was open for 0% of the time, Pallas kernels for 26%

profile of v4, /device:TPU:16, one launch (start us, length us, event | category | flops | bytes accessed | tf_op | source)
XLA Modules:
  0.0 58.0 jit_solution(1027288788065799724)
XLA Ops:
  0.0 4.5 %pack.1 = (bf16[4,128,1280]{2,1,0:T(8,128)(2,1)}, bf16[2,2,128,128]{3,2,1,0:T(8,128)(2,1)}, bf16[2,2,128,128]{3,2,1,0:T(8,128)(2,1)}, bf16[2,2,128,128]{3,2,1,0:...) custom-call(s32[8,16]{1,0:T(8,128)} %ids_hbm.1, ...), custom_call_target="tpu_custom_call" | custom-call | tf_op jit(solution)/shard_map/pack/pallas_call | solution.py:125
  4.5 0.0 copy-start.8
  4.5 0.0 copy-start.7
  4.5 0.0 copy-start.6
  4.5 0.0 copy-start.5
  4.5 0.0 copy-start.4
  4.5 0.0 copy-start.3
  4.5 0.0 copy-start.2
  4.5 0.0 copy-start
  4.5 0.0 copy-start.1
  4.6 3.8 %all-to-all-start = ((bf16[4,128,1280]{2,1,0:T(8,128)(2,1)}), bf16[4,128,1280]{2,1,0:T(8,128)(2,1)S(1)}, u32[]{:S(2)}, u32[]{:S(2)}) async-start(bf16[4,128,1280]{2,1,0:T(8,128)(2,1)} %get-tuple-element.18), calls=%async_computation | async-start | bytes 2621440 | tf_op jit(solution)/shard_map/all_to_all | solution.py:327
  8.4 0.0 copy-done.8
  8.4 0.0 collective-permute-start
  8.4 0.0 copy-done.7
  8.4 1.6 %collective-permute-start.1 = (bf16[2,2,128,128]{3,2,1,0:T(8,128)(2,1)S(1)}, bf16[2,2,128,128]{3,2,1,0:T(8,128)(2,1)S(1)}, u32[]{:S(2)}, u32[]{:S(2)}) collective-permute-start(bf16[2,2,128,128]{3,2,1,0:T(8,128)(2,1)S(1)} %copy-done.7), channel_id=1, source_target_pairs={{0,8},{4,12},{8,0},{12,4},{16,24},{20,28},{24,16},{28,20},{1,9},{5... | collective-permute-start | bytes 393224 | tf_op jit(solution)/shard_map/ppermute | solution.py:318
  10.0 0.0 copy-done.6
  10.0 0.3 collective-permute-start.2
  10.3 0.0 copy-done.5
  10.3 0.4 collective-permute-start.3
  10.6 0.0 copy-done.4
  10.7 2.2 %collective-permute-start.4 = (bf16[2,2,128,128]{3,2,1,0:T(8,128)(2,1)S(1)}, bf16[2,2,128,128]{3,2,1,0:T(8,128)(2,1)S(1)}, u32[]{:S(2)}, u32[]{:S(2)}) collective-permute-start(bf16[2,2,128,128]{3,2,1,0:T(8,128)(2,1)S(1)} %copy-done.4), channel_id=1, source_target_pairs={{0,20},{4,16},{8,28},{12,24},{16,4},{20,0},{24,12},{28,8},{1,21},{... | collective-permute-start | bytes 393224 | tf_op jit(solution)/shard_map/ppermute | solution.py:318
  12.9 0.0 collective-permute-done.rest_1_
  12.9 0.0 copy-done.3
  12.9 0.6 %collective-permute-start.5 = (bf16[2,2,128,128]{3,2,1,0:T(8,128)(2,1)S(1)}, bf16[2,2,128,128]{3,2,1,0:T(8,128)(2,1)S(1)}, u32[]{:S(2)}, u32[]{:S(2)}) collective-permute-start(bf16[2,2,128,128]{3,2,1,0:T(8,128)(2,1)S(1)} %copy-done.3), channel_id=1, source_target_pairs={{0,24},{4,28},{8,16},{12,20},{16,8},{20,12},{24,0},{28,4},{1,25},{... | collective-permute-start | bytes 393224 | tf_op jit(solution)/shard_map/ppermute | solution.py:318
  13.5 3.0 %collective-permute-done.1.rest_2_ = bf16[2,2,128,128]{3,2,1,0:T(8,128)(2,1)S(1)} collective-permute-done((bf16[2,2,128,128]{3,2,1,0:T(8,128)(2,1)S(1)}, bf16[2,2,128,128]{3,2,1,0:T(8,128)(2,1)S(1)}, u32[]{:S(2)}, u32[]{:S(2)}) %collective-permute-start.1) | collective-permute-done | bytes 131104 | tf_op jit(solution)/shard_map/ppermute | solution.py:318
  16.4 0.0 copy-done.2
  16.4 0.0 collective-permute-start.6
  16.4 2.8 %collective-permute-done.2.rest_3_ = bf16[2,2,128,128]{3,2,1,0:T(8,128)(2,1)S(1)} collective-permute-done((bf16[2,2,128,128]{3,2,1,0:T(8,128)(2,1)S(1)}, bf16[2,2,128,128]{3,2,1,0:T(8,128)(2,1)S(1)}, u32[]{:S(2)}, u32[]{:S(2)}) %collective-permute-start.2) | collective-permute-done | bytes 131104 | tf_op jit(solution)/shard_map/ppermute | solution.py:318
  19.2 5.6 %all-to-all-done.span_ref = bf16[4,128,1280]{2,1,0:T(8,128)(2,1)S(1)} async-done(((bf16[4,128,1280]{2,1,0:T(8,128)(2,1)}), bf16[4,128,1280]{2,1,0:T(8,128)(2,1)S(1)}, u32[]{:S(2)}, u32[]{:S(2)}) %all-to-all-start) | async-done | bytes 1310752 | tf_op jit(solution)/shard_map/all_to_all | solution.py:327
  24.8 0.0 copy-done
  24.8 0.0 copy-done.1
  24.8 8.5 %attend_near.1 = (f32[4,1024,256]{2,1,0:T(8,128)S(1)}, f32[4,1024,128]{2,1,0:T(8,128)S(1)}) custom-call(f32[16,128]{1,0:T(8,128)S(1)} %copy-done, bf16[4,128,1280]{2,1,0:T(8,128)(2,1)S(1)} %all-to-all-done.span_ref, bf16[2,2,128,128]{3,2,1,0:T(8,128)(2,1)S(1)} %copy-done.1, bf16[2,2,128,128]{3,2,1,0:T(8,128)(2,1)S(1)} %collective-permute-done.rest_1_, ...), custom_call_target="tpu_custom_call" | custom-call | tf_op jit(solution)/shard_map/attend_near/pallas_call | solution.py:226
  33.3 0.0 collective-permute-done.3.rest_0_
  33.3 0.0 collective-permute-done.4.rest_1_
  33.3 1.2 %collective-permute-done.5.rest_2_ = bf16[2,2,128,128]{3,2,1,0:T(8,128)(2,1)S(1)} collective-permute-done((bf16[2,2,128,128]{3,2,1,0:T(8,128)(2,1)S(1)}, bf16[2,2,128,128]{3,2,1,0:T(8,128)(2,1)S(1)}, u32[]{:S(2)}, u32[]{:S(2)}) %collective-permute-start.5) | collective-permute-done | bytes 131104 | tf_op jit(solution)/shard_map/ppermute | solution.py:318
  34.5 1.7 %collective-permute-done.6.rest_3_ = bf16[2,2,128,128]{3,2,1,0:T(8,128)(2,1)S(1)} collective-permute-done((bf16[2,2,128,128]{3,2,1,0:T(8,128)(2,1)S(1)}, bf16[2,2,128,128]{3,2,1,0:T(8,128)(2,1)S(1)}, u32[]{:S(2)}, u32[]{:S(2)}) %collective-permute-start.6) | collective-permute-done | bytes 131104 | tf_op jit(solution)/shard_map/ppermute | solution.py:318
  36.1 2.1 %attend_far.5 = bf16[128,1024]{1,0:T(8,128)(2,1)S(1)} custom-call(f32[16,128]{1,0:T(8,128)S(1)} %copy-done, bf16[4,128,1280]{2,1,0:T(8,128)(2,1)S(1)} %all-to-all-done.span_ref, f32[4,1024,256]{2,1,0:T(8,128)S(1)} %get-tuple-element.23.sum_ref, f32[4,1024,128]{2,1,0:T(8,128)S(1)} %get-tuple-element.24.peak_ref, ...), custom_call_target="tpu_custom_call" | custom-call | tf_op jit(solution)/shard_map/attend_far/pallas_call | solution.py:267
  38.2 2.1 %collective-permute-start.7 = (bf16[128,1024]{1,0:T(8,128)(2,1)S(1)}, bf16[128,1024]{1,0:T(8,128)(2,1)S(1)}, u32[]{:S(2)}, u32[]{:S(2)}) collective-permute-start(bf16[128,1024]{1,0:T(8,128)(2,1)S(1)} %attend_far.5), channel_id=1, source_target_pairs={{0,1},{1,0},{2,3},{3,2},{4,5},{5,4},{6,7},{7,6},{8,9},{9,8},{10,11... | collective-permute-start | bytes 786440 | tf_op jit(solution)/shard_map/ppermute | solution.py:318
  40.3 2.2 %attend_far.6 = bf16[128,1024]{1,0:T(8,128)(2,1)S(1)} custom-call(f32[16,128]{1,0:T(8,128)S(1)} %copy-done, bf16[4,128,1280]{2,1,0:T(8,128)(2,1)S(1)} %all-to-all-done.span_ref, f32[4,1024,256]{2,1,0:T(8,128)S(1)} %get-tuple-element.23.sum_ref, f32[4,1024,128]{2,1,0:T(8,128)S(1)} %get-tuple-element.24.peak_ref, ...), custom_call_target="tpu_custom_call" | custom-call | tf_op jit(solution)/shard_map/attend_far/pallas_call | solution.py:267
  42.5 1.5 %collective-permute-start.8 = (bf16[128,1024]{1,0:T(8,128)(2,1)S(1)}, bf16[128,1024]{1,0:T(8,128)(2,1)S(1)}, u32[]{:S(2)}, u32[]{:S(2)}) collective-permute-start(bf16[128,1024]{1,0:T(8,128)(2,1)S(1)} %attend_far.6), channel_id=1, source_target_pairs={{0,2},{1,3},{2,0},{3,1},{4,6},{5,7},{6,4},{7,5},{8,10},{9,11},{10,... | collective-permute-start | bytes 786440 | tf_op jit(solution)/shard_map/ppermute | solution.py:318
  44.1 2.1 %attend_far.7 = bf16[128,1024]{1,0:T(8,128)(2,1)S(1)} custom-call(f32[16,128]{1,0:T(8,128)S(1)} %copy-done, bf16[4,128,1280]{2,1,0:T(8,128)(2,1)S(1)} %all-to-all-done.span_ref, f32[4,1024,256]{2,1,0:T(8,128)S(1)} %get-tuple-element.23.sum_ref, f32[4,1024,128]{2,1,0:T(8,128)S(1)} %get-tuple-element.24.peak_ref, ...), custom_call_target="tpu_custom_call" | custom-call | tf_op jit(solution)/shard_map/attend_far/pallas_call | solution.py:267
  46.1 0.1 collective-permute-start.9
  46.2 2.1 %attend_far.4.refs_0_ = f32[128,1024]{1,0:T(8,128)S(1)} custom-call(f32[16,128]{1,0:T(8,128)S(1)} %copy-done, bf16[4,128,1280]{2,1,0:T(8,128)(2,1)S(1)} %all-to-all-done.span_ref, f32[4,1024,256]{2,1,0:T(8,128)S(1)} %get-tuple-element.23.sum_ref, f32[4,1024,128]{2,1,0:T(8,128)S(1)} %get-tuple-element.24.peak_ref, ...), custom_call_target="tpu_custom_call" | custom-call | tf_op jit(solution)/shard_map/attend_far/pallas_call | solution.py:267
  48.3 0.0 collective-permute-done.7.refs_1_
  48.3 8.2 %collective-permute-done.8.refs_2_ = bf16[128,1024]{1,0:T(8,128)(2,1)S(1)} collective-permute-done((bf16[128,1024]{1,0:T(8,128)(2,1)S(1)}, bf16[128,1024]{1,0:T(8,128)(2,1)S(1)}, u32[]{:S(2)}, u32[]{:S(2)}) %collective-permute-start.8) | collective-permute-done | bytes 262176 | tf_op jit(solution)/shard_map/ppermute | solution.py:318
  56.5 0.0 collective-permute-done.9.refs_3_
  56.5 1.4 %join.1 = f32[1,128,4096]{2,1,0:T(8,128)} custom-call(f32[128,1024]{1,0:T(8,128)S(1)} %attend_far.4.refs_0_, bf16[128,1024]{1,0:T(8,128)(2,1)S(1)} %collective-permute-done.7.refs_1_, bf16[128,1024]{1,0:T(8,128)(2,1)S(1)} %collective-permute-done.8.refs_2_, bf16[128,1024]{1,0:T(8,128)(2,1)S(1)} %collective-permute-done.9.refs_3_), custom_call_target="tpu_custom_call" | custom-call | tf_op jit(solution)/shard_map/join/pallas_call | solution.py:303
Async XLA Ops:
  4.5 3.9 %copy-start.8 = (bf16[2,2,128,128]{3,2,1,0:T(8,128)(2,1)S(1)}, bf16[2,2,128,128]{3,2,1,0:T(8,128)(2,1)}, u32[]{:S(2)}) copy-start(bf16[2,2,128,128]{3,2,1,0:T(8,128)(2,1)} %get-tuple-element.20) | copy-start | bytes 393220
  4.5 3.9 %copy-start.7 = (bf16[2,2,128,128]{3,2,1,0:T(8,128)(2,1)S(1)}, bf16[2,2,128,128]{3,2,1,0:T(8,128)(2,1)}, u32[]{:S(2)}) copy-start(bf16[2,2,128,128]{3,2,1,0:T(8,128)(2,1)} %get-tuple-element.21) | copy-start | bytes 393220
  4.5 5.5 %copy-start.6 = (bf16[2,2,128,128]{3,2,1,0:T(8,128)(2,1)S(1)}, bf16[2,2,128,128]{3,2,1,0:T(8,128)(2,1)}, u32[]{:S(2)}) copy-start(bf16[2,2,128,128]{3,2,1,0:T(8,128)(2,1)} %get-tuple-element.22) | copy-start | bytes 393220
  4.5 5.8 %copy-start.5 = (bf16[2,2,128,128]{3,2,1,0:T(8,128)(2,1)S(1)}, bf16[2,2,128,128]{3,2,1,0:T(8,128)(2,1)}, u32[]{:S(2)}) copy-start(bf16[2,2,128,128]{3,2,1,0:T(8,128)(2,1)} %get-tuple-element.25) | copy-start | bytes 393220
  4.5 6.1 %copy-start.4 = (bf16[2,2,128,128]{3,2,1,0:T(8,128)(2,1)S(1)}, bf16[2,2,128,128]{3,2,1,0:T(8,128)(2,1)}, u32[]{:S(2)}) copy-start(bf16[2,2,128,128]{3,2,1,0:T(8,128)(2,1)} %get-tuple-element.26) | copy-start | bytes 393220
  4.5 8.3 %copy-start.3 = (bf16[2,2,128,128]{3,2,1,0:T(8,128)(2,1)S(1)}, bf16[2,2,128,128]{3,2,1,0:T(8,128)(2,1)}, u32[]{:S(2)}) copy-start(bf16[2,2,128,128]{3,2,1,0:T(8,128)(2,1)} %get-tuple-element.27) | copy-start | bytes 393220
  4.5 11.9 %copy-start.2 = (bf16[2,2,128,128]{3,2,1,0:T(8,128)(2,1)S(1)}, bf16[2,2,128,128]{3,2,1,0:T(8,128)(2,1)}, u32[]{:S(2)}) copy-start(bf16[2,2,128,128]{3,2,1,0:T(8,128)(2,1)} %get-tuple-element.28) | copy-start | bytes 393220
  4.5 20.2 %copy-start = (f32[16,128]{1,0:T(8,128)S(1)}, f32[16,128]{1,0:T(8,128)}, u32[]{:S(2)}) copy-start(f32[16,128]{1,0:T(8,128)} %get-tuple-element.17.used_ref) | copy-start | bytes 24580
  4.5 20.2 %copy-start.1 = (bf16[2,2,128,128]{3,2,1,0:T(8,128)(2,1)S(1)}, bf16[2,2,128,128]{3,2,1,0:T(8,128)(2,1)}, u32[]{:S(2)}) copy-start(bf16[2,2,128,128]{3,2,1,0:T(8,128)(2,1)} %get-tuple-element.19.rest_0_) | copy-start | bytes 393220
  4.6 20.2 %all-to-all-start = ((bf16[4,128,1280]{2,1,0:T(8,128)(2,1)}), bf16[4,128,1280]{2,1,0:T(8,128)(2,1)S(1)}, u32[]{:S(2)}, u32[]{:S(2)}) async-start(bf16[4,128,1280]{2,1,0:T(8,128)(2,1)} %get-tuple-element.18), calls=%async_computation | async-start | bytes 2621440 | tf_op jit(solution)/shard_map/all_to_all | solution.py:327
  8.4 4.5 %collective-permute-start = (bf16[2,2,128,128]{3,2,1,0:T(8,128)(2,1)S(1)}, bf16[2,2,128,128]{3,2,1,0:T(8,128)(2,1)S(1)}, u32[]{:S(2)}, u32[]{:S(2)}) collective-permute-start(bf16[2,2,128,128]{3,2,1,0:T(8,128)(2,1)S(1)} %copy-done.8), channel_id=1, source_target_pairs={{0,4},{4,0},{8,12},{12,8},{16,20},{20,16},{24,28},{28,24},{1,5},{5... | collective-permute-start | bytes 393224 | tf_op jit(solution)/shard_map/ppermute | solution.py:318
  8.4 8.0 %collective-permute-start.1 = (bf16[2,2,128,128]{3,2,1,0:T(8,128)(2,1)S(1)}, bf16[2,2,128,128]{3,2,1,0:T(8,128)(2,1)S(1)}, u32[]{:S(2)}, u32[]{:S(2)}) collective-permute-start(bf16[2,2,128,128]{3,2,1,0:T(8,128)(2,1)S(1)} %copy-done.7), channel_id=1, source_target_pairs={{0,8},{4,12},{8,0},{12,4},{16,24},{20,28},{24,16},{28,20},{1,9},{5... | collective-permute-start | bytes 393224 | tf_op jit(solution)/shard_map/ppermute | solution.py:318
  10.0 9.2 %collective-permute-start.2 = (bf16[2,2,128,128]{3,2,1,0:T(8,128)(2,1)S(1)}, bf16[2,2,128,128]{3,2,1,0:T(8,128)(2,1)S(1)}, u32[]{:S(2)}, u32[]{:S(2)}) collective-permute-start(bf16[2,2,128,128]{3,2,1,0:T(8,128)(2,1)S(1)} %copy-done.6), channel_id=1, source_target_pairs={{0,12},{4,8},{8,4},{12,0},{16,28},{20,24},{24,20},{28,16},{1,13},{... | collective-permute-start | bytes 393224 | tf_op jit(solution)/shard_map/ppermute | solution.py:318
  10.3 23.0 %collective-permute-start.3 = (bf16[2,2,128,128]{3,2,1,0:T(8,128)(2,1)S(1)}, bf16[2,2,128,128]{3,2,1,0:T(8,128)(2,1)S(1)}, u32[]{:S(2)}, u32[]{:S(2)}) collective-permute-start(bf16[2,2,128,128]{3,2,1,0:T(8,128)(2,1)S(1)} %copy-done.5), channel_id=1, source_target_pairs={{0,16},{4,20},{8,24},{12,28},{16,0},{20,4},{24,8},{28,12},{1,17},{... | collective-permute-start | bytes 393224 | tf_op jit(solution)/shard_map/ppermute | solution.py:318
  10.7 22.6 %collective-permute-start.4 = (bf16[2,2,128,128]{3,2,1,0:T(8,128)(2,1)S(1)}, bf16[2,2,128,128]{3,2,1,0:T(8,128)(2,1)S(1)}, u32[]{:S(2)}, u32[]{:S(2)}) collective-permute-start(bf16[2,2,128,128]{3,2,1,0:T(8,128)(2,1)S(1)} %copy-done.4), channel_id=1, source_target_pairs={{0,20},{4,16},{8,28},{12,24},{16,4},{20,0},{24,12},{28,8},{1,21},{... | collective-permute-start | bytes 393224 | tf_op jit(solution)/shard_map/ppermute | solution.py:318
  12.9 21.6 %collective-permute-start.5 = (bf16[2,2,128,128]{3,2,1,0:T(8,128)(2,1)S(1)}, bf16[2,2,128,128]{3,2,1,0:T(8,128)(2,1)S(1)}, u32[]{:S(2)}, u32[]{:S(2)}) collective-permute-start(bf16[2,2,128,128]{3,2,1,0:T(8,128)(2,1)S(1)} %copy-done.3), channel_id=1, source_target_pairs={{0,24},{4,28},{8,16},{12,20},{16,8},{20,12},{24,0},{28,4},{1,25},{... | collective-permute-start | bytes 393224 | tf_op jit(solution)/shard_map/ppermute | solution.py:318
  16.4 19.7 %collective-permute-start.6 = (bf16[2,2,128,128]{3,2,1,0:T(8,128)(2,1)S(1)}, bf16[2,2,128,128]{3,2,1,0:T(8,128)(2,1)S(1)}, u32[]{:S(2)}, u32[]{:S(2)}) collective-permute-start(bf16[2,2,128,128]{3,2,1,0:T(8,128)(2,1)S(1)} %copy-done.2), channel_id=1, source_target_pairs={{0,28},{4,24},{8,20},{12,16},{16,12},{20,8},{24,4},{28,0},{1,29},{... | collective-permute-start | bytes 393224 | tf_op jit(solution)/shard_map/ppermute | solution.py:318
  38.2 10.1 %collective-permute-start.7 = (bf16[128,1024]{1,0:T(8,128)(2,1)S(1)}, bf16[128,1024]{1,0:T(8,128)(2,1)S(1)}, u32[]{:S(2)}, u32[]{:S(2)}) collective-permute-start(bf16[128,1024]{1,0:T(8,128)(2,1)S(1)} %attend_far.5), channel_id=1, source_target_pairs={{0,1},{1,0},{2,3},{3,2},{4,5},{5,4},{6,7},{7,6},{8,9},{9,8},{10,11... | collective-permute-start | bytes 786440 | tf_op jit(solution)/shard_map/ppermute | solution.py:318
  42.5 14.0 %collective-permute-start.8 = (bf16[128,1024]{1,0:T(8,128)(2,1)S(1)}, bf16[128,1024]{1,0:T(8,128)(2,1)S(1)}, u32[]{:S(2)}, u32[]{:S(2)}) collective-permute-start(bf16[128,1024]{1,0:T(8,128)(2,1)S(1)} %attend_far.6), channel_id=1, source_target_pairs={{0,2},{1,3},{2,0},{3,1},{4,6},{5,7},{6,4},{7,5},{8,10},{9,11},{10,... | collective-permute-start | bytes 786440 | tf_op jit(solution)/shard_map/ppermute | solution.py:318
  46.1 10.4 %collective-permute-start.9 = (bf16[128,1024]{1,0:T(8,128)(2,1)S(1)}, bf16[128,1024]{1,0:T(8,128)(2,1)S(1)}, u32[]{:S(2)}, u32[]{:S(2)}) collective-permute-start(bf16[128,1024]{1,0:T(8,128)(2,1)S(1)} %attend_far.7), channel_id=1, source_target_pairs={{0,3},{1,2},{2,1},{3,0},{4,7},{5,6},{6,5},{7,4},{8,11},{9,10},{10,... | collective-permute-start | bytes 786440 | tf_op jit(solution)/shard_map/ppermute | solution.py:318

commit v5 on v4

--- a/solution.py
+++ b/solution.py
@@ -17,7 +17,7 @@
 EXP2_SCALE = math.log2(math.e) / math.sqrt(HEAD_DIM)
 SMALL = 8 * 2**20
 KERNEL_VMEM = 32 * 2**20
-ROWS = 256
+ROWS = 128
 ANY = pl.BlockSpec(memory_space=pl.ANY)
 HBM = pl.BlockSpec(memory_space=pltpu.HBM)
 SMEM = pl.BlockSpec(memory_space=pltpu.SMEM)
@@ -240,35 +240,38 @@
     )(used, span, *pages)
 
 
-def far_kernel(steps, ctx_step, used_ref, span_ref, sum_ref, peak_ref, *rest):
-    page_refs = rest[: len(steps)]
-    out_ref, k_ref, v_ref = rest[len(steps) :]
+def far_kernel(steps, ctx_steps, used_ref, span_ref, sum_ref, peak_ref, *rest):
+    page_refs, rest = rest[: len(steps)], rest[len(steps) :]
+    out_refs, (k_ref, v_ref) = rest[: len(ctx_steps)], rest[len(ctx_steps) :]
     tok_count = span_ref.shape[1]
-    ctx = lax.axis_index("cp") ^ ctx_step
     bias = place_pages(steps, used_ref, page_refs, k_ref, v_ref)
     group = ROWS // tok_count
-    for first in range(0, span_ref.shape[2] // HEAD_DIM - 2, group):
-        rows = pl.ds(first * tok_count, group * tok_count)
-        part = score(stack_heads(span_ref, ctx, first, group), k_ref[...]) + bias
-        near_peak = peak_ref[ctx, rows, :1]
-        peak = jnp.maximum(jnp.max(part, axis=1, keepdims=True), near_peak)
-        total = weigh(part, peak, v_ref[...])
-        total = total + sum_ref[ctx, rows, :] * jnp.exp2((near_peak - peak) * EXP2_SCALE)
-        mixed = (total[:, :HEAD_DIM] / total[:, HEAD_DIM:]).astype(out_ref.dtype)
-        for h in range(group):
-            place = (first + h) * HEAD_DIM
-            out_ref[:, place : place + HEAD_DIM] = mixed[h * tok_count : (h + 1) * tok_count]
-
-
-def attend_far(used, span, state, pages, steps, ctx_step):
+    for ctx_step, out_ref in zip(ctx_steps, out_refs):
+        ctx = lax.axis_index("cp") ^ ctx_step
+        for first in range(0, span_ref.shape[2] // HEAD_DIM - 2, group):
+            rows = pl.ds(first * tok_count, group * tok_count)
+            part = score(stack_heads(span_ref, ctx, first, group), k_ref[...]) + bias
+            near_peak = peak_ref[ctx, rows, :1]
+            peak = jnp.maximum(jnp.max(part, axis=1, keepdims=True), near_peak)
+            total = weigh(part, peak, v_ref[...])
+            total = total + sum_ref[ctx, rows, :] * jnp.exp2((near_peak - peak) * EXP2_SCALE)
+            mixed = (total[:, :HEAD_DIM] / total[:, HEAD_DIM:]).astype(out_ref.dtype)
+            for h in range(group):
+                place = (first + h) * HEAD_DIM
+                out_ref[:, place : place + HEAD_DIM] = mixed[h * tok_count : (h + 1) * tok_count]
+
+
+def attend_far(used, span, state, pages, steps, ctx_steps):
     ctx_count, tok_count, width = span.shape
     keys = len(steps) * CAP * pages[0].shape[2]
-    kind = jnp.bfloat16 if ctx_step else jnp.float32
+    kinds = [jnp.bfloat16 if step else jnp.float32 for step in ctx_steps]
     return pl.pallas_call(
-        functools.partial(far_kernel, steps, ctx_step),
-        out_shape=jax.ShapeDtypeStruct((tok_count, width - 2 * HEAD_DIM), kind),
+        functools.partial(far_kernel, steps, ctx_steps),
+        out_shape=[
+            jax.ShapeDtypeStruct((tok_count, width - 2 * HEAD_DIM), kind) for kind in kinds
+        ],
         in_specs=[VMEM] * (4 + len(steps)),
-        out_specs=VMEM,
+        out_specs=[VMEM] * len(ctx_steps),
         scratch_shapes=[
             pltpu.VMEM((keys, HEAD_DIM), jnp.bfloat16),
             pltpu.VMEM((keys, 2 * HEAD_DIM), jnp.bfloat16),
@@ -326,13 +329,15 @@
     )
     span = lax.all_to_all(packed, "cp", split_axis=0, concat_axis=0, tiled=True)
     fetched = [swap(part, "pool", step) if step else part for step, part in enumerate(pages)]
-    near = tuple(range(pool_count // 2))
-    far = tuple(range(pool_count // 2, pool_count))
-    state = attend_near(used, span, fetched[: len(near)], near)
+    near = tuple(step for step in range(pool_count) if step % 4 < 2)
+    far = tuple(step for step in range(pool_count) if step % 4 >= 2)
+    state = attend_near(used, span, [fetched[step] for step in near], near)
     parts = [None] * ctx_count
-    for step in reversed(range(ctx_count)):
-        part = attend_far(used, span, state, fetched[len(near) :], far, step)
-        parts[step] = swap(part, "cp", step) if step else part
+    order = ((ctx_count - 1,), tuple(range(1, ctx_count - 1)), (0,))
+    for ctx_steps in order:
+        out = attend_far(used, span, state, [fetched[step] for step in far], far, ctx_steps)
+        for step, part in zip(ctx_steps, out):
+            parts[step] = swap(part, "cp", step) if step else part
     return join(parts)
 
 

time: 58.4 us -> 54.1 us (0.926)
  waiting for transfers between devices: 22.4 us -> 17.7 us
  starting transfers between devices: 12.6 us -> 14.2 us
  Pallas kernels: 22.7 us -> 21.4 us
    ppermute x10, waiting for transfers between devices: 16.8 us -> 13.9 us  [swap(): lax.ppermute(x, axis, [(i, i ^ step) for i in range(lax.axis_size(axis))])]
    all_to_all x1, waiting for transfers between devices: 5.56 us -> 3.79 us  [body(): span = lax.all_to_all(packed, 'cp', split_axis=0, concat_axis=0, tiled=True)]
    ppermute x10, starting transfers between devices: 8.8 us -> 10.4 us  [swap(): lax.ppermute(x, axis, [(i, i ^ step) for i in range(lax.axis_size(axis))])]
    pallas_call x4 -> x3, Pallas kernels: 8.41 us -> 7.43 us  [attend_far(): pl.pallas_call(functools.partial(far_kernel, steps, ctx_steps), out_shape...]
where the time goes in v5:
time: 54.1 us; the launch traced here: 53.7 us
  Pallas kernels  21.4 us (40%)
  waiting for transfers between devices  17.7 us (33%)
  starting transfers between devices  14.2 us (26%)
    ppermute x10, waiting for transfers between devices, swap(): lax.ppermute(x, axis, [(i, i ^ step) for i in range(lax.axis_size(axis))])  13.9 us
    ppermute x10, starting transfers between devices, swap(): lax.ppermute(x, axis, [(i, i ^ step) for i in range(lax.axis_size(axis))])  10.4 us
    pallas_call x1, Pallas kernels, attend_near(): pl.pallas_call(functools.partial(near_kernel, steps), out_shape=[jax.Shap...  8.33 us
    pallas_call x3, Pallas kernels, attend_far(): pl.pallas_call(functools.partial(far_kernel, steps, ctx_steps), out_shape...  7.43 us
    pallas_call x1, Pallas kernels, pack(): pl.pallas_call(pack_kernel, out_shape=[jax.ShapeDtypeStruct(span_shape, j...  4.31 us
    all_to_all x1, starting transfers between devices, body(): span = lax.all_to_all(packed, 'cp', split_axis=0, concat_axis=0, tiled=True)  3.86 us
    all_to_all x1, waiting for transfers between devices, body(): span = lax.all_to_all(packed, 'cp', split_axis=0, concat_axis=0, tiled=True)  3.79 us
    pallas_call x1, Pallas kernels, join(): pl.pallas_call(join_kernel, out_shape=jax.ShapeDtypeStruct((1, tok_count,...  1.35 us
  transfers between devices with their start and end apart: 11, of which 6 were waited for; matrix products, arithmetic and copies ran while one was open for 0% of the time, Pallas kernels for 26%

profile of v5, /device:TPU:16, one launch (start us, length us, event | category | flops | bytes accessed | tf_op | source)
XLA Modules:
  0.0 53.7 jit_solution(13105001398683166524)
XLA Ops:
  0.0 4.3 %pack.1 = (bf16[4,128,1280]{2,1,0:T(8,128)(2,1)}, bf16[2,2,128,128]{3,2,1,0:T(8,128)(2,1)}, bf16[2,2,128,128]{3,2,1,0:T(8,128)(2,1)}, bf16[2,2,128,128]{3,2,1,0:...) custom-call(s32[8,16]{1,0:T(8,128)} %ids_hbm.1, ...), custom_call_target="tpu_custom_call" | custom-call | tf_op jit(solution)/shard_map/pack/pallas_call | solution.py:125
  4.3 0.0 copy-start.8
  4.3 0.0 copy-start.7
  4.3 0.0 copy-start.6
  4.3 0.0 copy-start.5
  4.4 0.0 copy-start.4
  4.4 0.0 copy-start.3
  4.4 0.0 copy-start.2
  4.4 0.0 copy-start
  4.4 0.0 copy-start.1
  4.4 3.9 %all-to-all-start = ((bf16[4,128,1280]{2,1,0:T(8,128)(2,1)}), bf16[4,128,1280]{2,1,0:T(8,128)(2,1)S(1)}, u32[]{:S(2)}, u32[]{:S(2)}) async-start(bf16[4,128,1280]{2,1,0:T(8,128)(2,1)} %get-tuple-element.20), calls=%async_computation | async-start | bytes 2621440 | tf_op jit(solution)/shard_map/all_to_all | solution.py:330
  8.3 0.0 copy-done.8
  8.3 0.0 collective-permute-start
  8.3 0.0 copy-done.7
  8.3 0.5 collective-permute-start.1
  8.8 0.0 copy-done.6
  8.8 2.3 %collective-permute-start.2 = (bf16[2,2,128,128]{3,2,1,0:T(8,128)(2,1)S(1)}, bf16[2,2,128,128]{3,2,1,0:T(8,128)(2,1)S(1)}, u32[]{:S(2)}, u32[]{:S(2)}) collective-permute-start(bf16[2,2,128,128]{3,2,1,0:T(8,128)(2,1)S(1)} %copy-done.6), channel_id=1, source_target_pairs={{0,20},{4,16},{8,28},{12,24},{16,4},{20,0},{24,12},{28,8},{1,21},{... | collective-permute-start | bytes 393224 | tf_op jit(solution)/shard_map/ppermute | solution.py:321
  11.0 0.0 copy-done.5
  11.1 1.6 %collective-permute-start.3 = (bf16[2,2,128,128]{3,2,1,0:T(8,128)(2,1)S(1)}, bf16[2,2,128,128]{3,2,1,0:T(8,128)(2,1)S(1)}, u32[]{:S(2)}, u32[]{:S(2)}) collective-permute-start(bf16[2,2,128,128]{3,2,1,0:T(8,128)(2,1)S(1)} %copy-done.5), channel_id=1, source_target_pairs={{0,8},{4,12},{8,0},{12,4},{16,24},{20,28},{24,16},{28,20},{1,9},{5... | collective-permute-start | bytes 393224 | tf_op jit(solution)/shard_map/ppermute | solution.py:321
  12.6 0.0 copy-done.4
  12.6 0.1 collective-permute-start.4
  12.8 0.0 collective-permute-done.rest_1_
  12.8 0.0 copy-done.3
  12.8 0.5 collective-permute-start.5
  13.3 5.0 %collective-permute-done.1.rest_2_ = bf16[2,2,128,128]{3,2,1,0:T(8,128)(2,1)S(1)} collective-permute-done((bf16[2,2,128,128]{3,2,1,0:T(8,128)(2,1)S(1)}, bf16[2,2,128,128]{3,2,1,0:T(8,128)(2,1)S(1)}, u32[]{:S(2)}, u32[]{:S(2)}) %collective-permute-start.1) | collective-permute-done | bytes 131104 | tf_op jit(solution)/shard_map/ppermute | solution.py:321
  18.3 0.0 copy-done.2
  18.3 1.7 %collective-permute-start.6 = (bf16[2,2,128,128]{3,2,1,0:T(8,128)(2,1)S(1)}, bf16[2,2,128,128]{3,2,1,0:T(8,128)(2,1)S(1)}, u32[]{:S(2)}, u32[]{:S(2)}) collective-permute-start(bf16[2,2,128,128]{3,2,1,0:T(8,128)(2,1)S(1)} %copy-done.2), channel_id=1, source_target_pairs={{0,28},{4,24},{8,20},{12,16},{16,12},{20,8},{24,4},{28,0},{1,29},{... | collective-permute-start | bytes 393224 | tf_op jit(solution)/shard_map/ppermute | solution.py:321
  20.0 1.1 %collective-permute-done.2.rest_3_ = bf16[2,2,128,128]{3,2,1,0:T(8,128)(2,1)S(1)} collective-permute-done((bf16[2,2,128,128]{3,2,1,0:T(8,128)(2,1)S(1)}, bf16[2,2,128,128]{3,2,1,0:T(8,128)(2,1)S(1)}, u32[]{:S(2)}, u32[]{:S(2)}) %collective-permute-start.2) | collective-permute-done | bytes 131104 | tf_op jit(solution)/shard_map/ppermute | solution.py:321
  21.1 3.8 %all-to-all-done.span_ref = bf16[4,128,1280]{2,1,0:T(8,128)(2,1)S(1)} async-done(((bf16[4,128,1280]{2,1,0:T(8,128)(2,1)}), bf16[4,128,1280]{2,1,0:T(8,128)(2,1)S(1)}, u32[]{:S(2)}, u32[]{:S(2)}) %all-to-all-start) | async-done | bytes 1310752 | tf_op jit(solution)/shard_map/all_to_all | solution.py:330
  24.9 0.0 copy-done
  24.9 0.0 copy-done.1
  24.9 8.3 %attend_near.1 = (f32[4,1024,256]{2,1,0:T(8,128)S(1)}, f32[4,1024,128]{2,1,0:T(8,128)S(1)}) custom-call(f32[16,128]{1,0:T(8,128)S(1)} %copy-done, bf16[4,128,1280]{2,1,0:T(8,128)(2,1)S(1)} %all-to-all-done.span_ref, bf16[2,2,128,128]{3,2,1,0:T(8,128)(2,1)S(1)} %copy-done.1, bf16[2,2,128,128]{3,2,1,0:T(8,128)(2,1)S(1)} %collective-permute-done.rest_1_, ...), custom_call_target="tpu_custom_call" | custom-call | tf_op jit(solution)/shard_map/attend_near/pallas_call | solution.py:226
  33.2 0.0 collective-permute-done.3.rest_0_
  33.2 0.0 collective-permute-done.4.rest_1_
  33.2 0.0 collective-permute-done.5.rest_2_
  33.2 1.5 %collective-permute-done.6.rest_3_ = bf16[2,2,128,128]{3,2,1,0:T(8,128)(2,1)S(1)} collective-permute-done((bf16[2,2,128,128]{3,2,1,0:T(8,128)(2,1)S(1)}, bf16[2,2,128,128]{3,2,1,0:T(8,128)(2,1)S(1)}, u32[]{:S(2)}, u32[]{:S(2)}) %collective-permute-start.6) | collective-permute-done | bytes 131104 | tf_op jit(solution)/shard_map/ppermute | solution.py:321
  34.8 1.9 %attend_far.5 = bf16[128,1024]{1,0:T(8,128)(2,1)S(1)} custom-call(f32[16,128]{1,0:T(8,128)S(1)} %copy-done, bf16[4,128,1280]{2,1,0:T(8,128)(2,1)S(1)} %all-to-all-done.span_ref, f32[4,1024,256]{2,1,0:T(8,128)S(1)} %get-tuple-element.25.sum_ref, f32[4,1024,128]{2,1,0:T(8,128)S(1)} %get-tuple-element.26.peak_ref, ...), custom_call_target="tpu_custom_call" | custom-call | tf_op jit(solution)/shard_map/attend_far/pallas_call | solution.py:268
  36.7 3.0 %collective-permute-start.9 = (bf16[128,1024]{1,0:T(8,128)(2,1)S(1)}, bf16[128,1024]{1,0:T(8,128)(2,1)S(1)}, u32[]{:S(2)}, u32[]{:S(2)}) collective-permute-start(bf16[128,1024]{1,0:T(8,128)(2,1)S(1)} %attend_far.5), channel_id=1, source_target_pairs={{0,3},{1,2},{2,1},{3,0},{4,7},{5,6},{6,5},{7,4},{8,11},{9,10},{10,... | collective-permute-start | bytes 786440 | tf_op jit(solution)/shard_map/ppermute | solution.py:321
  39.7 3.6 %attend_far.4 = (bf16[128,1024]{1,0:T(8,128)(2,1)S(1)}, bf16[128,1024]{1,0:T(8,128)(2,1)S(1)}) custom-call(f32[16,128]{1,0:T(8,128)S(1)} %copy-done, bf16[4,128,1280]{2,1,0:T(8,128)(2,1)S(1)} %all-to-all-done.span_ref, f32[4,1024,256]{2,1,0:T(8,128)S(1)} %get-tuple-element.25.sum_ref, f32[4,1024,128]{2,1,0:T(8,128)S(1)} %get-tuple-element.26.peak_ref, ...), custom_call_target="tpu_custom_call" | custom-call | tf_op jit(solution)/shard_map/attend_far/pallas_call | solution.py:268
  43.3 0.6 %collective-permute-start.7 = (bf16[128,1024]{1,0:T(8,128)(2,1)S(1)}, bf16[128,1024]{1,0:T(8,128)(2,1)S(1)}, u32[]{:S(2)}, u32[]{:S(2)}) collective-permute-start(bf16[128,1024]{1,0:T(8,128)(2,1)S(1)} %get-tuple-element.31), channel_id=1, source_target_pairs={{0,1},{1,0},{2,3},{3,2},{4,5},{5,4},{6,7},{7,6},{8,9},{9,8},{10,11... | collective-permute-start | bytes 786440 | tf_op jit(solution)/shard_map/ppermute | solution.py:321
  43.9 0.1 collective-permute-start.8
  44.0 1.9 %attend_far.3.refs_0_ = f32[128,1024]{1,0:T(8,128)S(1)} custom-call(f32[16,128]{1,0:T(8,128)S(1)} %copy-done, bf16[4,128,1280]{2,1,0:T(8,128)(2,1)S(1)} %all-to-all-done.span_ref, f32[4,1024,256]{2,1,0:T(8,128)S(1)} %get-tuple-element.25.sum_ref, f32[4,1024,128]{2,1,0:T(8,128)S(1)} %get-tuple-element.26.peak_ref, ...), custom_call_target="tpu_custom_call" | custom-call | tf_op jit(solution)/shard_map/attend_far/pallas_call | solution.py:268
  45.9 0.8 %collective-permute-done.9.refs_3_ = bf16[128,1024]{1,0:T(8,128)(2,1)S(1)} collective-permute-done((bf16[128,1024]{1,0:T(8,128)(2,1)S(1)}, bf16[128,1024]{1,0:T(8,128)(2,1)S(1)}, u32[]{:S(2)}, u32[]{:S(2)}) %collective-permute-start.9) | collective-permute-done | bytes 262176 | tf_op jit(solution)/shard_map/ppermute | solution.py:321
  46.7 5.5 %collective-permute-done.7.refs_1_ = bf16[128,1024]{1,0:T(8,128)(2,1)S(1)} collective-permute-done((bf16[128,1024]{1,0:T(8,128)(2,1)S(1)}, bf16[128,1024]{1,0:T(8,128)(2,1)S(1)}, u32[]{:S(2)}, u32[]{:S(2)}) %collective-permute-start.7) | collective-permute-done | bytes 262176 | tf_op jit(solution)/shard_map/ppermute | solution.py:321
  52.2 0.0 collective-permute-done.8.refs_2_
  52.2 1.4 %join.1 = f32[1,128,4096]{2,1,0:T(8,128)} custom-call(f32[128,1024]{1,0:T(8,128)S(1)} %attend_far.3.refs_0_, bf16[128,1024]{1,0:T(8,128)(2,1)S(1)} %collective-permute-done.7.refs_1_, bf16[128,1024]{1,0:T(8,128)(2,1)S(1)} %collective-permute-done.8.refs_2_, bf16[128,1024]{1,0:T(8,128)(2,1)S(1)} %collective-permute-done.9.refs_3_), custom_call_target="tpu_custom_call" | custom-call | tf_op jit(solution)/shard_map/join/pallas_call | solution.py:306
Async XLA Ops:
  4.3 4.0 %copy-start.8 = (bf16[2,2,128,128]{3,2,1,0:T(8,128)(2,1)S(1)}, bf16[2,2,128,128]{3,2,1,0:T(8,128)(2,1)}, u32[]{:S(2)}) copy-start(bf16[2,2,128,128]{3,2,1,0:T(8,128)(2,1)} %get-tuple-element.22) | copy-start | bytes 393220
  4.3 4.0 %copy-start.7 = (bf16[2,2,128,128]{3,2,1,0:T(8,128)(2,1)S(1)}, bf16[2,2,128,128]{3,2,1,0:T(8,128)(2,1)}, u32[]{:S(2)}) copy-start(bf16[2,2,128,128]{3,2,1,0:T(8,128)(2,1)} %get-tuple-element.23) | copy-start | bytes 393220
  4.3 4.4 %copy-start.6 = (bf16[2,2,128,128]{3,2,1,0:T(8,128)(2,1)S(1)}, bf16[2,2,128,128]{3,2,1,0:T(8,128)(2,1)}, u32[]{:S(2)}) copy-start(bf16[2,2,128,128]{3,2,1,0:T(8,128)(2,1)} %get-tuple-element.24) | copy-start | bytes 393220
  4.3 6.7 %copy-start.5 = (bf16[2,2,128,128]{3,2,1,0:T(8,128)(2,1)S(1)}, bf16[2,2,128,128]{3,2,1,0:T(8,128)(2,1)}, u32[]{:S(2)}) copy-start(bf16[2,2,128,128]{3,2,1,0:T(8,128)(2,1)} %get-tuple-element.27) | copy-start | bytes 393220
  4.4 8.3 %copy-start.4 = (bf16[2,2,128,128]{3,2,1,0:T(8,128)(2,1)S(1)}, bf16[2,2,128,128]{3,2,1,0:T(8,128)(2,1)}, u32[]{:S(2)}) copy-start(bf16[2,2,128,128]{3,2,1,0:T(8,128)(2,1)} %get-tuple-element.28) | copy-start | bytes 393220
  4.4 8.4 %copy-start.3 = (bf16[2,2,128,128]{3,2,1,0:T(8,128)(2,1)S(1)}, bf16[2,2,128,128]{3,2,1,0:T(8,128)(2,1)}, u32[]{:S(2)}) copy-start(bf16[2,2,128,128]{3,2,1,0:T(8,128)(2,1)} %get-tuple-element.29) | copy-start | bytes 393220
  4.4 13.9 %copy-start.2 = (bf16[2,2,128,128]{3,2,1,0:T(8,128)(2,1)S(1)}, bf16[2,2,128,128]{3,2,1,0:T(8,128)(2,1)}, u32[]{:S(2)}) copy-start(bf16[2,2,128,128]{3,2,1,0:T(8,128)(2,1)} %get-tuple-element.30) | copy-start | bytes 393220
  4.4 20.5 %copy-start = (f32[16,128]{1,0:T(8,128)S(1)}, f32[16,128]{1,0:T(8,128)}, u32[]{:S(2)}) copy-start(f32[16,128]{1,0:T(8,128)} %get-tuple-element.19.used_ref) | copy-start | bytes 24580
  4.4 20.5 %copy-start.1 = (bf16[2,2,128,128]{3,2,1,0:T(8,128)(2,1)S(1)}, bf16[2,2,128,128]{3,2,1,0:T(8,128)(2,1)}, u32[]{:S(2)}) copy-start(bf16[2,2,128,128]{3,2,1,0:T(8,128)(2,1)} %get-tuple-element.21.rest_0_) | copy-start | bytes 393220
  4.4 20.5 %all-to-all-start = ((bf16[4,128,1280]{2,1,0:T(8,128)(2,1)}), bf16[4,128,1280]{2,1,0:T(8,128)(2,1)S(1)}, u32[]{:S(2)}, u32[]{:S(2)}) async-start(bf16[4,128,1280]{2,1,0:T(8,128)(2,1)} %get-tuple-element.20), calls=%async_computation | async-start | bytes 2621440 | tf_op jit(solution)/shard_map/all_to_all | solution.py:330
  8.3 4.5 %collective-permute-start = (bf16[2,2,128,128]{3,2,1,0:T(8,128)(2,1)S(1)}, bf16[2,2,128,128]{3,2,1,0:T(8,128)(2,1)S(1)}, u32[]{:S(2)}, u32[]{:S(2)}) collective-permute-start(bf16[2,2,128,128]{3,2,1,0:T(8,128)(2,1)S(1)} %copy-done.8), channel_id=1, source_target_pairs={{0,4},{4,0},{8,12},{12,8},{16,20},{20,16},{24,28},{28,24},{1,5},{5... | collective-permute-start | bytes 393224 | tf_op jit(solution)/shard_map/ppermute | solution.py:321
  8.3 10.0 %collective-permute-start.1 = (bf16[2,2,128,128]{3,2,1,0:T(8,128)(2,1)S(1)}, bf16[2,2,128,128]{3,2,1,0:T(8,128)(2,1)S(1)}, u32[]{:S(2)}, u32[]{:S(2)}) collective-permute-start(bf16[2,2,128,128]{3,2,1,0:T(8,128)(2,1)S(1)} %copy-done.7), channel_id=1, source_target_pairs={{0,16},{4,20},{8,24},{12,28},{16,0},{20,4},{24,8},{28,12},{1,17},{... | collective-permute-start | bytes 393224 | tf_op jit(solution)/shard_map/ppermute | solution.py:321
  8.8 12.3 %collective-permute-start.2 = (bf16[2,2,128,128]{3,2,1,0:T(8,128)(2,1)S(1)}, bf16[2,2,128,128]{3,2,1,0:T(8,128)(2,1)S(1)}, u32[]{:S(2)}, u32[]{:S(2)}) collective-permute-start(bf16[2,2,128,128]{3,2,1,0:T(8,128)(2,1)S(1)} %copy-done.6), channel_id=1, source_target_pairs={{0,20},{4,16},{8,28},{12,24},{16,4},{20,0},{24,12},{28,8},{1,21},{... | collective-permute-start | bytes 393224 | tf_op jit(solution)/shard_map/ppermute | solution.py:321
  11.1 22.1 %collective-permute-start.3 = (bf16[2,2,128,128]{3,2,1,0:T(8,128)(2,1)S(1)}, bf16[2,2,128,128]{3,2,1,0:T(8,128)(2,1)S(1)}, u32[]{:S(2)}, u32[]{:S(2)}) collective-permute-start(bf16[2,2,128,128]{3,2,1,0:T(8,128)(2,1)S(1)} %copy-done.5), channel_id=1, source_target_pairs={{0,8},{4,12},{8,0},{12,4},{16,24},{20,28},{24,16},{28,20},{1,9},{5... | collective-permute-start | bytes 393224 | tf_op jit(solution)/shard_map/ppermute | solution.py:321
  12.6 20.6 %collective-permute-start.4 = (bf16[2,2,128,128]{3,2,1,0:T(8,128)(2,1)S(1)}, bf16[2,2,128,128]{3,2,1,0:T(8,128)(2,1)S(1)}, u32[]{:S(2)}, u32[]{:S(2)}) collective-permute-start(bf16[2,2,128,128]{3,2,1,0:T(8,128)(2,1)S(1)} %copy-done.4), channel_id=1, source_target_pairs={{0,12},{4,8},{8,4},{12,0},{16,28},{20,24},{24,20},{28,16},{1,13},{... | collective-permute-start | bytes 393224 | tf_op jit(solution)/shard_map/ppermute | solution.py:321
  12.8 20.5 %collective-permute-start.5 = (bf16[2,2,128,128]{3,2,1,0:T(8,128)(2,1)S(1)}, bf16[2,2,128,128]{3,2,1,0:T(8,128)(2,1)S(1)}, u32[]{:S(2)}, u32[]{:S(2)}) collective-permute-start(bf16[2,2,128,128]{3,2,1,0:T(8,128)(2,1)S(1)} %copy-done.3), channel_id=1, source_target_pairs={{0,24},{4,28},{8,16},{12,20},{16,8},{20,12},{24,0},{28,4},{1,25},{... | collective-permute-start | bytes 393224 | tf_op jit(solution)/shard_map/ppermute | solution.py:321
  18.3 16.5 %collective-permute-start.6 = (bf16[2,2,128,128]{3,2,1,0:T(8,128)(2,1)S(1)}, bf16[2,2,128,128]{3,2,1,0:T(8,128)(2,1)S(1)}, u32[]{:S(2)}, u32[]{:S(2)}) collective-permute-start(bf16[2,2,128,128]{3,2,1,0:T(8,128)(2,1)S(1)} %copy-done.2), channel_id=1, source_target_pairs={{0,28},{4,24},{8,20},{12,16},{16,12},{20,8},{24,4},{28,0},{1,29},{... | collective-permute-start | bytes 393224 | tf_op jit(solution)/shard_map/ppermute | solution.py:321
  36.7 10.0 %collective-permute-start.9 = (bf16[128,1024]{1,0:T(8,128)(2,1)S(1)}, bf16[128,1024]{1,0:T(8,128)(2,1)S(1)}, u32[]{:S(2)}, u32[]{:S(2)}) collective-permute-start(bf16[128,1024]{1,0:T(8,128)(2,1)S(1)} %attend_far.5), channel_id=1, source_target_pairs={{0,3},{1,2},{2,1},{3,0},{4,7},{5,6},{6,5},{7,4},{8,11},{9,10},{10,... | collective-permute-start | bytes 786440 | tf_op jit(solution)/shard_map/ppermute | solution.py:321
  43.3 8.9 %collective-permute-start.7 = (bf16[128,1024]{1,0:T(8,128)(2,1)S(1)}, bf16[128,1024]{1,0:T(8,128)(2,1)S(1)}, u32[]{:S(2)}, u32[]{:S(2)}) collective-permute-start(bf16[128,1024]{1,0:T(8,128)(2,1)S(1)} %get-tuple-element.31), channel_id=1, source_target_pairs={{0,1},{1,0},{2,3},{3,2},{4,5},{5,4},{6,7},{7,6},{8,9},{9,8},{10,11... | collective-permute-start | bytes 786440 | tf_op jit(solution)/shard_map/ppermute | solution.py:321
  43.9 8.3 %collective-permute-start.8 = (bf16[128,1024]{1,0:T(8,128)(2,1)S(1)}, bf16[128,1024]{1,0:T(8,128)(2,1)S(1)}, u32[]{:S(2)}, u32[]{:S(2)}) collective-permute-start(bf16[128,1024]{1,0:T(8,128)(2,1)S(1)} %get-tuple-element.32), channel_id=1, source_target_pairs={{0,2},{1,3},{2,0},{3,1},{4,6},{5,7},{6,4},{7,5},{8,10},{9,11},{10,... | collective-permute-start | bytes 786440 | tf_op jit(solution)/shard_map/ppermute | solution.py:321

commit v6 on v5

--- a/solution.py
+++ b/solution.py
@@ -281,40 +281,37 @@
     )(used, span, *state, *pages)
 
 
-def join_kernel(*refs):
-    count = len(refs) - 3
-    part_refs, (out_ref, wide_ref, sems) = refs[:count], refs[count:]
+def join_kernel(steps, *refs):
+    part_refs, (out_ref, wide_ref, sems) = refs[: len(steps)], refs[-3:]
     me = lax.axis_index("cp")
     width = part_refs[0].shape[1]
     copies = []
-    for step, part_ref in enumerate(part_refs):
-        source = part_ref
-        if step:
-            source = wide_ref.at[step - 1]
-            source[...] = part_ref[...].astype(jnp.float32)
+    for index, (step, part_ref) in enumerate(zip(steps, part_refs)):
+        source = wide_ref.at[index]
+        source[...] = part_ref[...].astype(jnp.float32)
         place = pl.ds(pl.multiple_of((me ^ step) * width, width), width)
-        copy = pltpu.make_async_copy(source, out_ref.at[0, :, place], sems.at[step])
+        copy = pltpu.make_async_copy(source, out_ref.at[0, :, place], sems.at[index])
         copy.start()
         copies.append(copy)
     for copy in copies:
         copy.wait()
 
 
-def join(parts):
+def join(parts, steps, count, into=None):
     tok_count, width = parts[0].shape
-    count = len(parts)
     return pl.pallas_call(
-        join_kernel,
+        functools.partial(join_kernel, steps),
         out_shape=jax.ShapeDtypeStruct((1, tok_count, count * width), jnp.float32),
-        in_specs=[VMEM] * count,
-        out_specs=ANY,
+        in_specs=[VMEM] * len(steps) + ([] if into is None else [HBM]),
+        out_specs=HBM,
         scratch_shapes=[
-            pltpu.VMEM((count - 1, tok_count, width), jnp.float32),
-            pltpu.SemaphoreType.DMA((count,)),
-        ],
+            pltpu.VMEM((len(steps), tok_count, width), jnp.float32),
+            pltpu.SemaphoreType.DMA((len(steps),)),
+        ],
+        input_output_aliases={} if into is None else {len(steps): 0},
         compiler_params=pltpu.CompilerParams(vmem_limit_bytes=SMALL),
         name="join",
-    )(*parts)
+    )(*parts, *([] if into is None else [into]))
 
 
 def swap(x, axis, step):
@@ -338,7 +335,9 @@
         out = attend_far(used, span, state, [fetched[step] for step in far], far, ctx_steps)
         for step, part in zip(ctx_steps, out):
             parts[step] = swap(part, "cp", step) if step else part
-    return join(parts)
+    early, late = (0, ctx_count - 1), tuple(range(1, ctx_count - 1))
+    attended = join([parts[step] for step in early], early, ctx_count)
+    return join([parts[step] for step in late], late, ctx_count, attended)
 
 
 def solution(mesh):

time: 54.1 us -> 53.7 us (level)
  waiting for transfers between devices: 17.7 us -> 17 us
    ppermute x10, waiting for transfers between devices: 13.9 us -> 13.2 us  [swap(): lax.ppermute(x, axis, [(i, i ^ step) for i in range(lax.axis_size(axis))])]
    pallas_call x1 -> x2, Pallas kernels: 1.35 us -> 2.03 us  [join(): pl.pallas_call(functools.partial(join_kernel, steps), out_shape=jax.Shape...]
  transfers between devices with their start and end apart: 11 -> 11, of which waited for: 6 -> 6; matrix products, arithmetic and copies ran while one was open for 0% -> 0% of each run, Pallas kernels for 26% -> 27%
where the time goes in v6:
time: 53.7 us; the launch traced here: 53.3 us
  Pallas kernels  21.5 us (40%)
  waiting for transfers between devices  17 us (32%)
  starting transfers between devices  14.4 us (27%)
    ppermute x10, waiting for transfers between devices, swap(): lax.ppermute(x, axis, [(i, i ^ step) for i in range(lax.axis_size(axis))])  13.2 us
    ppermute x10, starting transfers between devices, swap(): lax.ppermute(x, axis, [(i, i ^ step) for i in range(lax.axis_size(axis))])  10.6 us
    pallas_call x1, Pallas kernels, attend_near(): pl.pallas_call(functools.partial(near_kernel, steps), out_shape=[jax.Shap...  8 us
    pallas_call x3, Pallas kernels, attend_far(): pl.pallas_call(functools.partial(far_kernel, steps, ctx_steps), out_shape...  7.15 us
    pallas_call x1, Pallas kernels, pack(): pl.pallas_call(pack_kernel, out_shape=[jax.ShapeDtypeStruct(span_shape, j...  4.31 us
    all_to_all x1, starting transfers between devices, body(): span = lax.all_to_all(packed, 'cp', split_axis=0, concat_axis=0, tiled=True)  3.86 us
    all_to_all x1, waiting for transfers between devices, body(): span = lax.all_to_all(packed, 'cp', split_axis=0, concat_axis=0, tiled=True)  3.81 us
    pallas_call x2, Pallas kernels, join(): pl.pallas_call(functools.partial(join_kernel, steps), out_shape=jax.Shape...  2.03 us
  transfers between devices with their start and end apart: 11, of which 6 were waited for; matrix products, arithmetic and copies ran while one was open for 0% of the time, Pallas kernels for 27%

profile of v6, /device:TPU:16, one launch (start us, length us, event | category | flops | bytes accessed | tf_op | source)
XLA Modules:
  0.0 53.3 jit_solution(1166645721608823913)
XLA Ops:
  0.0 4.3 %pack.1 = (bf16[4,128,1280]{2,1,0:T(8,128)(2,1)}, bf16[2,2,128,128]{3,2,1,0:T(8,128)(2,1)}, bf16[2,2,128,128]{3,2,1,0:T(8,128)(2,1)}, bf16[2,2,128,128]{3,2,1,0:...) custom-call(s32[8,16]{1,0:T(8,128)} %ids_hbm.1, ...), custom_call_target="tpu_custom_call" | custom-call | tf_op jit(solution)/shard_map/pack/pallas_call | solution.py:125
  4.3 0.0 copy-start.8
  4.3 0.0 copy-start.7
  4.3 0.0 copy-start.6
  4.3 0.0 copy-start.5
  4.4 0.0 copy-start.4
  4.4 0.0 copy-start.3
  4.4 0.0 copy-start.2
  4.4 0.0 copy-start
  4.4 0.0 copy-start.1
  4.4 3.9 %all-to-all-start = ((bf16[4,128,1280]{2,1,0:T(8,128)(2,1)}), bf16[4,128,1280]{2,1,0:T(8,128)(2,1)S(1)}, u32[]{:S(2)}, u32[]{:S(2)}) async-start(bf16[4,128,1280]{2,1,0:T(8,128)(2,1)} %get-tuple-element.20), calls=%async_computation | async-start | bytes 2621440 | tf_op jit(solution)/shard_map/all_to_all | solution.py:327
  8.3 0.0 copy-done.8
  8.3 0.0 collective-permute-start
  8.3 0.0 copy-done.7
  8.3 0.4 collective-permute-start.1
  8.7 0.0 copy-done.6
  8.7 2.4 %collective-permute-start.2 = (bf16[2,2,128,128]{3,2,1,0:T(8,128)(2,1)S(1)}, bf16[2,2,128,128]{3,2,1,0:T(8,128)(2,1)S(1)}, u32[]{:S(2)}, u32[]{:S(2)}) collective-permute-start(bf16[2,2,128,128]{3,2,1,0:T(8,128)(2,1)S(1)} %copy-done.6), channel_id=1, source_target_pairs={{0,20},{4,16},{8,28},{12,24},{16,4},{20,0},{24,12},{28,8},{1,21},{... | collective-permute-start | bytes 393224 | tf_op jit(solution)/shard_map/ppermute | solution.py:318
  11.0 0.0 copy-done.5
  11.1 1.6 %collective-permute-start.3 = (bf16[2,2,128,128]{3,2,1,0:T(8,128)(2,1)S(1)}, bf16[2,2,128,128]{3,2,1,0:T(8,128)(2,1)S(1)}, u32[]{:S(2)}, u32[]{:S(2)}) collective-permute-start(bf16[2,2,128,128]{3,2,1,0:T(8,128)(2,1)S(1)} %copy-done.5), channel_id=1, source_target_pairs={{0,8},{4,12},{8,0},{12,4},{16,24},{20,28},{24,16},{28,20},{1,9},{5... | collective-permute-start | bytes 393224 | tf_op jit(solution)/shard_map/ppermute | solution.py:318
  12.6 0.0 copy-done.4
  12.6 0.1 collective-permute-start.4
  12.8 0.0 collective-permute-done.rest_1_
  12.8 0.0 copy-done.3
  12.8 0.6 %collective-permute-start.5 = (bf16[2,2,128,128]{3,2,1,0:T(8,128)(2,1)S(1)}, bf16[2,2,128,128]{3,2,1,0:T(8,128)(2,1)S(1)}, u32[]{:S(2)}, u32[]{:S(2)}) collective-permute-start(bf16[2,2,128,128]{3,2,1,0:T(8,128)(2,1)S(1)} %copy-done.3), channel_id=1, source_target_pairs={{0,24},{4,28},{8,16},{12,20},{16,8},{20,12},{24,0},{28,4},{1,25},{... | collective-permute-start | bytes 393224 | tf_op jit(solution)/shard_map/ppermute | solution.py:318
  13.4 4.8 %collective-permute-done.1.rest_2_ = bf16[2,2,128,128]{3,2,1,0:T(8,128)(2,1)S(1)} collective-permute-done((bf16[2,2,128,128]{3,2,1,0:T(8,128)(2,1)S(1)}, bf16[2,2,128,128]{3,2,1,0:T(8,128)(2,1)S(1)}, u32[]{:S(2)}, u32[]{:S(2)}) %collective-permute-start.1) | collective-permute-done | bytes 131104 | tf_op jit(solution)/shard_map/ppermute | solution.py:318
  18.2 0.0 copy-done.2
  18.2 1.8 %collective-permute-start.6 = (bf16[2,2,128,128]{3,2,1,0:T(8,128)(2,1)S(1)}, bf16[2,2,128,128]{3,2,1,0:T(8,128)(2,1)S(1)}, u32[]{:S(2)}, u32[]{:S(2)}) collective-permute-start(bf16[2,2,128,128]{3,2,1,0:T(8,128)(2,1)S(1)} %copy-done.2), channel_id=1, source_target_pairs={{0,28},{4,24},{8,20},{12,16},{16,12},{20,8},{24,4},{28,0},{1,29},{... | collective-permute-start | bytes 393224 | tf_op jit(solution)/shard_map/ppermute | solution.py:318
  20.0 1.0 %collective-permute-done.2.rest_3_ = bf16[2,2,128,128]{3,2,1,0:T(8,128)(2,1)S(1)} collective-permute-done((bf16[2,2,128,128]{3,2,1,0:T(8,128)(2,1)S(1)}, bf16[2,2,128,128]{3,2,1,0:T(8,128)(2,1)S(1)}, u32[]{:S(2)}, u32[]{:S(2)}) %collective-permute-start.2) | collective-permute-done | bytes 131104 | tf_op jit(solution)/shard_map/ppermute | solution.py:318
  21.0 3.8 %all-to-all-done.span_ref = bf16[4,128,1280]{2,1,0:T(8,128)(2,1)S(1)} async-done(((bf16[4,128,1280]{2,1,0:T(8,128)(2,1)}), bf16[4,128,1280]{2,1,0:T(8,128)(2,1)S(1)}, u32[]{:S(2)}, u32[]{:S(2)}) %all-to-all-start) | async-done | bytes 1310752 | tf_op jit(solution)/shard_map/all_to_all | solution.py:327
  24.8 0.0 copy-done
  24.8 0.0 copy-done.1
  24.8 8.0 %attend_near.1 = (f32[4,1024,256]{2,1,0:T(8,128)S(1)}, f32[4,1024,128]{2,1,0:T(8,128)S(1)}) custom-call(f32[16,128]{1,0:T(8,128)S(1)} %copy-done, bf16[4,128,1280]{2,1,0:T(8,128)(2,1)S(1)} %all-to-all-done.span_ref, bf16[2,2,128,128]{3,2,1,0:T(8,128)(2,1)S(1)} %copy-done.1, bf16[2,2,128,128]{3,2,1,0:T(8,128)(2,1)S(1)} %collective-permute-done.rest_1_, ...), custom_call_target="tpu_custom_call" | custom-call | tf_op jit(solution)/shard_map/attend_near/pallas_call | solution.py:226
  32.8 0.0 collective-permute-done.3.rest_0_
  32.8 0.0 collective-permute-done.4.rest_1_
  32.8 0.0 collective-permute-done.5.rest_2_
  32.8 1.9 %collective-permute-done.6.rest_3_ = bf16[2,2,128,128]{3,2,1,0:T(8,128)(2,1)S(1)} collective-permute-done((bf16[2,2,128,128]{3,2,1,0:T(8,128)(2,1)S(1)}, bf16[2,2,128,128]{3,2,1,0:T(8,128)(2,1)S(1)}, u32[]{:S(2)}, u32[]{:S(2)}) %collective-permute-start.6) | collective-permute-done | bytes 131104 | tf_op jit(solution)/shard_map/ppermute | solution.py:318
  34.8 1.9 %attend_far.5 = bf16[128,1024]{1,0:T(8,128)(2,1)S(1)} custom-call(f32[16,128]{1,0:T(8,128)S(1)} %copy-done, bf16[4,128,1280]{2,1,0:T(8,128)(2,1)S(1)} %all-to-all-done.span_ref, f32[4,1024,256]{2,1,0:T(8,128)S(1)} %get-tuple-element.25.sum_ref, f32[4,1024,128]{2,1,0:T(8,128)S(1)} %get-tuple-element.26.peak_ref, ...), custom_call_target="tpu_custom_call" | custom-call | tf_op jit(solution)/shard_map/attend_far/pallas_call | solution.py:268
  36.6 3.0 %collective-permute-start.9 = (bf16[128,1024]{1,0:T(8,128)(2,1)S(1)}, bf16[128,1024]{1,0:T(8,128)(2,1)S(1)}, u32[]{:S(2)}, u32[]{:S(2)}) collective-permute-start(bf16[128,1024]{1,0:T(8,128)(2,1)S(1)} %attend_far.5), channel_id=1, source_target_pairs={{0,3},{1,2},{2,1},{3,0},{4,7},{5,6},{6,5},{7,4},{8,11},{9,10},{10,... | collective-permute-start | bytes 786440 | tf_op jit(solution)/shard_map/ppermute | solution.py:318
  39.6 3.4 %attend_far.3 = (bf16[128,1024]{1,0:T(8,128)(2,1)S(1)}, bf16[128,1024]{1,0:T(8,128)(2,1)S(1)}) custom-call(f32[16,128]{1,0:T(8,128)S(1)} %copy-done, bf16[4,128,1280]{2,1,0:T(8,128)(2,1)S(1)} %all-to-all-done.span_ref, f32[4,1024,256]{2,1,0:T(8,128)S(1)} %get-tuple-element.25.sum_ref, f32[4,1024,128]{2,1,0:T(8,128)S(1)} %get-tuple-element.26.peak_ref, ...), custom_call_target="tpu_custom_call" | custom-call | tf_op jit(solution)/shard_map/attend_far/pallas_call | solution.py:268
  43.0 0.6 %collective-permute-start.7 = (bf16[128,1024]{1,0:T(8,128)(2,1)S(1)}, bf16[128,1024]{1,0:T(8,128)(2,1)S(1)}, u32[]{:S(2)}, u32[]{:S(2)}) collective-permute-start(bf16[128,1024]{1,0:T(8,128)(2,1)S(1)} %get-tuple-element.31), channel_id=1, source_target_pairs={{0,1},{1,0},{2,3},{3,2},{4,5},{5,4},{6,7},{7,6},{8,9},{9,8},{10,11... | collective-permute-start | bytes 786440 | tf_op jit(solution)/shard_map/ppermute | solution.py:318
  43.7 0.1 collective-permute-start.8
  43.7 1.9 %attend_far.4.refs_0_ = f32[128,1024]{1,0:T(8,128)S(1)} custom-call(f32[16,128]{1,0:T(8,128)S(1)} %copy-done, bf16[4,128,1280]{2,1,0:T(8,128)(2,1)S(1)} %all-to-all-done.span_ref, f32[4,1024,256]{2,1,0:T(8,128)S(1)} %get-tuple-element.25.sum_ref, f32[4,1024,128]{2,1,0:T(8,128)S(1)} %get-tuple-element.26.peak_ref, ...), custom_call_target="tpu_custom_call" | custom-call | tf_op jit(solution)/shard_map/attend_far/pallas_call | solution.py:268
  45.6 1.1 %collective-permute-done.9.refs_1_ = bf16[128,1024]{1,0:T(8,128)(2,1)S(1)} collective-permute-done((bf16[128,1024]{1,0:T(8,128)(2,1)S(1)}, bf16[128,1024]{1,0:T(8,128)(2,1)S(1)}, u32[]{:S(2)}, u32[]{:S(2)}) %collective-permute-start.9) | collective-permute-done | bytes 262176 | tf_op jit(solution)/shard_map/ppermute | solution.py:318
  46.7 1.0 %join.2.refs_2_ = f32[1,128,4096]{2,1,0:T(8,128)} custom-call(f32[128,1024]{1,0:T(8,128)S(1)} %attend_far.4.refs_0_, bf16[128,1024]{1,0:T(8,128)(2,1)S(1)} %collective-permute-done.9.refs_1_), custom_call_target="tpu_custom_call" | custom-call | tf_op jit(solution)/shard_map/join/pallas_call | solution.py:302
  47.7 4.3 %collective-permute-done.7.refs_0_ = bf16[128,1024]{1,0:T(8,128)(2,1)S(1)} collective-permute-done((bf16[128,1024]{1,0:T(8,128)(2,1)S(1)}, bf16[128,1024]{1,0:T(8,128)(2,1)S(1)}, u32[]{:S(2)}, u32[]{:S(2)}) %collective-permute-start.7) | collective-permute-done | bytes 262176 | tf_op jit(solution)/shard_map/ppermute | solution.py:318
  52.1 0.0 collective-permute-done.8.refs_1_
  52.1 1.0 %join.3 = f32[1,128,4096]{2,1,0:T(8,128)} custom-call(bf16[128,1024]{1,0:T(8,128)(2,1)S(1)} %collective-permute-done.7.refs_0_, bf16[128,1024]{1,0:T(8,128)(2,1)S(1)} %collective-permute-done.8.refs_1_, f32[1,128,4096]{2,1,0:T(8,128)} %join.2.refs_2_), custom_call_target="tpu_custom_call", output_to_operand_aliasing={{}: (2, {})} | custom-call | tf_op jit(solution)/shard_map/join/pallas_call | solution.py:302
Async XLA Ops:
  4.3 4.0 %copy-start.8 = (bf16[2,2,128,128]{3,2,1,0:T(8,128)(2,1)S(1)}, bf16[2,2,128,128]{3,2,1,0:T(8,128)(2,1)}, u32[]{:S(2)}) copy-start(bf16[2,2,128,128]{3,2,1,0:T(8,128)(2,1)} %get-tuple-element.22) | copy-start | bytes 393220
  4.3 4.0 %copy-start.7 = (bf16[2,2,128,128]{3,2,1,0:T(8,128)(2,1)S(1)}, bf16[2,2,128,128]{3,2,1,0:T(8,128)(2,1)}, u32[]{:S(2)}) copy-start(bf16[2,2,128,128]{3,2,1,0:T(8,128)(2,1)} %get-tuple-element.23) | copy-start | bytes 393220
  4.3 4.4 %copy-start.6 = (bf16[2,2,128,128]{3,2,1,0:T(8,128)(2,1)S(1)}, bf16[2,2,128,128]{3,2,1,0:T(8,128)(2,1)}, u32[]{:S(2)}) copy-start(bf16[2,2,128,128]{3,2,1,0:T(8,128)(2,1)} %get-tuple-element.24) | copy-start | bytes 393220
  4.3 6.7 %copy-start.5 = (bf16[2,2,128,128]{3,2,1,0:T(8,128)(2,1)S(1)}, bf16[2,2,128,128]{3,2,1,0:T(8,128)(2,1)}, u32[]{:S(2)}) copy-start(bf16[2,2,128,128]{3,2,1,0:T(8,128)(2,1)} %get-tuple-element.27) | copy-start | bytes 393220
  4.4 8.3 %copy-start.4 = (bf16[2,2,128,128]{3,2,1,0:T(8,128)(2,1)S(1)}, bf16[2,2,128,128]{3,2,1,0:T(8,128)(2,1)}, u32[]{:S(2)}) copy-start(bf16[2,2,128,128]{3,2,1,0:T(8,128)(2,1)} %get-tuple-element.28) | copy-start | bytes 393220
  4.4 8.4 %copy-start.3 = (bf16[2,2,128,128]{3,2,1,0:T(8,128)(2,1)S(1)}, bf16[2,2,128,128]{3,2,1,0:T(8,128)(2,1)}, u32[]{:S(2)}) copy-start(bf16[2,2,128,128]{3,2,1,0:T(8,128)(2,1)} %get-tuple-element.29) | copy-start | bytes 393220
  4.4 13.8 %copy-start.2 = (bf16[2,2,128,128]{3,2,1,0:T(8,128)(2,1)S(1)}, bf16[2,2,128,128]{3,2,1,0:T(8,128)(2,1)}, u32[]{:S(2)}) copy-start(bf16[2,2,128,128]{3,2,1,0:T(8,128)(2,1)} %get-tuple-element.30) | copy-start | bytes 393220
  4.4 20.4 %copy-start = (f32[16,128]{1,0:T(8,128)S(1)}, f32[16,128]{1,0:T(8,128)}, u32[]{:S(2)}) copy-start(f32[16,128]{1,0:T(8,128)} %get-tuple-element.19.used_ref) | copy-start | bytes 24580
  4.4 20.4 %copy-start.1 = (bf16[2,2,128,128]{3,2,1,0:T(8,128)(2,1)S(1)}, bf16[2,2,128,128]{3,2,1,0:T(8,128)(2,1)}, u32[]{:S(2)}) copy-start(bf16[2,2,128,128]{3,2,1,0:T(8,128)(2,1)} %get-tuple-element.21.rest_0_) | copy-start | bytes 393220
  4.4 20.4 %all-to-all-start = ((bf16[4,128,1280]{2,1,0:T(8,128)(2,1)}), bf16[4,128,1280]{2,1,0:T(8,128)(2,1)S(1)}, u32[]{:S(2)}, u32[]{:S(2)}) async-start(bf16[4,128,1280]{2,1,0:T(8,128)(2,1)} %get-tuple-element.20), calls=%async_computation | async-start | bytes 2621440 | tf_op jit(solution)/shard_map/all_to_all | solution.py:327
  8.3 4.5 %collective-permute-start = (bf16[2,2,128,128]{3,2,1,0:T(8,128)(2,1)S(1)}, bf16[2,2,128,128]{3,2,1,0:T(8,128)(2,1)S(1)}, u32[]{:S(2)}, u32[]{:S(2)}) collective-permute-start(bf16[2,2,128,128]{3,2,1,0:T(8,128)(2,1)S(1)} %copy-done.8), channel_id=1, source_target_pairs={{0,4},{4,0},{8,12},{12,8},{16,20},{20,16},{24,28},{28,24},{1,5},{5... | collective-permute-start | bytes 393224 | tf_op jit(solution)/shard_map/ppermute | solution.py:318
  8.3 9.9 %collective-permute-start.1 = (bf16[2,2,128,128]{3,2,1,0:T(8,128)(2,1)S(1)}, bf16[2,2,128,128]{3,2,1,0:T(8,128)(2,1)S(1)}, u32[]{:S(2)}, u32[]{:S(2)}) collective-permute-start(bf16[2,2,128,128]{3,2,1,0:T(8,128)(2,1)S(1)} %copy-done.7), channel_id=1, source_target_pairs={{0,16},{4,20},{8,24},{12,28},{16,0},{20,4},{24,8},{28,12},{1,17},{... | collective-permute-start | bytes 393224 | tf_op jit(solution)/shard_map/ppermute | solution.py:318
  8.7 12.3 %collective-permute-start.2 = (bf16[2,2,128,128]{3,2,1,0:T(8,128)(2,1)S(1)}, bf16[2,2,128,128]{3,2,1,0:T(8,128)(2,1)S(1)}, u32[]{:S(2)}, u32[]{:S(2)}) collective-permute-start(bf16[2,2,128,128]{3,2,1,0:T(8,128)(2,1)S(1)} %copy-done.6), channel_id=1, source_target_pairs={{0,20},{4,16},{8,28},{12,24},{16,4},{20,0},{24,12},{28,8},{1,21},{... | collective-permute-start | bytes 393224 | tf_op jit(solution)/shard_map/ppermute | solution.py:318
  11.1 21.7 %collective-permute-start.3 = (bf16[2,2,128,128]{3,2,1,0:T(8,128)(2,1)S(1)}, bf16[2,2,128,128]{3,2,1,0:T(8,128)(2,1)S(1)}, u32[]{:S(2)}, u32[]{:S(2)}) collective-permute-start(bf16[2,2,128,128]{3,2,1,0:T(8,128)(2,1)S(1)} %copy-done.5), channel_id=1, source_target_pairs={{0,8},{4,12},{8,0},{12,4},{16,24},{20,28},{24,16},{28,20},{1,9},{5... | collective-permute-start | bytes 393224 | tf_op jit(solution)/shard_map/ppermute | solution.py:318
  12.6 20.2 %collective-permute-start.4 = (bf16[2,2,128,128]{3,2,1,0:T(8,128)(2,1)S(1)}, bf16[2,2,128,128]{3,2,1,0:T(8,128)(2,1)S(1)}, u32[]{:S(2)}, u32[]{:S(2)}) collective-permute-start(bf16[2,2,128,128]{3,2,1,0:T(8,128)(2,1)S(1)} %copy-done.4), channel_id=1, source_target_pairs={{0,12},{4,8},{8,4},{12,0},{16,28},{20,24},{24,20},{28,16},{1,13},{... | collective-permute-start | bytes 393224 | tf_op jit(solution)/shard_map/ppermute | solution.py:318
  12.8 20.1 %collective-permute-start.5 = (bf16[2,2,128,128]{3,2,1,0:T(8,128)(2,1)S(1)}, bf16[2,2,128,128]{3,2,1,0:T(8,128)(2,1)S(1)}, u32[]{:S(2)}, u32[]{:S(2)}) collective-permute-start(bf16[2,2,128,128]{3,2,1,0:T(8,128)(2,1)S(1)} %copy-done.3), channel_id=1, source_target_pairs={{0,24},{4,28},{8,16},{12,20},{16,8},{20,12},{24,0},{28,4},{1,25},{... | collective-permute-start | bytes 393224 | tf_op jit(solution)/shard_map/ppermute | solution.py:318
  18.2 16.6 %collective-permute-start.6 = (bf16[2,2,128,128]{3,2,1,0:T(8,128)(2,1)S(1)}, bf16[2,2,128,128]{3,2,1,0:T(8,128)(2,1)S(1)}, u32[]{:S(2)}, u32[]{:S(2)}) collective-permute-start(bf16[2,2,128,128]{3,2,1,0:T(8,128)(2,1)S(1)} %copy-done.2), channel_id=1, source_target_pairs={{0,28},{4,24},{8,20},{12,16},{16,12},{20,8},{24,4},{28,0},{1,29},{... | collective-permute-start | bytes 393224 | tf_op jit(solution)/shard_map/ppermute | solution.py:318
  36.6 10.1 %collective-permute-start.9 = (bf16[128,1024]{1,0:T(8,128)(2,1)S(1)}, bf16[128,1024]{1,0:T(8,128)(2,1)S(1)}, u32[]{:S(2)}, u32[]{:S(2)}) collective-permute-start(bf16[128,1024]{1,0:T(8,128)(2,1)S(1)} %attend_far.5), channel_id=1, source_target_pairs={{0,3},{1,2},{2,1},{3,0},{4,7},{5,6},{6,5},{7,4},{8,11},{9,10},{10,... | collective-permute-start | bytes 786440 | tf_op jit(solution)/shard_map/ppermute | solution.py:318
  43.0 9.1 %collective-permute-start.7 = (bf16[128,1024]{1,0:T(8,128)(2,1)S(1)}, bf16[128,1024]{1,0:T(8,128)(2,1)S(1)}, u32[]{:S(2)}, u32[]{:S(2)}) collective-permute-start(bf16[128,1024]{1,0:T(8,128)(2,1)S(1)} %get-tuple-element.31), channel_id=1, source_target_pairs={{0,1},{1,0},{2,3},{3,2},{4,5},{5,4},{6,7},{7,6},{8,9},{9,8},{10,11... | collective-permute-start | bytes 786440 | tf_op jit(solution)/shard_map/ppermute | solution.py:318
  43.7 8.4 %collective-permute-start.8 = (bf16[128,1024]{1,0:T(8,128)(2,1)S(1)}, bf16[128,1024]{1,0:T(8,128)(2,1)S(1)}, u32[]{:S(2)}, u32[]{:S(2)}) collective-permute-start(bf16[128,1024]{1,0:T(8,128)(2,1)S(1)} %get-tuple-element.32), channel_id=1, source_target_pairs={{0,2},{1,3},{2,0},{3,1},{4,6},{5,7},{6,4},{7,5},{8,10},{9,11},{10,... | collective-permute-start | bytes 786440 | tf_op jit(solution)/shard_map/ppermute | solution.py:318

commit v7 on v6

--- a/solution.py
+++ b/solution.py
@@ -32,7 +32,7 @@
     span_out, rest = rest[0], rest[1:]
     pool_count, slot_count = ids_hbm.shape
     page_outs, rest = rest[:pool_count], rest[pool_count:]
-    used_ref, ids_ref, len_ref, found_ref, span_ref, pages_ref, list_sems, span_sems, sems, out_sems = rest
+    used_ref, ids_ref, len_ref, span_ref, pages_ref, list_sems, span_sems, sems, out_sems = rest
     ctx_count = span_ref.shape[0]
     pages_dev = keys_ref.shape[0]
     me = lax.axis_index("pool")
@@ -69,16 +69,16 @@
     for step in reversed(range(pool_count)):
         request = me ^ step
         live = len_ref[request]
-        for rank in range(CAP):
-            found_ref[step, rank] = 0
+        found = [jnp.int32(0)] * CAP
         count = jnp.int32(0)
         for slot in range(slot_count):
             local = ids_ref[request, slot] - low
             hit = (local >= 0) & (local < pages_dev) & (slot < live)
-            found_ref[step, count] = jnp.where(hit, local, 0)
-            count = jnp.minimum(count + hit.astype(jnp.int32), CAP)
-        for rank in range(CAP):
-            page = found_ref[step, rank]
+            found = [
+                jnp.where(hit & (count == rank), local, page) for rank, page in enumerate(found)
+            ]
+            count = count + hit.astype(jnp.int32)
+        for rank, page in enumerate(found):
             for which, source in enumerate((keys_ref, values_ref)):
                 copy = pltpu.make_async_copy(
                     source.at[page, :, columns],
@@ -132,7 +132,6 @@
         scratch_shapes=[
             pltpu.SMEM(page_ids.shape, jnp.int32),
             pltpu.SMEM(prefix_pages.shape, jnp.int32),
-            pltpu.SMEM((pool_count, CAP + 1), jnp.int32),
             pltpu.VMEM(span_shape, jnp.bfloat16),
             pltpu.VMEM((pool_count,) + page_shape, jnp.bfloat16),
             pltpu.SemaphoreType.DMA((2,)),

time: 53.7 us -> 53.7 us (level)
  no operation moved by 1% of the time
where the time goes in v7:
time: 53.7 us; the launch traced here: 53.2 us
  Pallas kernels  21.4 us (40%)
  waiting for transfers between devices  17.1 us (32%)
  starting transfers between devices  14.3 us (27%)
    ppermute x10, waiting for transfers between devices, swap(): lax.ppermute(x, axis, [(i, i ^ step) for i in range(lax.axis_size(axis))])  13.4 us
    ppermute x10, starting transfers between devices, swap(): lax.ppermute(x, axis, [(i, i ^ step) for i in range(lax.axis_size(axis))])  10.5 us
    pallas_call x1, Pallas kernels, attend_near(): pl.pallas_call(functools.partial(near_kernel, steps), out_shape=[jax.Shap...  8 us
    pallas_call x3, Pallas kernels, attend_far(): pl.pallas_call(functools.partial(far_kernel, steps, ctx_steps), out_shape...  7.14 us
    pallas_call x1, Pallas kernels, pack(): pl.pallas_call(pack_kernel, out_shape=[jax.ShapeDtypeStruct(span_shape, j...  4.24 us
    all_to_all x1, starting transfers between devices, body(): span = lax.all_to_all(packed, 'cp', split_axis=0, concat_axis=0, tiled=True)  3.86 us
    all_to_all x1, waiting for transfers between devices, body(): span = lax.all_to_all(packed, 'cp', split_axis=0, concat_axis=0, tiled=True)  3.74 us
    pallas_call x2, Pallas kernels, join(): pl.pallas_call(functools.partial(join_kernel, steps), out_shape=jax.Shape...  2.03 us
  transfers between devices with their start and end apart: 11, of which 6 were waited for; matrix products, arithmetic and copies ran while one was open for 0% of the time, Pallas kernels for 27%

profile of v7, /device:TPU:16, one launch (start us, length us, event | category | flops | bytes accessed | tf_op | source)
XLA Modules:
  0.0 53.2 jit_solution(15193624541894493177)
XLA Ops:
  0.0 4.2 %pack.1 = (bf16[4,128,1280]{2,1,0:T(8,128)(2,1)}, bf16[2,2,128,128]{3,2,1,0:T(8,128)(2,1)}, bf16[2,2,128,128]{3,2,1,0:T(8,128)(2,1)}, bf16[2,2,128,128]{3,2,1,0:...) custom-call(s32[8,16]{1,0:T(8,128)} %ids_hbm.1, ...), custom_call_target="tpu_custom_call" | custom-call | tf_op jit(solution)/shard_map/pack/pallas_call | solution.py:125
  4.3 0.0 copy-start.8
  4.3 0.0 copy-start.7
  4.3 0.0 copy-start.6
  4.3 0.0 copy-start.5
  4.3 0.0 copy-start.4
  4.3 0.0 copy-start.3
  4.3 0.0 copy-start.2
  4.3 0.0 copy-start
  4.3 0.0 copy-start.1
  4.3 3.9 %all-to-all-start = ((bf16[4,128,1280]{2,1,0:T(8,128)(2,1)}), bf16[4,128,1280]{2,1,0:T(8,128)(2,1)S(1)}, u32[]{:S(2)}, u32[]{:S(2)}) async-start(bf16[4,128,1280]{2,1,0:T(8,128)(2,1)} %get-tuple-element.20), calls=%async_computation | async-start | bytes 2621440 | tf_op jit(solution)/shard_map/all_to_all | solution.py:326
  8.2 0.0 copy-done.8
  8.2 0.0 collective-permute-start
  8.2 0.0 copy-done.7
  8.2 0.5 collective-permute-start.1
  8.7 0.0 copy-done.6
  8.7 2.3 %collective-permute-start.2 = (bf16[2,2,128,128]{3,2,1,0:T(8,128)(2,1)S(1)}, bf16[2,2,128,128]{3,2,1,0:T(8,128)(2,1)S(1)}, u32[]{:S(2)}, u32[]{:S(2)}) collective-permute-start(bf16[2,2,128,128]{3,2,1,0:T(8,128)(2,1)S(1)} %copy-done.6), channel_id=1, source_target_pairs={{0,20},{4,16},{8,28},{12,24},{16,4},{20,0},{24,12},{28,8},{1,21},{... | collective-permute-start | bytes 393224 | tf_op jit(solution)/shard_map/ppermute | solution.py:317
  11.0 0.0 copy-done.5
  11.0 1.6 %collective-permute-start.3 = (bf16[2,2,128,128]{3,2,1,0:T(8,128)(2,1)S(1)}, bf16[2,2,128,128]{3,2,1,0:T(8,128)(2,1)S(1)}, u32[]{:S(2)}, u32[]{:S(2)}) collective-permute-start(bf16[2,2,128,128]{3,2,1,0:T(8,128)(2,1)S(1)} %copy-done.5), channel_id=1, source_target_pairs={{0,8},{4,12},{8,0},{12,4},{16,24},{20,28},{24,16},{28,20},{1,9},{5... | collective-permute-start | bytes 393224 | tf_op jit(solution)/shard_map/ppermute | solution.py:317
  12.6 0.0 copy-done.4
  12.6 0.1 collective-permute-start.4
  12.7 0.0 collective-permute-done.rest_1_
  12.7 0.0 copy-done.3
  12.7 0.6 %collective-permute-start.5 = (bf16[2,2,128,128]{3,2,1,0:T(8,128)(2,1)S(1)}, bf16[2,2,128,128]{3,2,1,0:T(8,128)(2,1)S(1)}, u32[]{:S(2)}, u32[]{:S(2)}) collective-permute-start(bf16[2,2,128,128]{3,2,1,0:T(8,128)(2,1)S(1)} %copy-done.3), channel_id=1, source_target_pairs={{0,24},{4,28},{8,16},{12,20},{16,8},{20,12},{24,0},{28,4},{1,25},{... | collective-permute-start | bytes 393224 | tf_op jit(solution)/shard_map/ppermute | solution.py:317
  13.3 4.9 %collective-permute-done.1.rest_2_ = bf16[2,2,128,128]{3,2,1,0:T(8,128)(2,1)S(1)} collective-permute-done((bf16[2,2,128,128]{3,2,1,0:T(8,128)(2,1)S(1)}, bf16[2,2,128,128]{3,2,1,0:T(8,128)(2,1)S(1)}, u32[]{:S(2)}, u32[]{:S(2)}) %collective-permute-start.1) | collective-permute-done | bytes 131104 | tf_op jit(solution)/shard_map/ppermute | solution.py:317
  18.2 0.0 copy-done.2
  18.2 1.7 %collective-permute-start.6 = (bf16[2,2,128,128]{3,2,1,0:T(8,128)(2,1)S(1)}, bf16[2,2,128,128]{3,2,1,0:T(8,128)(2,1)S(1)}, u32[]{:S(2)}, u32[]{:S(2)}) collective-permute-start(bf16[2,2,128,128]{3,2,1,0:T(8,128)(2,1)S(1)} %copy-done.2), channel_id=1, source_target_pairs={{0,28},{4,24},{8,20},{12,16},{16,12},{20,8},{24,4},{28,0},{1,29},{... | collective-permute-start | bytes 393224 | tf_op jit(solution)/shard_map/ppermute | solution.py:317
  19.9 1.1 %collective-permute-done.2.rest_3_ = bf16[2,2,128,128]{3,2,1,0:T(8,128)(2,1)S(1)} collective-permute-done((bf16[2,2,128,128]{3,2,1,0:T(8,128)(2,1)S(1)}, bf16[2,2,128,128]{3,2,1,0:T(8,128)(2,1)S(1)}, u32[]{:S(2)}, u32[]{:S(2)}) %collective-permute-start.2) | collective-permute-done | bytes 131104 | tf_op jit(solution)/shard_map/ppermute | solution.py:317
  21.0 3.7 %all-to-all-done.span_ref = bf16[4,128,1280]{2,1,0:T(8,128)(2,1)S(1)} async-done(((bf16[4,128,1280]{2,1,0:T(8,128)(2,1)}), bf16[4,128,1280]{2,1,0:T(8,128)(2,1)S(1)}, u32[]{:S(2)}, u32[]{:S(2)}) %all-to-all-start) | async-done | bytes 1310752 | tf_op jit(solution)/shard_map/all_to_all | solution.py:326
  24.7 0.0 copy-done
  24.7 0.0 copy-done.1
  24.7 8.0 %attend_near.1 = (f32[4,1024,256]{2,1,0:T(8,128)S(1)}, f32[4,1024,128]{2,1,0:T(8,128)S(1)}) custom-call(f32[16,128]{1,0:T(8,128)S(1)} %copy-done, bf16[4,128,1280]{2,1,0:T(8,128)(2,1)S(1)} %all-to-all-done.span_ref, bf16[2,2,128,128]{3,2,1,0:T(8,128)(2,1)S(1)} %copy-done.1, bf16[2,2,128,128]{3,2,1,0:T(8,128)(2,1)S(1)} %collective-permute-done.rest_1_, ...), custom_call_target="tpu_custom_call" | custom-call | tf_op jit(solution)/shard_map/attend_near/pallas_call | solution.py:225
  32.7 0.0 collective-permute-done.3.rest_0_
  32.7 0.0 collective-permute-done.4.rest_1_
  32.8 0.0 collective-permute-done.5.rest_2_
  32.8 1.9 %collective-permute-done.6.rest_3_ = bf16[2,2,128,128]{3,2,1,0:T(8,128)(2,1)S(1)} collective-permute-done((bf16[2,2,128,128]{3,2,1,0:T(8,128)(2,1)S(1)}, bf16[2,2,128,128]{3,2,1,0:T(8,128)(2,1)S(1)}, u32[]{:S(2)}, u32[]{:S(2)}) %collective-permute-start.6) | collective-permute-done | bytes 131104 | tf_op jit(solution)/shard_map/ppermute | solution.py:317
  34.7 1.9 %attend_far.5 = bf16[128,1024]{1,0:T(8,128)(2,1)S(1)} custom-call(f32[16,128]{1,0:T(8,128)S(1)} %copy-done, bf16[4,128,1280]{2,1,0:T(8,128)(2,1)S(1)} %all-to-all-done.span_ref, f32[4,1024,256]{2,1,0:T(8,128)S(1)} %get-tuple-element.25.sum_ref, f32[4,1024,128]{2,1,0:T(8,128)S(1)} %get-tuple-element.26.peak_ref, ...), custom_call_target="tpu_custom_call" | custom-call | tf_op jit(solution)/shard_map/attend_far/pallas_call | solution.py:267
  36.6 3.0 %collective-permute-start.9 = (bf16[128,1024]{1,0:T(8,128)(2,1)S(1)}, bf16[128,1024]{1,0:T(8,128)(2,1)S(1)}, u32[]{:S(2)}, u32[]{:S(2)}) collective-permute-start(bf16[128,1024]{1,0:T(8,128)(2,1)S(1)} %attend_far.5), channel_id=1, source_target_pairs={{0,3},{1,2},{2,1},{3,0},{4,7},{5,6},{6,5},{7,4},{8,11},{9,10},{10,... | collective-permute-start | bytes 786440 | tf_op jit(solution)/shard_map/ppermute | solution.py:317
  39.5 3.4 %attend_far.3 = (bf16[128,1024]{1,0:T(8,128)(2,1)S(1)}, bf16[128,1024]{1,0:T(8,128)(2,1)S(1)}) custom-call(f32[16,128]{1,0:T(8,128)S(1)} %copy-done, bf16[4,128,1280]{2,1,0:T(8,128)(2,1)S(1)} %all-to-all-done.span_ref, f32[4,1024,256]{2,1,0:T(8,128)S(1)} %get-tuple-element.25.sum_ref, f32[4,1024,128]{2,1,0:T(8,128)S(1)} %get-tuple-element.26.peak_ref, ...), custom_call_target="tpu_custom_call" | custom-call | tf_op jit(solution)/shard_map/attend_far/pallas_call | solution.py:267
  43.0 0.6 %collective-permute-start.7 = (bf16[128,1024]{1,0:T(8,128)(2,1)S(1)}, bf16[128,1024]{1,0:T(8,128)(2,1)S(1)}, u32[]{:S(2)}, u32[]{:S(2)}) collective-permute-start(bf16[128,1024]{1,0:T(8,128)(2,1)S(1)} %get-tuple-element.31), channel_id=1, source_target_pairs={{0,1},{1,0},{2,3},{3,2},{4,5},{5,4},{6,7},{7,6},{8,9},{9,8},{10,11... | collective-permute-start | bytes 786440 | tf_op jit(solution)/shard_map/ppermute | solution.py:317
  43.6 0.1 collective-permute-start.8
  43.7 1.8 %attend_far.4.refs_0_ = f32[128,1024]{1,0:T(8,128)S(1)} custom-call(f32[16,128]{1,0:T(8,128)S(1)} %copy-done, bf16[4,128,1280]{2,1,0:T(8,128)(2,1)S(1)} %all-to-all-done.span_ref, f32[4,1024,256]{2,1,0:T(8,128)S(1)} %get-tuple-element.25.sum_ref, f32[4,1024,128]{2,1,0:T(8,128)S(1)} %get-tuple-element.26.peak_ref, ...), custom_call_target="tpu_custom_call" | custom-call | tf_op jit(solution)/shard_map/attend_far/pallas_call | solution.py:267
  45.5 1.1 %collective-permute-done.9.refs_1_ = bf16[128,1024]{1,0:T(8,128)(2,1)S(1)} collective-permute-done((bf16[128,1024]{1,0:T(8,128)(2,1)S(1)}, bf16[128,1024]{1,0:T(8,128)(2,1)S(1)}, u32[]{:S(2)}, u32[]{:S(2)}) %collective-permute-start.9) | collective-permute-done | bytes 262176 | tf_op jit(solution)/shard_map/ppermute | solution.py:317
  46.7 1.0 %join.2.refs_2_ = f32[1,128,4096]{2,1,0:T(8,128)} custom-call(f32[128,1024]{1,0:T(8,128)S(1)} %attend_far.4.refs_0_, bf16[128,1024]{1,0:T(8,128)(2,1)S(1)} %collective-permute-done.9.refs_1_), custom_call_target="tpu_custom_call" | custom-call | tf_op jit(solution)/shard_map/join/pallas_call | solution.py:301
  47.7 4.3 %collective-permute-done.7.refs_0_ = bf16[128,1024]{1,0:T(8,128)(2,1)S(1)} collective-permute-done((bf16[128,1024]{1,0:T(8,128)(2,1)S(1)}, bf16[128,1024]{1,0:T(8,128)(2,1)S(1)}, u32[]{:S(2)}, u32[]{:S(2)}) %collective-permute-start.7) | collective-permute-done | bytes 262176 | tf_op jit(solution)/shard_map/ppermute | solution.py:317
  52.0 0.0 collective-permute-done.8.refs_1_
  52.0 1.0 %join.3 = f32[1,128,4096]{2,1,0:T(8,128)} custom-call(bf16[128,1024]{1,0:T(8,128)(2,1)S(1)} %collective-permute-done.7.refs_0_, bf16[128,1024]{1,0:T(8,128)(2,1)S(1)} %collective-permute-done.8.refs_1_, f32[1,128,4096]{2,1,0:T(8,128)} %join.2.refs_2_), custom_call_target="tpu_custom_call", output_to_operand_aliasing={{}: (2, {})} | custom-call | tf_op jit(solution)/shard_map/join/pallas_call | solution.py:301
Async XLA Ops:
  4.3 4.0 %copy-start.8 = (bf16[2,2,128,128]{3,2,1,0:T(8,128)(2,1)S(1)}, bf16[2,2,128,128]{3,2,1,0:T(8,128)(2,1)}, u32[]{:S(2)}) copy-start(bf16[2,2,128,128]{3,2,1,0:T(8,128)(2,1)} %get-tuple-element.22) | copy-start | bytes 393220
  4.3 4.0 %copy-start.7 = (bf16[2,2,128,128]{3,2,1,0:T(8,128)(2,1)S(1)}, bf16[2,2,128,128]{3,2,1,0:T(8,128)(2,1)}, u32[]{:S(2)}) copy-start(bf16[2,2,128,128]{3,2,1,0:T(8,128)(2,1)} %get-tuple-element.23) | copy-start | bytes 393220
  4.3 4.4 %copy-start.6 = (bf16[2,2,128,128]{3,2,1,0:T(8,128)(2,1)S(1)}, bf16[2,2,128,128]{3,2,1,0:T(8,128)(2,1)}, u32[]{:S(2)}) copy-start(bf16[2,2,128,128]{3,2,1,0:T(8,128)(2,1)} %get-tuple-element.24) | copy-start | bytes 393220
  4.3 6.7 %copy-start.5 = (bf16[2,2,128,128]{3,2,1,0:T(8,128)(2,1)S(1)}, bf16[2,2,128,128]{3,2,1,0:T(8,128)(2,1)}, u32[]{:S(2)}) copy-start(bf16[2,2,128,128]{3,2,1,0:T(8,128)(2,1)} %get-tuple-element.27) | copy-start | bytes 393220
  4.3 8.3 %copy-start.4 = (bf16[2,2,128,128]{3,2,1,0:T(8,128)(2,1)S(1)}, bf16[2,2,128,128]{3,2,1,0:T(8,128)(2,1)}, u32[]{:S(2)}) copy-start(bf16[2,2,128,128]{3,2,1,0:T(8,128)(2,1)} %get-tuple-element.28) | copy-start | bytes 393220
  4.3 8.4 %copy-start.3 = (bf16[2,2,128,128]{3,2,1,0:T(8,128)(2,1)S(1)}, bf16[2,2,128,128]{3,2,1,0:T(8,128)(2,1)}, u32[]{:S(2)}) copy-start(bf16[2,2,128,128]{3,2,1,0:T(8,128)(2,1)} %get-tuple-element.29) | copy-start | bytes 393220
  4.3 13.9 %copy-start.2 = (bf16[2,2,128,128]{3,2,1,0:T(8,128)(2,1)S(1)}, bf16[2,2,128,128]{3,2,1,0:T(8,128)(2,1)}, u32[]{:S(2)}) copy-start(bf16[2,2,128,128]{3,2,1,0:T(8,128)(2,1)} %get-tuple-element.30) | copy-start | bytes 393220
  4.3 20.4 %copy-start = (f32[16,128]{1,0:T(8,128)S(1)}, f32[16,128]{1,0:T(8,128)}, u32[]{:S(2)}) copy-start(f32[16,128]{1,0:T(8,128)} %get-tuple-element.19.used_ref) | copy-start | bytes 24580
  4.3 20.4 %copy-start.1 = (bf16[2,2,128,128]{3,2,1,0:T(8,128)(2,1)S(1)}, bf16[2,2,128,128]{3,2,1,0:T(8,128)(2,1)}, u32[]{:S(2)}) copy-start(bf16[2,2,128,128]{3,2,1,0:T(8,128)(2,1)} %get-tuple-element.21.rest_0_) | copy-start | bytes 393220
  4.3 20.4 %all-to-all-start = ((bf16[4,128,1280]{2,1,0:T(8,128)(2,1)}), bf16[4,128,1280]{2,1,0:T(8,128)(2,1)S(1)}, u32[]{:S(2)}, u32[]{:S(2)}) async-start(bf16[4,128,1280]{2,1,0:T(8,128)(2,1)} %get-tuple-element.20), calls=%async_computation | async-start | bytes 2621440 | tf_op jit(solution)/shard_map/all_to_all | solution.py:326
  8.2 4.5 %collective-permute-start = (bf16[2,2,128,128]{3,2,1,0:T(8,128)(2,1)S(1)}, bf16[2,2,128,128]{3,2,1,0:T(8,128)(2,1)S(1)}, u32[]{:S(2)}, u32[]{:S(2)}) collective-permute-start(bf16[2,2,128,128]{3,2,1,0:T(8,128)(2,1)S(1)} %copy-done.8), channel_id=1, source_target_pairs={{0,4},{4,0},{8,12},{12,8},{16,20},{20,16},{24,28},{28,24},{1,5},{5... | collective-permute-start | bytes 393224 | tf_op jit(solution)/shard_map/ppermute | solution.py:317
  8.2 10.0 %collective-permute-start.1 = (bf16[2,2,128,128]{3,2,1,0:T(8,128)(2,1)S(1)}, bf16[2,2,128,128]{3,2,1,0:T(8,128)(2,1)S(1)}, u32[]{:S(2)}, u32[]{:S(2)}) collective-permute-start(bf16[2,2,128,128]{3,2,1,0:T(8,128)(2,1)S(1)} %copy-done.7), channel_id=1, source_target_pairs={{0,16},{4,20},{8,24},{12,28},{16,0},{20,4},{24,8},{28,12},{1,17},{... | collective-permute-start | bytes 393224 | tf_op jit(solution)/shard_map/ppermute | solution.py:317
  8.7 12.3 %collective-permute-start.2 = (bf16[2,2,128,128]{3,2,1,0:T(8,128)(2,1)S(1)}, bf16[2,2,128,128]{3,2,1,0:T(8,128)(2,1)S(1)}, u32[]{:S(2)}, u32[]{:S(2)}) collective-permute-start(bf16[2,2,128,128]{3,2,1,0:T(8,128)(2,1)S(1)} %copy-done.6), channel_id=1, source_target_pairs={{0,20},{4,16},{8,28},{12,24},{16,4},{20,0},{24,12},{28,8},{1,21},{... | collective-permute-start | bytes 393224 | tf_op jit(solution)/shard_map/ppermute | solution.py:317
  11.0 21.8 %collective-permute-start.3 = (bf16[2,2,128,128]{3,2,1,0:T(8,128)(2,1)S(1)}, bf16[2,2,128,128]{3,2,1,0:T(8,128)(2,1)S(1)}, u32[]{:S(2)}, u32[]{:S(2)}) collective-permute-start(bf16[2,2,128,128]{3,2,1,0:T(8,128)(2,1)S(1)} %copy-done.5), channel_id=1, source_target_pairs={{0,8},{4,12},{8,0},{12,4},{16,24},{20,28},{24,16},{28,20},{1,9},{5... | collective-permute-start | bytes 393224 | tf_op jit(solution)/shard_map/ppermute | solution.py:317
  12.6 20.2 %collective-permute-start.4 = (bf16[2,2,128,128]{3,2,1,0:T(8,128)(2,1)S(1)}, bf16[2,2,128,128]{3,2,1,0:T(8,128)(2,1)S(1)}, u32[]{:S(2)}, u32[]{:S(2)}) collective-permute-start(bf16[2,2,128,128]{3,2,1,0:T(8,128)(2,1)S(1)} %copy-done.4), channel_id=1, source_target_pairs={{0,12},{4,8},{8,4},{12,0},{16,28},{20,24},{24,20},{28,16},{1,13},{... | collective-permute-start | bytes 393224 | tf_op jit(solution)/shard_map/ppermute | solution.py:317
  12.7 20.1 %collective-permute-start.5 = (bf16[2,2,128,128]{3,2,1,0:T(8,128)(2,1)S(1)}, bf16[2,2,128,128]{3,2,1,0:T(8,128)(2,1)S(1)}, u32[]{:S(2)}, u32[]{:S(2)}) collective-permute-start(bf16[2,2,128,128]{3,2,1,0:T(8,128)(2,1)S(1)} %copy-done.3), channel_id=1, source_target_pairs={{0,24},{4,28},{8,16},{12,20},{16,8},{20,12},{24,0},{28,4},{1,25},{... | collective-permute-start | bytes 393224 | tf_op jit(solution)/shard_map/ppermute | solution.py:317
  18.2 16.5 %collective-permute-start.6 = (bf16[2,2,128,128]{3,2,1,0:T(8,128)(2,1)S(1)}, bf16[2,2,128,128]{3,2,1,0:T(8,128)(2,1)S(1)}, u32[]{:S(2)}, u32[]{:S(2)}) collective-permute-start(bf16[2,2,128,128]{3,2,1,0:T(8,128)(2,1)S(1)} %copy-done.2), channel_id=1, source_target_pairs={{0,28},{4,24},{8,20},{12,16},{16,12},{20,8},{24,4},{28,0},{1,29},{... | collective-permute-start | bytes 393224 | tf_op jit(solution)/shard_map/ppermute | solution.py:317
  36.6 10.1 %collective-permute-start.9 = (bf16[128,1024]{1,0:T(8,128)(2,1)S(1)}, bf16[128,1024]{1,0:T(8,128)(2,1)S(1)}, u32[]{:S(2)}, u32[]{:S(2)}) collective-permute-start(bf16[128,1024]{1,0:T(8,128)(2,1)S(1)} %attend_far.5), channel_id=1, source_target_pairs={{0,3},{1,2},{2,1},{3,0},{4,7},{5,6},{6,5},{7,4},{8,11},{9,10},{10,... | collective-permute-start | bytes 786440 | tf_op jit(solution)/shard_map/ppermute | solution.py:317
  43.0 9.0 %collective-permute-start.7 = (bf16[128,1024]{1,0:T(8,128)(2,1)S(1)}, bf16[128,1024]{1,0:T(8,128)(2,1)S(1)}, u32[]{:S(2)}, u32[]{:S(2)}) collective-permute-start(bf16[128,1024]{1,0:T(8,128)(2,1)S(1)} %get-tuple-element.31), channel_id=1, source_target_pairs={{0,1},{1,0},{2,3},{3,2},{4,5},{5,4},{6,7},{7,6},{8,9},{9,8},{10,11... | collective-permute-start | bytes 786440 | tf_op jit(solution)/shard_map/ppermute | solution.py:317
  43.6 8.4 %collective-permute-start.8 = (bf16[128,1024]{1,0:T(8,128)(2,1)S(1)}, bf16[128,1024]{1,0:T(8,128)(2,1)S(1)}, u32[]{:S(2)}, u32[]{:S(2)}) collective-permute-start(bf16[128,1024]{1,0:T(8,128)(2,1)S(1)} %get-tuple-element.32), channel_id=1, source_target_pairs={{0,2},{1,3},{2,0},{3,1},{4,6},{5,7},{6,4},{7,5},{8,10},{9,11},{10,... | collective-permute-start | bytes 786440 | tf_op jit(solution)/shard_map/ppermute | solution.py:317
